TPU v7x, 32 devices: a whole 2x2x4 slice. The times are simulated.
32 devices in a mesh: dp: 2 (over x), ctx: 16 (over z, y, core).
Axes of the slice: x: 2, y: 2, z: 4, core: 2. Of those that a mesh axis runs over, the one named last changes fastest.
Arguments:
- pre_gate: bfloat16 [2048, 4096], P('dp', 'ctx'), may hold values from -6 to 6
- values: bfloat16 [2048, 4096], P('dp', 'ctx'), may hold values from -6 to 6
- post_gate: bfloat16 [2048, 4096], P('dp', 'ctx'), may hold values from -6 to 6
- filters: float32 [256, 4096], P('ctx', 'dp'), may hold values from -0.09375 to 0.09375
- cotangent: bfloat16 [2048, 4096], P('dp', 'ctx'), may hold values from -6 to 6
Outputs:
- mixed: bfloat16 [2048, 4096], P('dp', 'ctx')
- pre_grad: bfloat16 [2048, 4096], P('dp', 'ctx')
- value_grad: bfloat16 [2048, 4096], P('dp', 'ctx')
- post_grad: bfloat16 [2048, 4096], P('dp', 'ctx')
- filter_grad: float32 [256, 4096], P('ctx', 'dp')
All inputs are finite; a program needn't handle non-finite values.
Results may differ from a plain program's by a relative error of at most 0.014.
Values may be sent and summed in bfloat16 or wider, within the bound.
No kernel may reach another device: no remote copies, remote signals or barrier semaphores. Data moves between devices by JAX's collectives and lax.ppermute only.
A program may use at most 64 MiB of HBM per device.

v0:
```python
import math

import jax
import jax.numpy as jnp
import numpy as np
from jax import lax
from jax.experimental import pallas as pl
from jax.experimental.pallas import tpu as pltpu
from jax.sharding import PartitionSpec as P


LANES = 128
SUBLANES = 8
VMEM_BYTES = 60 * 1024 * 1024
HEAVY = 1 << 37


def dft_table(size):
    angle = np.arange(size)[:, None] * (2.0 * np.arange(size)[None, :] + 1.0) * (math.pi / (2 * size))
    strips = size // LANES
    cos, sin = (part.reshape(size, strips, 1, LANES) for part in (np.cos(angle), np.sin(angle)))
    return jnp.asarray(np.concatenate([cos, -sin], axis=2).reshape(size, 2 * size), jnp.bfloat16)


def dot(left, right):
    return jnp.dot(left, right, preferred_element_type=jnp.float32)


def back(spectrum, table):
    result = lax.dot_general(spectrum, table, (((1,), (1,)), ((), ())), preferred_element_type=jnp.float32)
    return result * (2.0 / table.shape[1])


def alternating():
    odd = lax.broadcasted_iota(jnp.int32, (SUBLANES, LANES), 1) % 2
    return 1.0 - 2.0 * odd.astype(jnp.float32)


def place(half_blocks):
    index = lax.axis_index("ctx")
    return index // half_blocks, lax.rem(index, half_blocks)


def real_of(strip):
    return pl.ds(2 * strip * LANES, LANES)


def imag_of(strip):
    return pl.ds((2 * strip + 1) * LANES, LANES)


def begin(copies):
    for copy in copies:
        copy.start()
    return copies


def end(copies):
    for copy in copies:
        copy.wait()


def call(kernel, name, operands, outputs, scratch, weight=1, vmem=VMEM_BYTES):
    hbm = pl.BlockSpec(memory_space=pltpu.HBM)
    return pl.pallas_call(
        kernel,
        in_specs=[hbm] * len(operands),
        out_specs=[hbm] * len(outputs),
        out_shape=outputs,
        scratch_shapes=scratch,
        compiler_params=pltpu.CompilerParams(vmem_limit_bytes=vmem),
        cost_estimate=pl.CostEstimate(flops=weight, bytes_accessed=weight, transcendentals=0),
        name=name,
    )(*operands)


def gate(arrays, filters, repeats, half_blocks):
    rows_all, tokens = arrays[0].shape
    rows = rows_all // repeats
    share = rows // (2 * half_blocks)
    piece = (repeats, 2, share, tokens)

    def kernel(pre_ref, value_ref, post_ref, cot_ref, filt_ref, out_ref, even_ref, odd_ref, taps_ref, in_ref, result_ref, filt_in, taps_out, in_sems, out_sems, own_sems, taps_sems):
        half, me = place(half_blocks)
        sources = (pre_ref, value_ref, cot_ref, post_ref)

        def fetch(r):
            at = pl.ds(r * rows, rows)
            return [
                pltpu.make_async_copy(ref.at[at], in_ref.at[which, r], in_sems.at[which, r])
                for which, ref in enumerate(sources)
            ]

        for r in range(repeats):
            begin(fetch(r))
        loaded = begin([pltpu.make_async_copy(filt_ref, filt_in, taps_sems.at[0])])
        sent = []
        for r in range(repeats):
            end(fetch(r))
            for which in range(2):
                product = in_ref[2 * which, r].astype(jnp.float32) * in_ref[2 * which + 1, r].astype(jnp.float32)
                product = product.astype(jnp.bfloat16).reshape(2, half_blocks, share, tokens)
                at = half if which == 0 else 1 - half
                for side in range(2):
                    result_ref[at, :, r, side] = product[side]
            for to in range(2):
                copy = pltpu.make_async_copy(result_ref.at[0, :, r], out_ref.at[to, :, r], out_sems.at[to, r])
                sent += begin([copy])
        for at in range(half_blocks // 2):
            for odd, target in enumerate((even_ref, odd_ref)):
                source = result_ref.at[1, jnp.bitwise_xor(me, 2 * at + odd)]
                sent += begin([pltpu.make_async_copy(source, target.at[at], own_sems.at[odd, at])])
        end(loaded)
        taps_out[...] = filt_in[...].astype(jnp.bfloat16)
        sent += begin([pltpu.make_async_copy(taps_out, taps_ref, taps_sems.at[1])])
        end(sent)

    own_shape = jax.ShapeDtypeStruct((half_blocks // 2, *piece), jnp.bfloat16)
    return call(
        kernel,
        "gate",
        (*arrays, filters),
        [
            jax.ShapeDtypeStruct((2, half_blocks, *piece), jnp.bfloat16),
            own_shape,
            own_shape,
            jax.ShapeDtypeStruct(filters.shape, jnp.bfloat16),
        ],
        [
            pltpu.VMEM((4, repeats, rows, tokens), jnp.bfloat16),
            pltpu.VMEM((2, half_blocks, *piece), jnp.bfloat16),
            pltpu.VMEM(filters.shape, filters.dtype),
            pltpu.VMEM(filters.shape, jnp.bfloat16),
            pltpu.SemaphoreType.DMA((4, repeats)),
            pltpu.SemaphoreType.DMA((2, repeats)),
            pltpu.SemaphoreType.DMA((2, half_blocks // 2)),
            pltpu.SemaphoreType.DMA((2,)),
        ],
    )


def exchange_own(even, odd, half_blocks):
    def swap(array, slot):
        return lax.ppermute(array, "ctx", [(i, i ^ slot) for i in range(2 * half_blocks)])

    odd = swap(odd, 1)
    groups = [([0], even[:1]), ([1], odd[:1])]
    for at in range(1, half_blocks // 2):
        pair = jnp.concatenate([even[at : at + 1], odd[at : at + 1]])
        groups.append(([2 * at, 2 * at + 1], swap(pair, 2 * at)))
    return groups


def finish(returned, arrays, terms):
    half_blocks, _, repeats, sides, share, tokens = returned.shape
    count, rows = repeats * sides, half_blocks * share

    def kernel(recv_ref, pre_ref, value_ref, post_ref, cot_ref, mine_ref, theirs_ref, *refs):
        out_refs, (held_ref, total_ref, sems, total_sem) = refs[:5], refs[5:]
        half, _ = place(half_blocks)
        sent = []
        for part in range(count):
            r, side = part // sides, part % sides
            at = pl.ds(part * rows, rows)
            conv = recv_ref[:, half, r, side].reshape(rows, tokens).astype(jnp.float32)
            grad = recv_ref[:, 1 - half, r, side].reshape(rows, tokens).astype(jnp.float32)
            for which, (factor_ref, result) in enumerate(
                ((post_ref, conv), (value_ref, grad), (pre_ref, grad), (cot_ref, conv))
            ):
                held_ref[which, part] = (factor_ref[at].astype(jnp.float32) * result).astype(jnp.bfloat16)
                sent += begin(
                    [pltpu.make_async_copy(held_ref.at[which, part], out_refs[which].at[at], sems.at[which, part])]
                )
        total_ref[...] = mine_ref[...] + theirs_ref[...].astype(jnp.float32)
        sent += begin([pltpu.make_async_copy(total_ref, out_refs[4], total_sem)])
        end(sent)

    shapes = [jax.ShapeDtypeStruct(arrays[0].shape, jnp.bfloat16)] * 4
    return pl.pallas_call(
        kernel,
        in_specs=[pl.BlockSpec(memory_space=pltpu.VMEM)] * 7,
        out_specs=[pl.BlockSpec(memory_space=pltpu.HBM)] * 5,
        out_shape=shapes + [jax.ShapeDtypeStruct(terms[0].shape, jnp.float32)],
        scratch_shapes=[
            pltpu.VMEM((4, count, rows, tokens), jnp.bfloat16),
            pltpu.VMEM(terms[0].shape, jnp.float32),
            pltpu.SemaphoreType.DMA((4, count)),
            pltpu.SemaphoreType.DMA,
        ],
        compiler_params=pltpu.CompilerParams(vmem_limit_bytes=VMEM_BYTES // 6),
        name="finish",
    )(returned, *arrays, *terms)


def pack_taps(taps, pair, half_blocks):
    share, lags = taps.shape

    def kernel(taps_ref, pair_ref, out_ref, held_ref, sems):
        half, _ = place(half_blocks)
        end(
            begin(
                [
                    pltpu.make_async_copy(taps_ref, held_ref.at[half], sems.at[0]),
                    pltpu.make_async_copy(pair_ref, held_ref.at[1 - half], sems.at[1]),
                ]
            )
        )
        end(begin([pltpu.make_async_copy(held_ref, out_ref, sems.at[2])]))

    return call(
        kernel,
        "pack_taps",
        (taps, pair),
        [jax.ShapeDtypeStruct((2, share, lags), jnp.bfloat16)],
        [pltpu.VMEM((2, share, lags), jnp.bfloat16), pltpu.SemaphoreType.DMA((3,))],
        weight=HEAVY,
    )[0]


def transform_taps(here, there, half_blocks, groups, table):
    sides, share, lags = here.shape
    size = table.shape[0]
    count = groups * lags // size
    rows, width = sides * share, 2 * size

    def kernel(here_ref, there_ref, table_hbm, out_hbm, piece_ref, table_ref, stage_ref, out_ref, sems):
        sources = (here_ref, there_ref)
        loads = begin([pltpu.make_async_copy(ref, piece_ref.at[at], sems.at[at]) for at, ref in enumerate(sources)])
        tabled = begin([pltpu.make_async_copy(table_hbm, table_ref, sems.at[2])])
        half, _ = place(half_blocks)
        group = lax.axis_index("dp")
        end(loads)
        for at in range(2):
            first = (group if at == 0 else 1 - group) * (lags // size)
            for side in range(sides):
                for k in range(lags // size):
                    piece = piece_ref[at, side, :, k * size : (k + 1) * size]
                    stage_ref[first + k, side * share : (side + 1) * share] = piece
        end(tabled)
        spectrum = dot(stage_ref[...].reshape(count * rows, size), table_ref[...]).reshape(count, rows, width)
        turn = jnp.where(half == 0, 1.0, -1.0).astype(jnp.float32)
        sign = alternating()[:1]
        sent = []
        for k in range(count):
            for strip in range(size // LANES):
                re = slice(2 * strip * LANES, (2 * strip + 1) * LANES)
                im = slice((2 * strip + 1) * LANES, (2 * strip + 2) * LANES)
                real, imag = spectrum[k, :, re], spectrum[k, :, im]
                if k > 0:
                    real, imag = real - sign * spectrum[k - 1, :, im], imag + sign * spectrum[k - 1, :, re]
                out_ref[k, :, re] = real.astype(jnp.bfloat16)
                out_ref[k, :, im] = (turn * imag).astype(jnp.bfloat16)
            sent += begin([pltpu.make_async_copy(out_ref.at[k], out_hbm.at[k], sems.at[3 + k])])
        end(sent)

    return call(
        kernel,
        "taps",
        (here, there, table),
        [jax.ShapeDtypeStruct((count, rows, width), jnp.bfloat16)],
        [
            pltpu.VMEM((2, sides, share, lags), jnp.bfloat16),
            pltpu.VMEM((size, width), jnp.bfloat16),
            pltpu.VMEM((count, rows, size), jnp.bfloat16),
            pltpu.VMEM((count, rows, width), jnp.bfloat16),
            pltpu.SemaphoreType.DMA((3 + count,)),
        ],
    )[0]


def add(total, term):
    return term if total is None else (total[0] + term[0], total[1] + term[1])


def times(a, b):
    return a[0] * b[0] - a[1] * b[1], a[0] * b[1] + a[1] * b[0]


def conj_times(a, b):
    return a[0] * b[0] + a[1] * b[1], a[0] * b[1] - a[1] * b[0]


def transform(stage_ref, table_ref, spec_ref):
    width = spec_ref.shape[-1]
    staged = stage_ref[...].reshape(-1, stage_ref.shape[-1])
    for strip in range(width // (2 * LANES)):
        columns = slice(2 * strip * LANES, 2 * (strip + 1) * LANES)
        spec_ref[..., columns] = dot(staged, table_ref[:, columns]).reshape(spec_ref.shape[:-1] + (2 * LANES,))


def stage_copies(source, base, stage_ref, sems, outer, half_blocks):
    count, _, size = stage_ref.shape
    tokens = source.shape[2]
    merge = size // tokens
    half, _ = place(half_blocks)
    copies = []
    for k in range(count):
        block = order(k, count, half, outer)
        for q in range(merge):
            target = stage_ref.at[k, :, pl.ds(q * tokens, tokens)]
            copies.append(pltpu.make_async_copy(source.at[base + block * merge + q], target, sems.at[k, q]))
    return copies


def stage_all(near_hbm, own_refs, slots, stage_ref, sems, half_blocks):
    _, count, _, size = stage_ref.shape
    tokens = near_hbm.shape[2]
    merge = size // tokens
    half, me = place(half_blocks)
    near = stage_copies(near_hbm, half * half_blocks, stage_ref.at[0], sems.at[0], True, half_blocks)
    far = stage_copies(near_hbm, (1 - half) * half_blocks, stage_ref.at[1], sems.at[1], False, half_blocks)
    own = []
    for group, ref in zip(slots, own_refs):
        for at, slot in enumerate(group):
            position = jnp.bitwise_xor(me, slot)
            k = order(position // merge, count, half, False)
            start = pl.multiple_of(lax.rem(position, merge) * tokens, tokens)
            target = stage_ref.at[2, k, :, pl.ds(start, tokens)]
            own.append(pltpu.make_async_copy(ref.at[at], target, sems.at[2, slot // merge, slot % merge]))
    return begin(near) + begin(far), begin(own)


def order(k, count, half, outer):
    return jnp.where(half == (0 if outer else 1), k, count - 1 - k)


def tile_loop(rows, body):
    @pl.loop(0, rows // SUBLANES)
    def _(tile):
        body(pl.multiple_of(tile * SUBLANES, SUBLANES))


def parts(ref, k, row, strip):
    return ref[k, row, real_of(strip)], ref[k, row, imag_of(strip)]


def keep(ref, k, row, strip, value):
    ref[k, row, real_of(strip)], ref[k, row, imag_of(strip)] = value


def give_back(prod_ref, table_ref, held_ref, out_ref, sems, outer, half_blocks):
    count, rows, width = prod_ref.shape
    merge, tokens = held_ref.shape[1], held_ref.shape[3]
    half, _ = place(half_blocks)
    sent = []
    spectrum = prod_ref[...].astype(jnp.bfloat16).reshape(count * rows, width)
    for q in range(merge):
        result = back(spectrum, table_ref[q * tokens : (q + 1) * tokens])
        held_ref[:, q] = result.astype(jnp.bfloat16).reshape(count, rows, tokens)
        for k in range(count):
            block = order(k, count, half, outer)
            sent += begin(
                [pltpu.make_async_copy(held_ref.at[k, q], out_ref.at[block * merge + q], sems.at[k, q])]
            )
    end(sent)


def results(near, own, filt, half_blocks, table):
    slots = [group for group, _ in own]
    _, rows, tokens = near.shape
    size, width = table.shape
    merge = size // tokens
    count = half_blocks // merge
    filters = filt.shape[1]

    def kernel(near_hbm, *refs):
        own_hbm, (filt_hbm, table_hbm, out_hbm) = refs[: len(own)], refs[len(own) : len(own) + 3]
        stage_ref, filt_in, filt_ref, table_ref, spec_ref, prod_ref, held_ref, sems, stage_sems, out_sems = refs[len(own) + 3 :]
        tabled = begin([pltpu.make_async_copy(table_hbm, table_ref, sems.at[0])])
        staged, later = stage_all(near_hbm, own_hbm, slots, stage_ref, stage_sems, half_blocks)
        rest = begin([pltpu.make_async_copy(filt_hbm, filt_in, sems.at[1])])
        end(staged)
        end(tabled)
        end(later)
        transform(stage_ref, table_ref, spec_ref)
        end(rest)
        filt_ref[...] = filt_in[...].astype(jnp.float32)

        def tile(first):
            row = pl.ds(first, SUBLANES)
            tap_row = pl.ds(pl.multiple_of(lax.rem(first, filters), SUBLANES), SUBLANES)
            for strip in range(size // LANES):
                taps = [parts(filt_ref, k, tap_row, strip) for k in range(2 * count)]
                near, far, own = ([parts(spec_ref.at[which], k, row, strip) for k in range(count)] for which in range(3))
                for out in range(count):
                    total = None
                    for k in range(out + 1):
                        total = add(total, times(taps[out - k], near[k]))
                    keep(prod_ref.at[0], out, row, strip, total)
                for out in range(count):
                    total = None
                    for k in range(out + 1):
                        total = add(total, conj_times(taps[out - k], own[k]))
                    for k in range(count):
                        total = add(total, conj_times(taps[count + out - k], far[k]))
                    keep(prod_ref.at[1], out, row, strip, total)

        tile_loop(rows, tile)
        half, _ = place(half_blocks)
        spectrum = prod_ref[...].astype(jnp.bfloat16).reshape(2 * count * rows, width)
        sent = []
        for q in range(merge):
            result = back(spectrum, table_ref[q * tokens : (q + 1) * tokens]).astype(jnp.bfloat16)
            held_ref[:, :, q] = result.reshape(2, count, rows, tokens)
            for which in range(2):
                for k in range(count):
                    position = order(k, count, half, which == 0) * merge + q
                    copy = pltpu.make_async_copy(
                        held_ref.at[which, k, q], out_hbm.at[position, which], out_sems.at[which, k, q]
                    )
                    sent += begin([copy])
        end(sent)

    return call(
        kernel,
        "results",
        (near, *[array for _, array in own], filt, table),
        [jax.ShapeDtypeStruct((half_blocks, 2, rows, tokens), jnp.bfloat16)],
        [
            pltpu.VMEM((3, count, rows, size), jnp.bfloat16),
            pltpu.VMEM((2 * count, filters, width), jnp.bfloat16),
            pltpu.VMEM((2 * count, filters, width), jnp.float32),
            pltpu.VMEM(table.shape, jnp.bfloat16),
            pltpu.VMEM((3, count, rows, width), jnp.float32),
            pltpu.VMEM((2, count, rows, width), jnp.float32),
            pltpu.VMEM((2, count, merge, rows, tokens), jnp.bfloat16),
            pltpu.SemaphoreType.DMA((2,)),
            pltpu.SemaphoreType.DMA((3, count, merge)),
            pltpu.SemaphoreType.DMA((2, count, merge)),
        ],
        weight=HEAVY,
    )[0]


def lag_products(near_ref, other_ref, row_at, strip, repeats, filters, totals):
    count = near_ref.shape[0]
    sums = [None] * len(totals)
    for repeat in range(repeats):
        row = pl.ds(pl.multiple_of(repeat * filters + row_at, SUBLANES), SUBLANES)
        near = [parts(near_ref, k, row, strip) for k in range(count)]
        other = [parts(other_ref, k, row, strip) for k in range(count)]
        for at, total in enumerate(totals):
            for a in range(count):
                if 0 <= total - a < count:
                    sums[at] = add(sums[at], conj_times(near[a], other[total - a]))
    return sums


def join_lags(ref, row, joint_ref, base):
    lags, size = ref.shape[0], ref.shape[2] // 2
    sign = alternating()[:1]
    for k in range(lags):
        for strip in range(size // LANES):
            real, imag = parts(ref, k, row, strip)
            if k + 1 < lags:
                next_real, next_imag = parts(ref, k + 1, row, strip)
                real, imag = real + sign * next_imag, imag - sign * next_real
            keep(joint_ref, base + k, slice(None), strip, (real.astype(jnp.bfloat16), imag.astype(jnp.bfloat16)))


def filter_terms(near, own, filters, half_blocks, table):
    slots = [group for group, _ in own]
    _, rows, tokens = near.shape
    size, width = table.shape
    merge = size // tokens
    count = half_blocks // merge
    kept, lags = filters // 2, count * size
    repeats = rows // filters

    def kernel(near_hbm, *refs):
        own_hbm, refs = refs[: len(own)], refs[len(own) :]
        table_hbm, give_hbm, mine_hbm, theirs_hbm, stage_ref, table_ref, spec_ref, local_ref, cross_ref, joint_ref, held_ref = refs[:11]
        give_ref, mine_ref, theirs_ref, sems, stage_sems = refs[11:]
        tabled = begin([pltpu.make_async_copy(table_hbm, table_ref, sems.at[0])])
        staged, later = stage_all(near_hbm, own_hbm, slots, stage_ref, stage_sems, half_blocks)
        half, _ = place(half_blocks)
        group = lax.axis_index("dp")
        turn = jnp.where(half == 0, 1.0, -1.0).astype(jnp.float32)
        end(tabled)
        end(staged)
        end(later)
        transform(stage_ref, table_ref, spec_ref)
        near_ref, far_ref, own_ref = (spec_ref.at[which] for which in range(3))

        def local_tile(first):
            for strip in range(size // LANES):
                sums = lag_products(near_ref, own_ref, first, strip, repeats, filters, [count - 1 - k for k in range(count)])
                for k, (real, imag) in enumerate(sums):
                    keep(local_ref, k, pl.ds(first, SUBLANES), strip, (real, turn * imag))

        tile_loop(filters, local_tile)
        mine = pl.multiple_of(half * kept, SUBLANES)
        other = pl.multiple_of((1 - half) * kept, SUBLANES)
        join_lags(local_ref, pl.ds(other, kept), joint_ref, 0)
        result = back(joint_ref[:count].reshape(count * kept, width), table_ref[...]).reshape(count, kept, size)
        for k in range(count):
            give_ref[:, k * size : (k + 1) * size] = result[k].astype(jnp.bfloat16)
        sent = begin([pltpu.make_async_copy(give_ref, give_hbm, sems.at[1])])

        def cross_tile(first):
            row = pl.ds(first, SUBLANES)
            at = pl.ds(pl.multiple_of(mine + first, SUBLANES), SUBLANES)
            for strip in range(size // LANES):
                totals = [2 * count - 1 - k for k in range(1, 2 * count)]
                sums = lag_products(near_ref, far_ref, mine + first, strip, repeats, filters, totals)
                keep(cross_ref, 0, row, strip, parts(local_ref, 0, at, strip))
                for k, (real, imag) in enumerate(sums, 1):
                    value = (real, turn * imag)
                    keep(cross_ref, k, row, strip, add(value, parts(local_ref, k, at, strip)) if k < count else value)

        tile_loop(kept, cross_tile)
        join_lags(cross_ref, slice(None), joint_ref, 0)
        result = back(joint_ref[...].reshape(2 * count * kept, width), table_ref[...])
        held_ref[...] = result.reshape(2, count, kept, size)
        for k in range(count):
            columns = slice(k * size, (k + 1) * size)
            mine_ref[:, columns] = held_ref[group, k]
            theirs_ref[:, columns] = held_ref[1 - group, k].astype(jnp.bfloat16)
        sent += begin(
            [
                pltpu.make_async_copy(theirs_ref, theirs_hbm, sems.at[2]),
                pltpu.make_async_copy(mine_ref, mine_hbm, sems.at[3]),
            ]
        )
        end(sent)

    return call(
        kernel,
        "filter_terms",
        (near, *[array for _, array in own], table),
        [
            jax.ShapeDtypeStruct((kept, lags), jnp.bfloat16),
            jax.ShapeDtypeStruct((kept, lags), jnp.float32),
            jax.ShapeDtypeStruct((kept, lags), jnp.bfloat16),
        ],
        [
            pltpu.VMEM((3, count, rows, size), jnp.bfloat16),
            pltpu.VMEM(table.shape, jnp.bfloat16),
            pltpu.VMEM((3, count, rows, width), jnp.float32),
            pltpu.VMEM((count, filters, width), jnp.float32),
            pltpu.VMEM((2 * count, kept, width), jnp.float32),
            pltpu.VMEM((2 * count, kept, width), jnp.bfloat16),
            pltpu.VMEM((2, count, kept, size), jnp.float32),
            pltpu.VMEM((kept, lags), jnp.bfloat16),
            pltpu.VMEM((kept, lags), jnp.float32),
            pltpu.VMEM((kept, lags), jnp.bfloat16),
            pltpu.SemaphoreType.DMA((4,)),
            pltpu.SemaphoreType.DMA((3, count, merge)),
        ],
    )


def body(pre_gate, values, post_gate, filters, cotangent):
    blocks = lax.axis_size("ctx")
    groups = lax.axis_size("dp")
    half_blocks = blocks // 2
    local_rows, tokens = pre_gate.shape
    local_filters = filters.shape[0]
    repeats = local_rows // (local_filters * blocks)
    rows = 2 * local_filters * repeats
    table = dft_table(2 * tokens)
    arrays = (pre_gate, values, post_gate, cotangent)
    sides = [list(range(half_blocks)), list(range(half_blocks, blocks))]

    def swap(array):
        return lax.ppermute(array, "ctx", [(i, i ^ half_blocks) for i in range(blocks)])

    def other_group(array):
        return lax.ppermute(array, "dp", [(0, 1), (1, 0)])

    near, even, odd, taps = gate(arrays, filters, repeats, half_blocks)
    here = pack_taps(taps, swap(taps), half_blocks)
    odd, here = lax.optimization_barrier((odd, here))
    near = lax.all_to_all(near.reshape(blocks, rows, tokens), "ctx", split_axis=0, concat_axis=0, tiled=True)
    shape = (half_blocks // 2, rows, tokens)
    own = exchange_own(even.reshape(shape), odd.reshape(shape), half_blocks)
    filt = transform_taps(here, other_group(here), half_blocks, groups, table)

    result = results(near, own, filt, half_blocks, table)
    result, near = lax.optimization_barrier((result, near))
    returned = lax.all_to_all(
        result, "ctx", split_axis=0, concat_axis=0, tiled=True, axis_index_groups=sides
    )
    give, mine, theirs = filter_terms(near, own, 2 * local_filters, half_blocks, table)
    given = swap(give)
    to_first = lax.ppermute(give, ("dp", "ctx"), [(blocks + i, i ^ half_blocks) for i in range(blocks)])
    first = jnp.where(lax.axis_index("dp") == 0, given.astype(jnp.float32), 0.0) + to_first.astype(jnp.float32)
    terms = (mine + first, other_group(theirs))
    mixed, pre_grad, value_grad, post_grad, filter_grad = finish(
        returned.reshape(half_blocks, 2, repeats, 2, local_filters, tokens), arrays, terms
    )
    return (mixed, pre_grad, value_grad, post_grad, filter_grad)


def matmul(left, right):
    return jnp.dot(left, right, precision=lax.Precision.HIGHEST, preferred_element_type=jnp.float32)


def contract(form, left, right):
    return jnp.einsum(
        form, left, right, precision=lax.Precision.HIGHEST, preferred_element_type=jnp.float32
    )


def phases(height, width, modulus):
    product = lax.broadcasted_iota(jnp.int32, (height, width), 0) * lax.broadcasted_iota(
        jnp.int32, (height, width), 1
    )
    return (product % modulus).astype(jnp.float32) * (2.0 * math.pi / modulus)


def build_tables(blocks, tokens):
    factor = 1
    for candidate in range(1, tokens + 1):
        if tokens % candidate == 0 and candidate * candidate <= tokens:
            factor = candidate
    second = tokens // factor
    rows = blocks + 1
    total = 2 * blocks * tokens
    first_angle = phases(rows, blocks, 2 * blocks)
    twist_angle = phases(rows, tokens, total)
    inner_angle = phases(factor, factor, factor)
    middle_angle = phases(factor, second, tokens)
    outer_angle = phases(second, second, second)
    back_angle = phases(blocks, rows, 2 * blocks)
    column = lax.broadcasted_iota(jnp.int32, (blocks, rows), 1)
    weight = jnp.where((column == 0) | (column == blocks), 1.0, 2.0).astype(jnp.float32) / total
    return {
        "first_cos": jnp.cos(first_angle),
        "first_nsin": -jnp.sin(first_angle),
        "twist_cos": jnp.cos(twist_angle),
        "twist_sin": jnp.sin(twist_angle),
        "inner_cos": jnp.cos(inner_angle),
        "inner_sin": jnp.sin(inner_angle),
        "middle_cos": jnp.cos(middle_angle),
        "middle_sin": jnp.sin(middle_angle),
        "outer_cos": jnp.cos(outer_angle),
        "outer_sin": jnp.sin(outer_angle),
        "back_cos": weight * jnp.cos(back_angle),
        "back_sin": weight * jnp.sin(back_angle),
    }


def expand(table, ndim):
    return table.reshape((table.shape[0],) + (1,) * (ndim - 2) + (table.shape[1],))


def block_table(cos_part, sin_part):
    return jnp.stack([jnp.stack([cos_part, sin_part]), jnp.stack([-sin_part, cos_part])])


def wave(real_part, imag_part, tables, sign):
    shape = real_part.shape
    factor = tables["inner_cos"].shape[0]
    second = tables["outer_cos"].shape[0]
    stacked = jnp.stack(
        [real_part.reshape(-1, factor, second), imag_part.reshape(-1, factor, second)]
    )
    inner_table = block_table(tables["inner_cos"], sign * tables["inner_sin"])
    middle = contract("prab,pqac->qrcb", stacked, inner_table)
    middle_cos = tables["middle_cos"]
    middle_sin = sign * tables["middle_sin"]
    real_turn = middle[0] * middle_cos - middle[1] * middle_sin
    imag_turn = middle[0] * middle_sin + middle[1] * middle_cos
    turned = jnp.stack([real_turn, imag_turn])
    outer_table = block_table(tables["outer_cos"], sign * tables["outer_sin"])
    result = contract("prcb,pqbd->qrdc", turned, outer_table)
    return (result[0].reshape(shape), result[1].reshape(shape))


def finish_forward(real_first, imag_first, tables):
    ndim = real_first.ndim
    twist_cos = expand(tables["twist_cos"], ndim)
    twist_sin = expand(tables["twist_sin"], ndim)
    real_twist = real_first * twist_cos + imag_first * twist_sin
    imag_twist = imag_first * twist_cos - real_first * twist_sin
    return wave(real_twist, imag_twist, tables, -1.0)


def spectrum(signal, tables):
    flat = signal.reshape(signal.shape[0], -1)
    shape = (tables["first_cos"].shape[0],) + signal.shape[1:]
    real_first = matmul(tables["first_cos"], flat).reshape(shape)
    imag_first = matmul(tables["first_nsin"], flat).reshape(shape)
    return finish_forward(real_first, imag_first, tables)


def inverse_prepare(real_spec, imag_spec, tables):
    ndim = real_spec.ndim
    real_wave, imag_wave = wave(real_spec, imag_spec, tables, 1.0)
    twist_cos = expand(tables["twist_cos"], ndim)
    twist_sin = expand(tables["twist_sin"], ndim)
    real_twist = real_wave * twist_cos - imag_wave * twist_sin
    imag_twist = real_wave * twist_sin + imag_wave * twist_cos
    rows = real_spec.shape[0]
    return (real_twist.reshape(rows, -1), imag_twist.reshape(rows, -1))


def inverse_full(real_spec, imag_spec, tables):
    real_flat, imag_flat = inverse_prepare(real_spec, imag_spec, tables)
    signal = matmul(tables["back_cos"], real_flat) - matmul(tables["back_sin"], imag_flat)
    return signal.reshape((tables["back_cos"].shape[0],) + real_spec.shape[1:])


def plain_body(pre_gate, values, post_gate, filters, cotangent):
    blocks = lax.axis_size("ctx")
    groups = lax.axis_size("dp")
    local_rows = pre_gate.shape[0]
    tokens = pre_gate.shape[1]
    local_filters = filters.shape[0]
    repeats = local_rows // (local_filters * blocks)
    share = blocks // groups
    tables = build_tables(blocks, tokens)
    gated = (pre_gate.astype(jnp.float32) * values.astype(jnp.float32)).astype(jnp.bfloat16)
    conv_grad = (cotangent.astype(jnp.float32) * post_gate.astype(jnp.float32)).astype(jnp.bfloat16)
    gated_blocks = gated.reshape(repeats, blocks, local_filters, tokens)
    grad_blocks = conv_grad.reshape(repeats, blocks, local_filters, tokens)
    tap_local = jnp.transpose(filters.reshape(local_filters, share, tokens), (1, 0, 2))
    piece = lax.all_gather(tap_local, "dp", axis=0, tiled=True)
    count = piece.shape[0]
    flat = piece.reshape(count, -1)
    cos_cols = tables["first_cos"]
    sin_cols = tables["first_nsin"]
    real_first = matmul(cos_cols, flat)
    imag_first = matmul(sin_cols, flat)
    spec_shape = (blocks + 1, 1, local_filters, tokens)
    filt_real, filt_imag = finish_forward(
        real_first.reshape(spec_shape), imag_first.reshape(spec_shape), tables
    )

    def single_spectrum(received):
        signal = received.reshape(blocks, -1, received.shape[2], received.shape[3])
        return spectrum(signal.astype(jnp.float32), tables)

    gated_real, gated_imag = single_spectrum(
        lax.all_to_all(gated_blocks, "ctx", split_axis=1, concat_axis=0, tiled=True)
    )
    prod_real = gated_real * filt_real - gated_imag * filt_imag
    prod_imag = gated_real * filt_imag + gated_imag * filt_real
    result = inverse_full(prod_real, prod_imag, tables).astype(jnp.bfloat16)
    conv_chan = result.reshape(blocks * repeats, 1, local_filters, tokens)
    conv_seq = lax.all_to_all(conv_chan, "ctx", split_axis=0, concat_axis=1, tiled=True)
    grad_real, grad_imag = single_spectrum(
        lax.all_to_all(grad_blocks, "ctx", split_axis=1, concat_axis=0, tiled=True)
    )
    prod_real = filt_real * grad_real + filt_imag * grad_imag
    prod_imag = filt_real * grad_imag - filt_imag * grad_real
    result = inverse_full(prod_real, prod_imag, tables).astype(jnp.bfloat16)
    gated_chan_grad = result.reshape(blocks * repeats, 1, local_filters, tokens)
    gated_seq_grad = lax.all_to_all(gated_chan_grad, "ctx", split_axis=0, concat_axis=1, tiled=True)
    cross_real = jnp.sum(gated_real * grad_real + gated_imag * grad_imag, axis=1)
    cross_imag = jnp.sum(gated_real * grad_imag - gated_imag * grad_real, axis=1)
    wave_real, wave_imag = inverse_prepare(cross_real, cross_imag, tables)
    cos_rows = tables["back_cos"]
    sin_rows = tables["back_sin"]
    term = matmul(cos_rows, wave_real) - matmul(sin_rows, wave_imag)
    summed = lax.psum_scatter(
        term.reshape(lax.axis_size("dp") * share, local_filters, tokens).astype(jnp.bfloat16),
        "dp",
        scatter_dimension=0,
        tiled=True,
    ).astype(jnp.float32)
    filter_grad = jnp.transpose(summed, (1, 0, 2)).reshape(local_filters, share * tokens)
    conv_full = conv_seq.reshape(pre_gate.shape).astype(jnp.float32)
    gated_grad = gated_seq_grad.reshape(pre_gate.shape).astype(jnp.float32)
    mixed = (post_gate.astype(jnp.float32) * conv_full).astype(jnp.bfloat16)
    post_grad = (cotangent.astype(jnp.float32) * conv_full).astype(jnp.bfloat16)
    pre_grad = (gated_grad * values.astype(jnp.float32)).astype(jnp.bfloat16)
    value_grad = (gated_grad * pre_gate.astype(jnp.float32)).astype(jnp.bfloat16)
    return (mixed, pre_grad, value_grad, post_grad, filter_grad)


def solution(mesh):
    placed = (P("dp", "ctx"), P("dp", "ctx"), P("dp", "ctx"), P("ctx", "dp"), P("dp", "ctx"))
    groups, blocks = mesh.shape["dp"], mesh.shape["ctx"]

    def program(pre_gate, values, post_gate, filters, cotangent):
        kernels = groups == 2 and blocks >= 8 and blocks & (blocks - 1) == 0 and filters.shape[0] % 16 == 0
        return (body if kernels else plain_body)(pre_gate, values, post_gate, filters, cotangent)

    return jax.shard_map(
        program,
        mesh=mesh,
        in_specs=placed,
        out_specs=(P("dp", "ctx"), P("dp", "ctx"), P("dp", "ctx"), P("dp", "ctx"), P("ctx", "dp")),
        check_vma=False,
    )
```

profile of v0, /device:TPU:6, one launch (start us, length us, event | category | flops | bytes accessed | tf_op | source)
XLA Modules:
  0.0 73.5 jit_solution(1188406342173417024)
XLA Ops:
  0.6 2.8 %gate.1 = (bf16[2,8,4,2,16,256]{5,4,3,2,1,0:T(8,128)(2,1)}, bf16[4,4,2,16,256]{4,3,2,1,0:T(8,128)(2,1)}, bf16[4,4,2,16,256]{4,3,2,1,0:T(8,128)(2,1)}, bf16[16,2048]{1,0:T(8,128)(2,1)}) custom-call(bf16[1024,256]{1,0:T(8,128)(2,1)} %pre_ref.3, bf16[1024,256]{1,0:T(8,128)(2,1)} %value_ref.3, bf16[1024,256]{1,0:T(8,128)(2,1)} %post_ref.3, ...), custom_call_target="tpu_custom_call" | custom-call | flops 1 | bytes 1 | tf_op jit(solution)/shard_map/gate/pallas_call | solution.py:65
  3.5 2.7 %collective-permute-start = (bf16[16,2048]{1,0:T(8,128)(2,1)}, bf16[16,2048]{1,0:T(8,128)(2,1)S(1)}, u32[]{:S(2)}, u32[]{:S(2)}) collective-permute-start(bf16[16,2048]{1,0:T(8,128)(2,1)} %get-tuple-element.19.taps_ref), channel_id=1, source_target_pairs={{0,8},{1,9},{2,10},{3,11},{4,12},{5,13},{6,14},{7,15},{8,0},{9,1},... | collective-permute-start | bytes 196616 | tf_op jit(solution)/shard_map/ppermute | solution.py:566
  6.1 4.3 %all-to-all-start = ((bf16[16,128,256]{2,1,0:T(8,128)(2,1)}), bf16[16,128,256]{2,1,0:T(8,128)(2,1)S(1)}, u32[]{:S(2)}, u32[]{:S(2)}) async-start(bf16[16,128,256]{2,1,0:T(8,128)(2,1)} %bitcast.8), calls=%async_computation | async-start | bytes 2097152 | tf_op jit(solution)/shard_map/all_to_all | solution.py:574
  10.5 0.6 copy-done.12
  11.1 1.5 %pack_taps.1.here_ref = bf16[2,16,2048]{2,1,0:T(8,128)(2,1)} custom-call(bf16[16,2048]{1,0:T(8,128)(2,1)} %get-tuple-element.19.taps_ref, bf16[16,2048]{1,0:T(8,128)(2,1)} %copy-done.12), custom_call_target="tpu_custom_call" | custom-call | flops 137438953472 | bytes 137438953472 | tf_op jit(solution)/shard_map/pack_taps/pallas_call | solution.py:65
  12.9 0.6 fusion
  14.4 0.6 fusion.1
  15.5 1.7 %collective-permute-start.3 = (bf16[2,128,256]{2,1,0:T(8,128)(2,1)S(1)}, bf16[2,128,256]{2,1,0:T(8,128)(2,1)S(1)}, u32[]{:S(2)}, u32[]{:S(2)}) collective-permute-start(bf16[2,128,256]{2,1,0:T(8,128)(2,1)S(1)} %pad_maximum_fusion.1), channel_id=1, source_target_pairs={{0,4},{1,5},{2,6},{3,7},{4,0},{5,1},{6,2},{7,3},{8,12},{9,13},{10,... | collective-permute-start | bytes 393224 | tf_op jit(solution)/shard_map/ppermute | solution.py:144
  17.2 1.5 %collective-permute-start.4 = (bf16[2,128,256]{2,1,0:T(8,128)(2,1)S(1)}, bf16[2,128,256]{2,1,0:T(8,128)(2,1)S(1)}, u32[]{:S(2)}, u32[]{:S(2)}) collective-permute-start(bf16[2,128,256]{2,1,0:T(8,128)(2,1)S(1)} %pad_maximum_fusion.2), channel_id=1, source_target_pairs={{0,6},{1,7},{2,4},{3,5},{4,2},{5,3},{6,0},{7,1},{8,14},{9,15},{10,... | collective-permute-start | bytes 393224 | tf_op jit(solution)/shard_map/ppermute | solution.py:144
  18.8 0.8 %collective-permute-done.5.there_ref = bf16[2,16,2048]{2,1,0:T(8,128)(2,1)S(1)} collective-permute-done((bf16[2,16,2048]{2,1,0:T(8,128)(2,1)S(1)}, bf16[2,16,2048]{2,1,0:T(8,128)(2,1)S(1)}, u32[]{:S(2)}, u32[]{:S(2)}) %collective-permute-start.5) | collective-permute-done | bytes 131104 | tf_op jit(solution)/shard_map/ppermute | solution.py:569
  19.6 0.7 copy-done.7
  20.3 2.6 %taps.1.refs_5_ = bf16[8,32,1024]{2,1,0:T(8,128)(2,1)} custom-call(bf16[2,16,2048]{2,1,0:T(8,128)(2,1)} %pack_taps.1.here_ref, bf16[2,16,2048]{2,1,0:T(8,128)(2,1)} %copy-done.7, bf16[512,1024]{1,0:T(8,128)(2,1)} %constant.12.clone.table_hbm.refs_6_.refs_5_), custom_call_target="tpu_custom_call" | custom-call | flops 1 | bytes 1 | tf_op jit(solution)/shard_map/taps/pallas_call | solution.py:65
  22.9 1.3 %collective-permute-done.2.refs_2_ = bf16[2,128,256]{2,1,0:T(8,128)(2,1)S(1)} collective-permute-done((bf16[2,128,256]{2,1,0:T(8,128)(2,1)S(1)}, bf16[2,128,256]{2,1,0:T(8,128)(2,1)S(1)}, u32[]{:S(2)}, u32[]{:S(2)}) %collective-permute-start.2) | collective-permute-done | bytes 131104 | tf_op jit(solution)/shard_map/ppermute | solution.py:144
  24.1 7.3 %collective-permute-done.3.refs_3_ = bf16[2,128,256]{2,1,0:T(8,128)(2,1)S(1)} collective-permute-done((bf16[2,128,256]{2,1,0:T(8,128)(2,1)S(1)}, bf16[2,128,256]{2,1,0:T(8,128)(2,1)S(1)}, u32[]{:S(2)}, u32[]{:S(2)}) %collective-permute-start.3) | collective-permute-done | bytes 131104 | tf_op jit(solution)/shard_map/ppermute | solution.py:144
  31.4 4.2 %collective-permute-done.4.refs_4_ = bf16[2,128,256]{2,1,0:T(8,128)(2,1)S(1)} collective-permute-done((bf16[2,128,256]{2,1,0:T(8,128)(2,1)S(1)}, bf16[2,128,256]{2,1,0:T(8,128)(2,1)S(1)}, u32[]{:S(2)}, u32[]{:S(2)}) %collective-permute-start.4) | collective-permute-done | bytes 131104 | tf_op jit(solution)/shard_map/ppermute | solution.py:144
  35.6 0.6 copy-done.10
  36.6 8.9 %results.1 = bf16[8,2,128,256]{3,2,1,0:T(8,128)(2,1)} custom-call(bf16[16,128,256]{2,1,0:T(8,128)(2,1)} %copy-done.4, bf16[1,128,256]{2,1,0:T(8,128)(2,1)} %bitcast.9, bf16[1,128,256]{2,1,0:T(8,128)(2,1)} %get-tuple-element.34.refs_1_, bf16[2,128,256]{2,1,0:T(8,128)(2,1)} %copy-done.8, bf16[2,128,256]{2,1,0:T(8,128)(2,1)} %copy-done.9, ...), custom_call_target="tpu_custom_call" | custom-call | flops 137438953472 | bytes 137438953472 | tf_op jit(solution)/shard_map/results/pallas_call | solution.py:65
  45.5 5.0 %all-to-all-start.1 = ((bf16[8,2,128,256]{3,2,1,0:T(8,128)(2,1)}), bf16[8,2,128,256]{3,2,1,0:T(8,128)(2,1)S(1)}, u32[]{:S(2)}, u32[]{:S(2)}) async-start(bf16[8,2,128,256]{3,2,1,0:T(8,128)(2,1)} %results.1), calls=%async_computation.1 | async-start | bytes 2097152 | tf_op jit(solution)/shard_map/all_to_all | solution.py:581
  50.5 7.0 %filter_terms.1 = (bf16[16,2048]{1,0:T(8,128)(2,1)}, f32[16,2048]{1,0:T(8,128)}, bf16[16,2048]{1,0:T(8,128)(2,1)}) custom-call(bf16[16,128,256]{2,1,0:T(8,128)(2,1)} %copy-done.4, bf16[1,128,256]{2,1,0:T(8,128)(2,1)} %bitcast.10, bf16[1,128,256]{2,1,0:T(8,128)(2,1)} %get-tuple-element.34.refs_1_, bf16[2,128,256]{2,1,0:T(8,128)(2,1)} %copy-done.8, ...), custom_call_target="tpu_custom_call" | custom-call | flops 1 | bytes 1 | tf_op jit(solution)/shard_map/filter_terms/pallas_call | solution.py:65
  57.5 5.5 %collective-permute-start.7 = (bf16[16,2048]{1,0:T(8,128)(2,1)}, bf16[16,2048]{1,0:T(8,128)(2,1)S(1)}, u32[]{:S(2)}, u32[]{:S(2)}) collective-permute-start(bf16[16,2048]{1,0:T(8,128)(2,1)} %get-tuple-element.25), channel_id=1, source_target_pairs={{16,8},{17,9},{18,10},{19,11},{20,12},{21,13},{22,14},{23,15},{24,... | collective-permute-start | bytes 196616 | tf_op jit(solution)/shard_map/ppermute | solution.py:586
  63.2 2.5 %collective-permute-done.7 = bf16[16,2048]{1,0:T(8,128)(2,1)S(1)} collective-permute-done((bf16[16,2048]{1,0:T(8,128)(2,1)}, bf16[16,2048]{1,0:T(8,128)(2,1)S(1)}, u32[]{:S(2)}, u32[]{:S(2)}) %collective-permute-start.7) | collective-permute-done | bytes 65568 | tf_op jit(solution)/shard_map/ppermute | solution.py:586
  65.7 5.2 %collective-permute-done.6 = bf16[16,2048]{1,0:T(8,128)(2,1)S(1)} collective-permute-done((bf16[16,2048]{1,0:T(8,128)(2,1)}, bf16[16,2048]{1,0:T(8,128)(2,1)S(1)}, u32[]{:S(2)}, u32[]{:S(2)}) %collective-permute-start.6) | collective-permute-done | bytes 65568 | tf_op jit(solution)/shard_map/ppermute | solution.py:566
  70.9 0.9 %add_add_fusion.mine_ref = f32[16,2048]{1,0:T(8,128)S(1)} fusion(f32[16,2048]{1,0:T(8,128)} %get-tuple-element.24, bf16[16,2048]{1,0:T(8,128)(2,1)S(1)} %collective-permute-done.7, bf16[16,2048]{1,0:T(8,128)(2,1)S(1)} %collective-permute-done.6, pred[]{:T(512)S(6)} %eq.3), kind=kLoop, calls=%fused_computation.3 | loop fusion | flops 163840 | bytes 393217 | tf_op jit(solution)/shard_map/add | solution.py:588
  71.9 1.7 %finish.1 = (bf16[1024,256]{1,0:T(8,128)(2,1)}, bf16[1024,256]{1,0:T(8,128)(2,1)}, bf16[1024,256]{1,0:T(8,128)(2,1)}, bf16[1024,256]{1,0:T(8,128)(2,1)}, f32[16,2048]{1,0:T(8,128)}) custom-call(bf16[8,2,4,2,16,256]{5,4,3,2,1,0:T(8,128)(2,1)S(1)} %bitcast.7, bf16[1024,256]{1,0:T(8,128)(2,1)S(1)} %copy-done, bf16[1024,256]{1,0:T(8,128)(2,1)S(1)} %copy-done.1, ...), custom_call_target="tpu_custom_call" | custom-call | tf_op jit(solution)/shard_map/finish/pallas_call | solution.py:179
  (36 shorter events, 2.0 us)
Async XLA Ops:
  3.5 7.0 %collective-permute-start = (bf16[16,2048]{1,0:T(8,128)(2,1)}, bf16[16,2048]{1,0:T(8,128)(2,1)S(1)}, u32[]{:S(2)}, u32[]{:S(2)}) collective-permute-start(bf16[16,2048]{1,0:T(8,128)(2,1)} %get-tuple-element.19.taps_ref), channel_id=1, source_target_pairs={{0,8},{1,9},{2,10},{3,11},{4,12},{5,13},{6,14},{7,15},{8,0},{9,1},... | collective-permute-start | bytes 196616 | tf_op jit(solution)/shard_map/ppermute | solution.py:566
  6.1 29.5 %all-to-all-start = ((bf16[16,128,256]{2,1,0:T(8,128)(2,1)}), bf16[16,128,256]{2,1,0:T(8,128)(2,1)S(1)}, u32[]{:S(2)}, u32[]{:S(2)}) async-start(bf16[16,128,256]{2,1,0:T(8,128)(2,1)} %bitcast.8), calls=%async_computation | async-start | bytes 2097152 | tf_op jit(solution)/shard_map/all_to_all | solution.py:574
  10.5 2.2 %copy-start.11 = (bf16[4,4,2,16,256]{4,3,2,1,0:T(8,128)(2,1)S(1)}, bf16[4,4,2,16,256]{4,3,2,1,0:T(8,128)(2,1)}, u32[]{:S(2)}) copy-start(bf16[4,4,2,16,256]{4,3,2,1,0:T(8,128)(2,1)} %get-tuple-element.20) | copy-start | bytes 786436
  10.5 2.4 %copy-start.5 = (bf16[4,4,2,16,256]{4,3,2,1,0:T(8,128)(2,1)S(1)}, bf16[4,4,2,16,256]{4,3,2,1,0:T(8,128)(2,1)}, u32[]{:S(2)}) copy-start(bf16[4,4,2,16,256]{4,3,2,1,0:T(8,128)(2,1)} %get-tuple-element.17) | copy-start | bytes 786436
  10.5 0.6 copy-start.12
  12.7 1.7 %collective-permute-start.1 = (bf16[4,128,256]{2,1,0:T(8,128)(2,1)S(1)}, bf16[4,128,256]{2,1,0:T(8,128)(2,1)S(1)}, u32[]{:S(2)}, u32[]{:S(2)}) collective-permute-start(bf16[4,128,256]{2,1,0:T(8,128)(2,1)S(1)} %bitcast.14), channel_id=1, source_target_pairs={{0,1},{1,0},{2,3},{3,2},{4,5},{5,4},{6,7},{7,6},{8,9},{9,8},{10,11... | collective-permute-start | bytes 786440 | tf_op jit(solution)/shard_map/ppermute | solution.py:144
  12.9 0.9 %copy-start.6 = (bf16[2,16,2048]{2,1,0:T(8,128)(2,1)S(1)}, bf16[2,16,2048]{2,1,0:T(8,128)(2,1)}, u32[]{:S(2)}) copy-start(bf16[2,16,2048]{2,1,0:T(8,128)(2,1)} %pack_taps.1.here_ref) | copy-start | bytes 393220
  13.8 5.8 %collective-permute-start.5 = (bf16[2,16,2048]{2,1,0:T(8,128)(2,1)S(1)}, bf16[2,16,2048]{2,1,0:T(8,128)(2,1)S(1)}, u32[]{:S(2)}, u32[]{:S(2)}) collective-permute-start(bf16[2,16,2048]{2,1,0:T(8,128)(2,1)S(1)} %copy-done.6), channel_id=1, source_target_pairs={{0,16},{16,0},{1,17},{17,1},{2,18},{18,2},{3,19},{19,3},{4,20},{20... | collective-permute-start | bytes 393224 | tf_op jit(solution)/shard_map/ppermute | solution.py:569
  15.1 9.1 %collective-permute-start.2 = (bf16[2,128,256]{2,1,0:T(8,128)(2,1)S(1)}, bf16[2,128,256]{2,1,0:T(8,128)(2,1)S(1)}, u32[]{:S(2)}, u32[]{:S(2)}) collective-permute-start(bf16[2,128,256]{2,1,0:T(8,128)(2,1)S(1)} %pad_maximum_fusion), channel_id=1, source_target_pairs={{0,2},{1,3},{2,0},{3,1},{4,6},{5,7},{6,4},{7,5},{8,10},{9,11},{10,... | collective-permute-start | bytes 393224 | tf_op jit(solution)/shard_map/ppermute | solution.py:144
  15.5 16.0 %collective-permute-start.3 = (bf16[2,128,256]{2,1,0:T(8,128)(2,1)S(1)}, bf16[2,128,256]{2,1,0:T(8,128)(2,1)S(1)}, u32[]{:S(2)}, u32[]{:S(2)}) collective-permute-start(bf16[2,128,256]{2,1,0:T(8,128)(2,1)S(1)} %pad_maximum_fusion.1), channel_id=1, source_target_pairs={{0,4},{1,5},{2,6},{3,7},{4,0},{5,1},{6,2},{7,3},{8,12},{9,13},{10,... | collective-permute-start | bytes 393224 | tf_op jit(solution)/shard_map/ppermute | solution.py:144
  17.2 18.4 %collective-permute-start.4 = (bf16[2,128,256]{2,1,0:T(8,128)(2,1)S(1)}, bf16[2,128,256]{2,1,0:T(8,128)(2,1)S(1)}, u32[]{:S(2)}, u32[]{:S(2)}) collective-permute-start(bf16[2,128,256]{2,1,0:T(8,128)(2,1)S(1)} %pad_maximum_fusion.2), channel_id=1, source_target_pairs={{0,6},{1,7},{2,4},{3,5},{4,2},{5,3},{6,0},{7,1},{8,14},{9,15},{10,... | collective-permute-start | bytes 393224 | tf_op jit(solution)/shard_map/ppermute | solution.py:144
  19.6 0.7 copy-start.7
  24.1 11.5 %copy-start.8 = (bf16[2,128,256]{2,1,0:T(8,128)(2,1)}, bf16[2,128,256]{2,1,0:T(8,128)(2,1)S(1)}, u32[]{:S(2)}) copy-start(bf16[2,128,256]{2,1,0:T(8,128)(2,1)S(1)} %collective-permute-done.2.refs_2_) | copy-start | bytes 393220
  31.4 4.2 %copy-start.9 = (bf16[2,128,256]{2,1,0:T(8,128)(2,1)}, bf16[2,128,256]{2,1,0:T(8,128)(2,1)S(1)}, u32[]{:S(2)}) copy-start(bf16[2,128,256]{2,1,0:T(8,128)(2,1)S(1)} %collective-permute-done.3.refs_3_) | copy-start | bytes 393220
  35.6 0.7 copy-start.10
  35.6 1.0 %copy-start.4 = (bf16[16,128,256]{2,1,0:T(8,128)(2,1)}, bf16[16,128,256]{2,1,0:T(8,128)(2,1)S(1)}, u32[]{:S(2)}) copy-start(bf16[16,128,256]{2,1,0:T(8,128)(2,1)S(1)} %all-to-all-done.near_hbm) | copy-start | bytes 3145732
  45.5 26.3 %all-to-all-start.1 = ((bf16[8,2,128,256]{3,2,1,0:T(8,128)(2,1)}), bf16[8,2,128,256]{3,2,1,0:T(8,128)(2,1)S(1)}, u32[]{:S(2)}, u32[]{:S(2)}) async-start(bf16[8,2,128,256]{3,2,1,0:T(8,128)(2,1)} %results.1), calls=%async_computation.1 | async-start | bytes 2097152 | tf_op jit(solution)/shard_map/all_to_all | solution.py:581
  50.5 21.4 %copy-start = (bf16[1024,256]{1,0:T(8,128)(2,1)S(1)}, bf16[1024,256]{1,0:T(8,128)(2,1)}, u32[]{:S(2)}) copy-start(bf16[1024,256]{1,0:T(8,128)(2,1)} %pre_ref.3) | copy-start | bytes 1572868
  50.5 21.4 %copy-start.1 = (bf16[1024,256]{1,0:T(8,128)(2,1)S(1)}, bf16[1024,256]{1,0:T(8,128)(2,1)}, u32[]{:S(2)}) copy-start(bf16[1024,256]{1,0:T(8,128)(2,1)} %value_ref.3) | copy-start | bytes 1572868
  50.5 21.4 %copy-start.2 = (bf16[1024,256]{1,0:T(8,128)(2,1)S(1)}, bf16[1024,256]{1,0:T(8,128)(2,1)}, u32[]{:S(2)}) copy-start(bf16[1024,256]{1,0:T(8,128)(2,1)} %post_ref.3) | copy-start | bytes 1572868
  50.5 21.4 %copy-start.3 = (bf16[1024,256]{1,0:T(8,128)(2,1)S(1)}, bf16[1024,256]{1,0:T(8,128)(2,1)}, u32[]{:S(2)}) copy-start(bf16[1024,256]{1,0:T(8,128)(2,1)} %cot_ref.3) | copy-start | bytes 1572868
  57.5 8.2 %collective-permute-start.7 = (bf16[16,2048]{1,0:T(8,128)(2,1)}, bf16[16,2048]{1,0:T(8,128)(2,1)S(1)}, u32[]{:S(2)}, u32[]{:S(2)}) collective-permute-start(bf16[16,2048]{1,0:T(8,128)(2,1)} %get-tuple-element.25), channel_id=1, source_target_pairs={{16,8},{17,9},{18,10},{19,11},{20,12},{21,13},{22,14},{23,15},{24,... | collective-permute-start | bytes 196616 | tf_op jit(solution)/shard_map/ppermute | solution.py:586
  63.0 7.9 %collective-permute-start.6 = (bf16[16,2048]{1,0:T(8,128)(2,1)}, bf16[16,2048]{1,0:T(8,128)(2,1)S(1)}, u32[]{:S(2)}, u32[]{:S(2)}) collective-permute-start(bf16[16,2048]{1,0:T(8,128)(2,1)} %get-tuple-element.25), channel_id=1, source_target_pairs={{0,8},{1,9},{2,10},{3,11},{4,12},{5,13},{6,14},{7,15},{8,0},{9,1},... | collective-permute-start | bytes 196616 | tf_op jit(solution)/shard_map/ppermute | solution.py:566
  63.1 8.7 %collective-permute-start.8 = (bf16[16,2048]{1,0:T(8,128)(2,1)}, bf16[16,2048]{1,0:T(8,128)(2,1)S(1)}, u32[]{:S(2)}, u32[]{:S(2)}) collective-permute-start(bf16[16,2048]{1,0:T(8,128)(2,1)} %get-tuple-element.26), channel_id=1, source_target_pairs={{0,16},{16,0},{1,17},{17,1},{2,18},{18,2},{3,19},{19,3},{4,20},{20... | collective-permute-start | bytes 196616 | tf_op jit(solution)/shard_map/ppermute | solution.py:569
where the time goes:
time: 74 us; the launch traced here: 73.5 us
  Pallas kernels  24.5 us (33%)
  starting transfers between devices  22.1 us (30%)
  waiting for transfers between devices  21.3 us (29%)
  local copies, waits for them, and re-layouts  3.86 us (5%)
  other arithmetic  0.97 us (1%)
  between operations  0.84 us (1%)
    pallas_call x5, Pallas kernels, call(): pl.pallas_call(kernel, in_specs=[hbm] * len(operands), out_specs=[hbm] *...  22.9 us
    ppermute x4, waiting for transfers between devices, swap(): lax.ppermute(array, 'ctx', [(i, i ^ slot) for i in range(2 * half_blocks)])  12.7 us
    ppermute x1, starting transfers between devices, body(): lax.ppermute(give, ('dp', 'ctx'), [(blocks + i, i ^ half_blocks) for i in...  5.54 us
    ppermute x2, waiting for transfers between devices, swap(): lax.ppermute(array, 'ctx', [(i, i ^ half_blocks) for i in range(blocks)])  5.19 us
    all_to_all x1, starting transfers between devices, body(): lax.all_to_all(result, 'ctx', split_axis=0, concat_axis=0, tiled=True, ax...  4.97 us
    all_to_all x1, starting transfers between devices, body(): lax.all_to_all(near.reshape(blocks, rows, tokens), 'ctx', split_axis=0, c...  4.33 us
    ppermute x4, starting transfers between devices, swap(): lax.ppermute(array, 'ctx', [(i, i ^ slot) for i in range(2 * half_blocks)])  3.9 us
    ppermute x2, starting transfers between devices, swap(): lax.ppermute(array, 'ctx', [(i, i ^ half_blocks) for i in range(blocks)])  2.72 us
  transfers between devices with their start and end apart: 11, of which 6 were waited for; matrix products, arithmetic and copies ran while one was open for 3% of the time, Pallas kernels for 15%

commit v1 on v0

--- a/solution.py
+++ b/solution.py
@@ -151,12 +151,12 @@
     return groups
 
 
-def finish(returned, arrays, terms):
+def finish(returned, arrays):
     half_blocks, _, repeats, sides, share, tokens = returned.shape
     count, rows = repeats * sides, half_blocks * share
 
-    def kernel(recv_ref, pre_ref, value_ref, post_ref, cot_ref, mine_ref, theirs_ref, *refs):
-        out_refs, (held_ref, total_ref, sems, total_sem) = refs[:5], refs[5:]
+    def kernel(recv_ref, pre_ref, value_ref, post_ref, cot_ref, *refs):
+        out_refs, (held_ref, sems) = refs[:4], refs[4:]
         half, _ = place(half_blocks)
         sent = []
         for part in range(count):
@@ -171,25 +171,21 @@
                 sent += begin(
                     [pltpu.make_async_copy(held_ref.at[which, part], out_refs[which].at[at], sems.at[which, part])]
                 )
-        total_ref[...] = mine_ref[...] + theirs_ref[...].astype(jnp.float32)
-        sent += begin([pltpu.make_async_copy(total_ref, out_refs[4], total_sem)])
         end(sent)
 
     shapes = [jax.ShapeDtypeStruct(arrays[0].shape, jnp.bfloat16)] * 4
     return pl.pallas_call(
         kernel,
-        in_specs=[pl.BlockSpec(memory_space=pltpu.VMEM)] * 7,
-        out_specs=[pl.BlockSpec(memory_space=pltpu.HBM)] * 5,
-        out_shape=shapes + [jax.ShapeDtypeStruct(terms[0].shape, jnp.float32)],
+        in_specs=[pl.BlockSpec(memory_space=pltpu.VMEM)] * 5,
+        out_specs=[pl.BlockSpec(memory_space=pltpu.HBM)] * 4,
+        out_shape=shapes,
         scratch_shapes=[
             pltpu.VMEM((4, count, rows, tokens), jnp.bfloat16),
-            pltpu.VMEM(terms[0].shape, jnp.float32),
             pltpu.SemaphoreType.DMA((4, count)),
-            pltpu.SemaphoreType.DMA,
         ],
         compiler_params=pltpu.CompilerParams(vmem_limit_bytes=VMEM_BYTES // 6),
         name="finish",
-    )(returned, *arrays, *terms)
+    )(returned, *arrays)
 
 
 def pack_taps(taps, pair, half_blocks):
@@ -428,6 +424,7 @@
             pltpu.SemaphoreType.DMA((3, count, merge)),
             pltpu.SemaphoreType.DMA((2, count, merge)),
         ],
+        vmem=VMEM_BYTES // 2,
         weight=HEAVY,
     )[0]
 
@@ -469,8 +466,8 @@
 
     def kernel(near_hbm, *refs):
         own_hbm, refs = refs[: len(own)], refs[len(own) :]
-        table_hbm, give_hbm, mine_hbm, theirs_hbm, stage_ref, table_ref, spec_ref, local_ref, cross_ref, joint_ref, held_ref = refs[:11]
-        give_ref, mine_ref, theirs_ref, sems, stage_sems = refs[11:]
+        table_hbm, give_hbm, mine_hbm, upper_hbm, lower_hbm, stage_ref, table_ref, spec_ref, local_ref, cross_ref, joint_ref = refs[:11]
+        held_ref, give_ref, mine_ref, theirs_ref, sems, stage_sems = refs[11:]
         tabled = begin([pltpu.make_async_copy(table_hbm, table_ref, sems.at[0])])
         staged, later = stage_all(near_hbm, own_hbm, slots, stage_ref, stage_sems, half_blocks)
         half, _ = place(half_blocks)
@@ -518,8 +515,9 @@
             theirs_ref[:, columns] = held_ref[1 - group, k].astype(jnp.bfloat16)
         sent += begin(
             [
-                pltpu.make_async_copy(theirs_ref, theirs_hbm, sems.at[2]),
-                pltpu.make_async_copy(mine_ref, mine_hbm, sems.at[3]),
+                pltpu.make_async_copy(theirs_ref.at[pl.ds(0, kept // 2)], upper_hbm, sems.at[2]),
+                pltpu.make_async_copy(theirs_ref.at[pl.ds(kept // 2, kept // 2)], lower_hbm, sems.at[3]),
+                pltpu.make_async_copy(mine_ref, mine_hbm, sems.at[4]),
             ]
         )
         end(sent)
@@ -531,7 +529,8 @@
         [
             jax.ShapeDtypeStruct((kept, lags), jnp.bfloat16),
             jax.ShapeDtypeStruct((kept, lags), jnp.float32),
-            jax.ShapeDtypeStruct((kept, lags), jnp.bfloat16),
+            jax.ShapeDtypeStruct((kept // 2, lags), jnp.bfloat16),
+            jax.ShapeDtypeStruct((kept // 2, lags), jnp.bfloat16),
         ],
         [
             pltpu.VMEM((3, count, rows, size), jnp.bfloat16),
@@ -544,7 +543,7 @@
             pltpu.VMEM((kept, lags), jnp.bfloat16),
             pltpu.VMEM((kept, lags), jnp.float32),
             pltpu.VMEM((kept, lags), jnp.bfloat16),
-            pltpu.SemaphoreType.DMA((4,)),
+            pltpu.SemaphoreType.DMA((5,)),
             pltpu.SemaphoreType.DMA((3, count, merge)),
         ],
     )
@@ -581,14 +580,14 @@
     returned = lax.all_to_all(
         result, "ctx", split_axis=0, concat_axis=0, tiled=True, axis_index_groups=sides
     )
-    give, mine, theirs = filter_terms(near, own, 2 * local_filters, half_blocks, table)
-    given = swap(give)
-    to_first = lax.ppermute(give, ("dp", "ctx"), [(blocks + i, i ^ half_blocks) for i in range(blocks)])
-    first = jnp.where(lax.axis_index("dp") == 0, given.astype(jnp.float32), 0.0) + to_first.astype(jnp.float32)
-    terms = (mine + first, other_group(theirs))
-    mixed, pre_grad, value_grad, post_grad, filter_grad = finish(
-        returned.reshape(half_blocks, 2, repeats, 2, local_filters, tokens), arrays, terms
-    )
+    give, mine, upper, lower = filter_terms(near, own, 2 * local_filters, half_blocks, table)
+    to_first = [(blocks + i, i ^ half_blocks) for i in range(blocks)]
+    halves = (swap(give), lax.ppermute(give, ("dp", "ctx"), to_first))
+    theirs = jnp.concatenate([other_group(upper), other_group(lower)])
+    outputs = finish(returned.reshape(half_blocks, 2, repeats, 2, local_filters, tokens), arrays)
+    mine, mixed, pre_grad, value_grad, post_grad = lax.optimization_barrier((mine, *outputs))
+    first = jnp.where(lax.axis_index("dp") == 0, 1.0, 0.0)
+    filter_grad = mine + theirs.astype(jnp.float32) + first * (halves[0].astype(jnp.float32) + halves[1].astype(jnp.float32))
     return (mixed, pre_grad, value_grad, post_grad, filter_grad)
 
 

time: 74 us -> 71 us (0.959)
  waiting for transfers between devices: 21.3 us -> 18.2 us
  starting transfers between devices: 22.1 us -> 24.1 us
  Pallas kernels: 24.5 us -> 23 us
    ppermute x1, waiting for transfers between devices: 2.53 us -> 0.01 us  [body(): halves = (swap(give), lax.ppermute(give, ('dp', 'ctx'), to_first))]
    ppermute x2 -> x3, starting transfers between devices: 0.62 us -> 2.63 us  [other_group(): return lax.ppermute(array, 'dp', [(0, 1), (1, 0)])]
    ppermute x2, waiting for transfers between devices: 5.19 us -> 3.24 us  [swap(): lax.ppermute(array, 'ctx', [(i, i ^ half_blocks) for i in range(blocks)])]
    pallas_call x5, Pallas kernels: 22.9 us -> 21.4 us  [call(): pl.pallas_call(kernel, in_specs=[hbm] * len(operands), out_specs=[hbm] *...]
    slice x2, local copies, waits for them, and re-layouts: 1.29 us -> 0.04 us  [exchange_own(): pair = jnp.concatenate([even[at:at + 1], odd[at:at + 1]])]
    unnamed x26 -> x36, local copies, waits for them, and re-layouts: 2.57 us -> 3.64 us
    ppermute x2 -> x3, waiting for transfers between devices: 0.84 us -> 1.63 us  [other_group(): return lax.ppermute(array, 'dp', [(0, 1), (1, 0)])]
  transfers between devices with their start and end apart: 11 -> 12, of which waited for: 6 -> 7; matrix products, arithmetic and copies ran while one was open for 3% -> 0% of each run, Pallas kernels for 15% -> 18%
where the time goes in v1:
time: 71 us; the launch traced here: 70.6 us
  starting transfers between devices  24.1 us (34%)
  Pallas kernels  23 us (32%)
  waiting for transfers between devices  18.2 us (26%)
  local copies, waits for them, and re-layouts  3.68 us (5%)
  between operations  0.89 us (1%)
  other arithmetic  0.74 us (1%)
    pallas_call x5, Pallas kernels, call(): pl.pallas_call(kernel, in_specs=[hbm] * len(operands), out_specs=[hbm] *...  21.4 us
    ppermute x4, waiting for transfers between devices, swap(): lax.ppermute(array, 'ctx', [(i, i ^ slot) for i in range(2 * half_blocks)])  12.7 us
    ppermute x1, starting transfers between devices, body(): halves = (swap(give), lax.ppermute(give, ('dp', 'ctx'), to_first))  5.54 us
    all_to_all x1, starting transfers between devices, body(): lax.all_to_all(result, 'ctx', split_axis=0, concat_axis=0, tiled=True, ax...  4.96 us
    all_to_all x1, starting transfers between devices, body(): lax.all_to_all(near.reshape(blocks, rows, tokens), 'ctx', split_axis=0, c...  4.33 us
    ppermute x4, starting transfers between devices, swap(): lax.ppermute(array, 'ctx', [(i, i ^ slot) for i in range(2 * half_blocks)])  3.9 us
    unnamed x36, local copies, waits for them, and re-layouts  3.64 us
    ppermute x2, waiting for transfers between devices, swap(): lax.ppermute(array, 'ctx', [(i, i ^ half_blocks) for i in range(blocks)])  3.24 us
  transfers between devices with their start and end apart: 12, of which 7 were waited for; matrix products, arithmetic and copies ran while one was open for 0% of the time, Pallas kernels for 18%

profile of v1, /device:TPU:6, one launch (start us, length us, event | category | flops | bytes accessed | tf_op | source)
XLA Modules:
  0.0 70.6 jit_solution(8052517369827865758)
XLA Ops:
  0.6 2.8 %gate.1 = (bf16[2,8,4,2,16,256]{5,4,3,2,1,0:T(8,128)(2,1)}, bf16[4,4,2,16,256]{4,3,2,1,0:T(8,128)(2,1)}, bf16[4,4,2,16,256]{4,3,2,1,0:T(8,128)(2,1)}, bf16[16,2048]{1,0:T(8,128)(2,1)}) custom-call(bf16[1024,256]{1,0:T(8,128)(2,1)} %pre_ref.3, bf16[1024,256]{1,0:T(8,128)(2,1)} %value_ref.3, bf16[1024,256]{1,0:T(8,128)(2,1)} %post_ref.3, ...), custom_call_target="tpu_custom_call" | custom-call | flops 1 | bytes 1 | tf_op jit(solution)/shard_map/gate/pallas_call | solution.py:65
  3.5 2.7 %collective-permute-start = (bf16[16,2048]{1,0:T(8,128)(2,1)}, bf16[16,2048]{1,0:T(8,128)(2,1)S(1)}, u32[]{:S(2)}, u32[]{:S(2)}) collective-permute-start(bf16[16,2048]{1,0:T(8,128)(2,1)} %get-tuple-element.29.taps_ref), channel_id=1, source_target_pairs={{0,8},{1,9},{2,10},{3,11},{4,12},{5,13},{6,14},{7,15},{8,0},{9,1},... | collective-permute-start | bytes 196616 | tf_op jit(solution)/shard_map/ppermute | solution.py:565
  6.1 4.3 %all-to-all-start = ((bf16[16,128,256]{2,1,0:T(8,128)(2,1)}), bf16[16,128,256]{2,1,0:T(8,128)(2,1)S(1)}, u32[]{:S(2)}, u32[]{:S(2)}) async-start(bf16[16,128,256]{2,1,0:T(8,128)(2,1)} %bitcast.10), calls=%async_computation | async-start | bytes 2097152 | tf_op jit(solution)/shard_map/all_to_all | solution.py:573
  10.5 0.6 copy-done.17
  11.1 1.5 %pack_taps.1.here_ref = bf16[2,16,2048]{2,1,0:T(8,128)(2,1)} custom-call(bf16[16,2048]{1,0:T(8,128)(2,1)} %get-tuple-element.29.taps_ref, bf16[16,2048]{1,0:T(8,128)(2,1)} %copy-done.17), custom_call_target="tpu_custom_call" | custom-call | flops 137438953472 | bytes 137438953472 | tf_op jit(solution)/shard_map/pack_taps/pallas_call | solution.py:65
  12.9 0.9 %copy-done.13 = bf16[2,16,2048]{2,1,0:T(8,128)(2,1)S(1)} copy-done((bf16[2,16,2048]{2,1,0:T(8,128)(2,1)S(1)}, bf16[2,16,2048]{2,1,0:T(8,128)(2,1)}, u32[]{:S(2)}) %copy-start.13) | copy-done | bytes 131096
  14.9 1.7 %collective-permute-start.3 = (bf16[2,128,256]{2,1,0:T(8,128)(2,1)S(1)}, bf16[2,128,256]{2,1,0:T(8,128)(2,1)S(1)}, u32[]{:S(2)}, u32[]{:S(2)}) collective-permute-start(bf16[2,128,256]{2,1,0:T(8,128)(2,1)S(1)} %pad_maximum_fusion.1), channel_id=1, source_target_pairs={{0,4},{1,5},{2,6},{3,7},{4,0},{5,1},{6,2},{7,3},{8,12},{9,13},{10,... | collective-permute-start | bytes 393224 | tf_op jit(solution)/shard_map/ppermute | solution.py:144
  16.6 1.5 %collective-permute-start.4 = (bf16[2,128,256]{2,1,0:T(8,128)(2,1)S(1)}, bf16[2,128,256]{2,1,0:T(8,128)(2,1)S(1)}, u32[]{:S(2)}, u32[]{:S(2)}) collective-permute-start(bf16[2,128,256]{2,1,0:T(8,128)(2,1)S(1)} %pad_maximum_fusion.2), channel_id=1, source_target_pairs={{0,6},{1,7},{2,4},{3,5},{4,2},{5,3},{6,0},{7,1},{8,14},{9,15},{10,... | collective-permute-start | bytes 393224 | tf_op jit(solution)/shard_map/ppermute | solution.py:144
  18.2 1.4 %collective-permute-done.5.there_ref = bf16[2,16,2048]{2,1,0:T(8,128)(2,1)S(1)} collective-permute-done((bf16[2,16,2048]{2,1,0:T(8,128)(2,1)S(1)}, bf16[2,16,2048]{2,1,0:T(8,128)(2,1)S(1)}, u32[]{:S(2)}, u32[]{:S(2)}) %collective-permute-start.5) | collective-permute-done | bytes 131104 | tf_op jit(solution)/shard_map/ppermute | solution.py:568
  19.6 0.7 copy-done.14
  20.2 2.6 %taps.1.refs_5_ = bf16[8,32,1024]{2,1,0:T(8,128)(2,1)} custom-call(bf16[2,16,2048]{2,1,0:T(8,128)(2,1)} %pack_taps.1.here_ref, bf16[2,16,2048]{2,1,0:T(8,128)(2,1)} %copy-done.14, bf16[512,1024]{1,0:T(8,128)(2,1)} %constant.14.clone.table_hbm.refs_6_.refs_5_), custom_call_target="tpu_custom_call" | custom-call | flops 1 | bytes 1 | tf_op jit(solution)/shard_map/taps/pallas_call | solution.py:65
  22.9 1.2 %collective-permute-done.2.refs_2_ = bf16[2,128,256]{2,1,0:T(8,128)(2,1)S(1)} collective-permute-done((bf16[2,128,256]{2,1,0:T(8,128)(2,1)S(1)}, bf16[2,128,256]{2,1,0:T(8,128)(2,1)S(1)}, u32[]{:S(2)}, u32[]{:S(2)}) %collective-permute-start.2) | collective-permute-done | bytes 131104 | tf_op jit(solution)/shard_map/ppermute | solution.py:144
  24.1 7.4 %collective-permute-done.3.refs_3_ = bf16[2,128,256]{2,1,0:T(8,128)(2,1)S(1)} collective-permute-done((bf16[2,128,256]{2,1,0:T(8,128)(2,1)S(1)}, bf16[2,128,256]{2,1,0:T(8,128)(2,1)S(1)}, u32[]{:S(2)}, u32[]{:S(2)}) %collective-permute-start.3) | collective-permute-done | bytes 131104 | tf_op jit(solution)/shard_map/ppermute | solution.py:144
  31.4 4.2 %collective-permute-done.4.refs_4_ = bf16[2,128,256]{2,1,0:T(8,128)(2,1)S(1)} collective-permute-done((bf16[2,128,256]{2,1,0:T(8,128)(2,1)S(1)}, bf16[2,128,256]{2,1,0:T(8,128)(2,1)S(1)}, u32[]{:S(2)}, u32[]{:S(2)}) %collective-permute-start.4) | collective-permute-done | bytes 131104 | tf_op jit(solution)/shard_map/ppermute | solution.py:144
  35.6 1.4 %copy-done.6 = bf16[8,32,1024]{2,1,0:T(8,128)(2,1)S(1)} copy-done((bf16[8,32,1024]{2,1,0:T(8,128)(2,1)S(1)}, bf16[8,32,1024]{2,1,0:T(8,128)(2,1)}, u32[]{:S(2)}) %copy-start.6) | copy-done | bytes 524312
  37.1 7.4 %results.1 = bf16[8,2,128,256]{3,2,1,0:T(8,128)(2,1)} custom-call(bf16[16,128,256]{2,1,0:T(8,128)(2,1)S(1)} %all-to-all-done.near_hbm, bf16[1,128,256]{2,1,0:T(8,128)(2,1)S(1)} %bitcast.8, bf16[1,128,256]{2,1,0:T(8,128)(2,1)S(1)} %get-tuple-element.54.refs_1_, bf16[2,128,256]{2,1,0:T(8,128)(2,1)S(1)} %collective-permute-done.2.refs_2_, ...), custom_call_target="tpu_custom_call" | custom-call | flops 137438953472 | bytes 137438953472 | tf_op jit(solution)/shard_map/results/pallas_call | solution.py:65
  44.5 5.0 %all-to-all-start.1 = ((bf16[8,2,128,256]{3,2,1,0:T(8,128)(2,1)}), bf16[8,2,128,256]{3,2,1,0:T(8,128)(2,1)S(1)}, u32[]{:S(2)}, u32[]{:S(2)}) async-start(bf16[8,2,128,256]{3,2,1,0:T(8,128)(2,1)} %results.1), calls=%async_computation.1 | async-start | bytes 2097152 | tf_op jit(solution)/shard_map/all_to_all | solution.py:580
  49.5 7.0 %filter_terms.1 = (bf16[16,2048]{1,0:T(8,128)(2,1)}, f32[16,2048]{1,0:T(8,128)}, bf16[8,2048]{1,0:T(8,128)(2,1)}, bf16[8,2048]{1,0:T(8,128)(2,1)}) custom-call(bf16[16,128,256]{2,1,0:T(8,128)(2,1)} %copy-done.1, bf16[1,128,256]{2,1,0:T(8,128)(2,1)} %bitcast.9, bf16[1,128,256]{2,1,0:T(8,128)(2,1)} %copy-done.8, bf16[2,128,256]{2,1,0:T(8,128)(2,1)} %copy-done.9, ...), custom_call_target="tpu_custom_call" | custom-call | flops 1 | bytes 1 | tf_op jit(solution)/shard_map/filter_terms/pallas_call | solution.py:65
  56.5 5.5 %collective-permute-start.9 = (bf16[16,2048]{1,0:T(8,128)(2,1)}, bf16[16,2048]{1,0:T(8,128)(2,1)S(1)}, u32[]{:S(2)}, u32[]{:S(2)}) collective-permute-start(bf16[16,2048]{1,0:T(8,128)(2,1)} %get-tuple-element.46), channel_id=1, source_target_pairs={{16,8},{17,9},{18,10},{19,11},{20,12},{21,13},{22,14},{23,15},{24,... | collective-permute-start | bytes 196616 | tf_op jit(solution)/shard_map/ppermute | solution.py:585
  62.2 2.0 %collective-permute-start.6 = (bf16[8,2048]{1,0:T(8,128)(2,1)}, bf16[8,2048]{1,0:T(8,128)(2,1)S(1)}, u32[]{:S(2)}, u32[]{:S(2)}) collective-permute-start(bf16[8,2048]{1,0:T(8,128)(2,1)} %get-tuple-element.44), channel_id=1, source_target_pairs={{0,16},{16,0},{1,17},{17,1},{2,18},{18,2},{3,19},{19,3},{4,20},{20... | collective-permute-start | bytes 98312 | tf_op jit(solution)/shard_map/ppermute | solution.py:568
  64.2 0.6 all-to-all-done.1
  64.8 1.6 %finish.1 = (bf16[1024,256]{1,0:T(8,128)(2,1)}, bf16[1024,256]{1,0:T(8,128)(2,1)}, bf16[1024,256]{1,0:T(8,128)(2,1)}, bf16[1024,256]{1,0:T(8,128)(2,1)}) custom-call(bf16[8,2,4,2,16,256]{5,4,3,2,1,0:T(8,128)(2,1)S(1)} %bitcast.7, bf16[1024,256]{1,0:T(8,128)(2,1)S(1)} %copy-done.2, bf16[1024,256]{1,0:T(8,128)(2,1)S(1)} %copy-done.3, ...), custom_call_target="tpu_custom_call" | custom-call | tf_op jit(solution)/shard_map/finish/pallas_call | solution.py:177
  66.7 3.2 %collective-permute-done.8 = bf16[16,2048]{1,0:T(8,128)(2,1)S(1)} collective-permute-done((bf16[16,2048]{1,0:T(8,128)(2,1)}, bf16[16,2048]{1,0:T(8,128)(2,1)S(1)}, u32[]{:S(2)}, u32[]{:S(2)}) %collective-permute-start.8) | collective-permute-done | bytes 65568 | tf_op jit(solution)/shard_map/ppermute | solution.py:565
  69.9 0.7 multiply_add_fusion
  (48 shorter events, 1.7 us)
Async XLA Ops:
  3.5 7.0 %collective-permute-start = (bf16[16,2048]{1,0:T(8,128)(2,1)}, bf16[16,2048]{1,0:T(8,128)(2,1)S(1)}, u32[]{:S(2)}, u32[]{:S(2)}) collective-permute-start(bf16[16,2048]{1,0:T(8,128)(2,1)} %get-tuple-element.29.taps_ref), channel_id=1, source_target_pairs={{0,8},{1,9},{2,10},{3,11},{4,12},{5,13},{6,14},{7,15},{8,0},{9,1},... | collective-permute-start | bytes 196616 | tf_op jit(solution)/shard_map/ppermute | solution.py:565
  6.1 29.5 %all-to-all-start = ((bf16[16,128,256]{2,1,0:T(8,128)(2,1)}), bf16[16,128,256]{2,1,0:T(8,128)(2,1)S(1)}, u32[]{:S(2)}, u32[]{:S(2)}) async-start(bf16[16,128,256]{2,1,0:T(8,128)(2,1)} %bitcast.10), calls=%async_computation | async-start | bytes 2097152 | tf_op jit(solution)/shard_map/all_to_all | solution.py:573
  12.7 1.7 %collective-permute-start.1 = (bf16[4,128,256]{2,1,0:T(8,128)(2,1)S(1)}, bf16[4,128,256]{2,1,0:T(8,128)(2,1)S(1)}, u32[]{:S(2)}, u32[]{:S(2)}) collective-permute-start(bf16[4,128,256]{2,1,0:T(8,128)(2,1)S(1)} %bitcast.14), channel_id=1, source_target_pairs={{0,1},{1,0},{2,3},{3,2},{4,5},{5,4},{6,7},{7,6},{8,9},{9,8},{10,11... | collective-permute-start | bytes 786440 | tf_op jit(solution)/shard_map/ppermute | solution.py:144
  13.8 21.8 %copy-start.7 = (bf16[1,4,2,16,256]{4,3,2,1,0:T(8,128)(2,1)}, bf16[1,4,2,16,256]{4,3,2,1,0:T(8,128)(2,1)S(1)}, u32[]{:S(2)}) copy-start(bf16[1,4,2,16,256]{4,3,2,1,0:T(8,128)(2,1)S(1)} %get-tuple-element.50) | copy-start | bytes 196612
  13.8 5.8 %collective-permute-start.5 = (bf16[2,16,2048]{2,1,0:T(8,128)(2,1)S(1)}, bf16[2,16,2048]{2,1,0:T(8,128)(2,1)S(1)}, u32[]{:S(2)}, u32[]{:S(2)}) collective-permute-start(bf16[2,16,2048]{2,1,0:T(8,128)(2,1)S(1)} %copy-done.13), channel_id=1, source_target_pairs={{0,16},{16,0},{1,17},{17,1},{2,18},{18,2},{3,19},{19,3},{4,20},{20... | collective-permute-start | bytes 393224 | tf_op jit(solution)/shard_map/ppermute | solution.py:568
  14.4 21.2 %copy-start.8 = (bf16[1,128,256]{2,1,0:T(8,128)(2,1)}, bf16[1,128,256]{2,1,0:T(8,128)(2,1)S(1)}, u32[]{:S(2)}) copy-start(bf16[1,128,256]{2,1,0:T(8,128)(2,1)S(1)} %get-tuple-element.54.refs_1_) | copy-start | bytes 196612
  14.4 9.7 %collective-permute-start.2 = (bf16[2,128,256]{2,1,0:T(8,128)(2,1)S(1)}, bf16[2,128,256]{2,1,0:T(8,128)(2,1)S(1)}, u32[]{:S(2)}, u32[]{:S(2)}) collective-permute-start(bf16[2,128,256]{2,1,0:T(8,128)(2,1)S(1)} %pad_maximum_fusion), channel_id=1, source_target_pairs={{0,2},{1,3},{2,0},{3,1},{4,6},{5,7},{6,4},{7,5},{8,10},{9,11},{10,... | collective-permute-start | bytes 393224 | tf_op jit(solution)/shard_map/ppermute | solution.py:144
  14.9 16.6 %collective-permute-start.3 = (bf16[2,128,256]{2,1,0:T(8,128)(2,1)S(1)}, bf16[2,128,256]{2,1,0:T(8,128)(2,1)S(1)}, u32[]{:S(2)}, u32[]{:S(2)}) collective-permute-start(bf16[2,128,256]{2,1,0:T(8,128)(2,1)S(1)} %pad_maximum_fusion.1), channel_id=1, source_target_pairs={{0,4},{1,5},{2,6},{3,7},{4,0},{5,1},{6,2},{7,3},{8,12},{9,13},{10,... | collective-permute-start | bytes 393224 | tf_op jit(solution)/shard_map/ppermute | solution.py:144
  16.6 19.0 %copy-start = (bf16[512,1024]{1,0:T(8,128)(2,1)S(1)}, bf16[512,1024]{1,0:T(8,128)(2,1)}, u32[]{:S(2)}) copy-start(bf16[512,1024]{1,0:T(8,128)(2,1)} %constant.14.clone.table_hbm.refs_6_.refs_5_) | copy-start | bytes 3145732
  16.6 19.0 %collective-permute-start.4 = (bf16[2,128,256]{2,1,0:T(8,128)(2,1)S(1)}, bf16[2,128,256]{2,1,0:T(8,128)(2,1)S(1)}, u32[]{:S(2)}, u32[]{:S(2)}) collective-permute-start(bf16[2,128,256]{2,1,0:T(8,128)(2,1)S(1)} %pad_maximum_fusion.2), channel_id=1, source_target_pairs={{0,6},{1,7},{2,4},{3,5},{4,2},{5,3},{6,0},{7,1},{8,14},{9,15},{10,... | collective-permute-start | bytes 393224 | tf_op jit(solution)/shard_map/ppermute | solution.py:144
  24.1 20.4 %copy-start.9 = (bf16[2,128,256]{2,1,0:T(8,128)(2,1)}, bf16[2,128,256]{2,1,0:T(8,128)(2,1)S(1)}, u32[]{:S(2)}) copy-start(bf16[2,128,256]{2,1,0:T(8,128)(2,1)S(1)} %collective-permute-done.2.refs_2_) | copy-start | bytes 393220
  31.4 13.1 %copy-start.10 = (bf16[2,128,256]{2,1,0:T(8,128)(2,1)}, bf16[2,128,256]{2,1,0:T(8,128)(2,1)S(1)}, u32[]{:S(2)}) copy-start(bf16[2,128,256]{2,1,0:T(8,128)(2,1)S(1)} %collective-permute-done.3.refs_3_) | copy-start | bytes 393220
  35.6 8.9 %copy-start.11 = (bf16[2,128,256]{2,1,0:T(8,128)(2,1)}, bf16[2,128,256]{2,1,0:T(8,128)(2,1)S(1)}, u32[]{:S(2)}) copy-start(bf16[2,128,256]{2,1,0:T(8,128)(2,1)S(1)} %collective-permute-done.4.refs_4_) | copy-start | bytes 393220
  35.6 8.9 %copy-start.1 = (bf16[16,128,256]{2,1,0:T(8,128)(2,1)}, bf16[16,128,256]{2,1,0:T(8,128)(2,1)S(1)}, u32[]{:S(2)}) copy-start(bf16[16,128,256]{2,1,0:T(8,128)(2,1)S(1)} %all-to-all-done.near_hbm) | copy-start | bytes 3145732
  44.5 20.3 %all-to-all-start.1 = ((bf16[8,2,128,256]{3,2,1,0:T(8,128)(2,1)}), bf16[8,2,128,256]{3,2,1,0:T(8,128)(2,1)S(1)}, u32[]{:S(2)}, u32[]{:S(2)}) async-start(bf16[8,2,128,256]{3,2,1,0:T(8,128)(2,1)} %results.1), calls=%async_computation.1 | async-start | bytes 2097152 | tf_op jit(solution)/shard_map/all_to_all | solution.py:580
  49.5 15.3 %copy-start.2 = (bf16[1024,256]{1,0:T(8,128)(2,1)S(1)}, bf16[1024,256]{1,0:T(8,128)(2,1)}, u32[]{:S(2)}) copy-start(bf16[1024,256]{1,0:T(8,128)(2,1)} %pre_ref.3) | copy-start | bytes 1572868
  49.5 15.3 %copy-start.3 = (bf16[1024,256]{1,0:T(8,128)(2,1)S(1)}, bf16[1024,256]{1,0:T(8,128)(2,1)}, u32[]{:S(2)}) copy-start(bf16[1024,256]{1,0:T(8,128)(2,1)} %value_ref.3) | copy-start | bytes 1572868
  49.5 15.3 %copy-start.4 = (bf16[1024,256]{1,0:T(8,128)(2,1)S(1)}, bf16[1024,256]{1,0:T(8,128)(2,1)}, u32[]{:S(2)}) copy-start(bf16[1024,256]{1,0:T(8,128)(2,1)} %post_ref.3) | copy-start | bytes 1572868
  49.5 15.3 %copy-start.5 = (bf16[1024,256]{1,0:T(8,128)(2,1)S(1)}, bf16[1024,256]{1,0:T(8,128)(2,1)}, u32[]{:S(2)}) copy-start(bf16[1024,256]{1,0:T(8,128)(2,1)} %cot_ref.3) | copy-start | bytes 1572868
  56.5 10.2 %collective-permute-start.9 = (bf16[16,2048]{1,0:T(8,128)(2,1)}, bf16[16,2048]{1,0:T(8,128)(2,1)S(1)}, u32[]{:S(2)}, u32[]{:S(2)}) collective-permute-start(bf16[16,2048]{1,0:T(8,128)(2,1)} %get-tuple-element.46), channel_id=1, source_target_pairs={{16,8},{17,9},{18,10},{19,11},{20,12},{21,13},{22,14},{23,15},{24,... | collective-permute-start | bytes 196616 | tf_op jit(solution)/shard_map/ppermute | solution.py:585
  62.0 7.9 %collective-permute-start.8 = (bf16[16,2048]{1,0:T(8,128)(2,1)}, bf16[16,2048]{1,0:T(8,128)(2,1)S(1)}, u32[]{:S(2)}, u32[]{:S(2)}) collective-permute-start(bf16[16,2048]{1,0:T(8,128)(2,1)} %get-tuple-element.46), channel_id=1, source_target_pairs={{0,8},{1,9},{2,10},{3,11},{4,12},{5,13},{6,14},{7,15},{8,0},{9,1},... | collective-permute-start | bytes 196616 | tf_op jit(solution)/shard_map/ppermute | solution.py:565
  62.1 4.3 %collective-permute-start.7 = (bf16[8,2048]{1,0:T(8,128)(2,1)}, bf16[8,2048]{1,0:T(8,128)(2,1)S(1)}, u32[]{:S(2)}, u32[]{:S(2)}) collective-permute-start(bf16[8,2048]{1,0:T(8,128)(2,1)} %get-tuple-element.45), channel_id=1, source_target_pairs={{0,16},{16,0},{1,17},{17,1},{2,18},{18,2},{3,19},{19,3},{4,20},{20... | collective-permute-start | bytes 98312 | tf_op jit(solution)/shard_map/ppermute | solution.py:568
  62.2 4.5 %collective-permute-start.6 = (bf16[8,2048]{1,0:T(8,128)(2,1)}, bf16[8,2048]{1,0:T(8,128)(2,1)S(1)}, u32[]{:S(2)}, u32[]{:S(2)}) collective-permute-start(bf16[8,2048]{1,0:T(8,128)(2,1)} %get-tuple-element.44), channel_id=1, source_target_pairs={{0,16},{16,0},{1,17},{17,1},{2,18},{18,2},{3,19},{19,3},{4,20},{20... | collective-permute-start | bytes 98312 | tf_op jit(solution)/shard_map/ppermute | solution.py:568
  64.8 5.1 %copy-start.15 = (f32[16,2048]{1,0:T(8,128)S(1)}, f32[16,2048]{1,0:T(8,128)}, u32[]{:S(2)}) copy-start(f32[16,2048]{1,0:T(8,128)} %get-tuple-element.43) | copy-start | bytes 393220
  (6 other events, 8.3 us)

commit v2 on v1

--- a/solution.py
+++ b/solution.py
@@ -60,11 +60,11 @@
         copy.wait()
 
 
-def call(kernel, name, operands, outputs, scratch, weight=1, vmem=VMEM_BYTES):
+def call(kernel, name, operands, outputs, scratch, weight=1, vmem=VMEM_BYTES, space=pltpu.HBM):
     hbm = pl.BlockSpec(memory_space=pltpu.HBM)
     return pl.pallas_call(
         kernel,
-        in_specs=[hbm] * len(operands),
+        in_specs=[pl.BlockSpec(memory_space=space)] * len(operands),
         out_specs=[hbm] * len(outputs),
         out_shape=outputs,
         scratch_shapes=scratch,
@@ -210,6 +210,7 @@
         [jax.ShapeDtypeStruct((2, share, lags), jnp.bfloat16)],
         [pltpu.VMEM((2, share, lags), jnp.bfloat16), pltpu.SemaphoreType.DMA((3,))],
         weight=HEAVY,
+        vmem=VMEM_BYTES // 12,
     )[0]
 
 
@@ -261,6 +262,7 @@
             pltpu.VMEM((count, rows, width), jnp.bfloat16),
             pltpu.SemaphoreType.DMA((3 + count,)),
         ],
+        vmem=VMEM_BYTES // 6,
     )[0]
 
 
@@ -359,18 +361,24 @@
     count = half_blocks // merge
     filters = filt.shape[1]
 
-    def kernel(near_hbm, *refs):
-        own_hbm, (filt_hbm, table_hbm, out_hbm) = refs[: len(own)], refs[len(own) : len(own) + 3]
-        stage_ref, filt_in, filt_ref, table_ref, spec_ref, prod_ref, held_ref, sems, stage_sems, out_sems = refs[len(own) + 3 :]
-        tabled = begin([pltpu.make_async_copy(table_hbm, table_ref, sems.at[0])])
-        staged, later = stage_all(near_hbm, own_hbm, slots, stage_ref, stage_sems, half_blocks)
-        rest = begin([pltpu.make_async_copy(filt_hbm, filt_in, sems.at[1])])
-        end(staged)
-        end(tabled)
-        end(later)
+    def kernel(near_ref, *refs):
+        own_refs, (filt_in, table_ref, out_hbm) = refs[: len(own)], refs[len(own) : len(own) + 3]
+        stage_ref, filt_ref, spec_ref, prod_ref, held_ref, out_sems = refs[len(own) + 3 :]
+        half, me = place(half_blocks)
+        for k in range(count):
+            for q in range(merge):
+                lanes = pl.ds(q * tokens, tokens)
+                outer, inner = order(k, count, half, True), order(k, count, half, False)
+                stage_ref[0, k, :, lanes] = near_ref[half * half_blocks + outer * merge + q]
+                stage_ref[1, k, :, lanes] = near_ref[(1 - half) * half_blocks + inner * merge + q]
+        for group, ref in zip(slots, own_refs):
+            for at, slot in enumerate(group):
+                position = jnp.bitwise_xor(me, slot)
+                k = order(position // merge, count, half, False)
+                start = pl.multiple_of(lax.rem(position, merge) * tokens, tokens)
+                stage_ref[2, k, :, pl.ds(start, tokens)] = ref[at]
+        filt_ref[...] = filt_in[...].astype(jnp.float32)
         transform(stage_ref, table_ref, spec_ref)
-        end(rest)
-        filt_ref[...] = filt_in[...].astype(jnp.float32)
 
         def tile(first):
             row = pl.ds(first, SUBLANES)
@@ -392,7 +400,6 @@
                     keep(prod_ref.at[1], out, row, strip, total)
 
         tile_loop(rows, tile)
-        half, _ = place(half_blocks)
         spectrum = prod_ref[...].astype(jnp.bfloat16).reshape(2 * count * rows, width)
         sent = []
         for q in range(merge):
@@ -414,18 +421,15 @@
         [jax.ShapeDtypeStruct((half_blocks, 2, rows, tokens), jnp.bfloat16)],
         [
             pltpu.VMEM((3, count, rows, size), jnp.bfloat16),
-            pltpu.VMEM((2 * count, filters, width), jnp.bfloat16),
             pltpu.VMEM((2 * count, filters, width), jnp.float32),
-            pltpu.VMEM(table.shape, jnp.bfloat16),
             pltpu.VMEM((3, count, rows, width), jnp.float32),
             pltpu.VMEM((2, count, rows, width), jnp.float32),
             pltpu.VMEM((2, count, merge, rows, tokens), jnp.bfloat16),
-            pltpu.SemaphoreType.DMA((2,)),
-            pltpu.SemaphoreType.DMA((3, count, merge)),
             pltpu.SemaphoreType.DMA((2, count, merge)),
         ],
         vmem=VMEM_BYTES // 2,
         weight=HEAVY,
+        space=pltpu.VMEM,
     )[0]
 
 

time: 71 us -> 69.1 us (0.973)
  waiting for transfers between devices: 18.2 us -> 21.9 us
  local copies, waits for them, and re-layouts: 3.68 us -> 0.61 us
  Pallas kernels: 23 us -> 20.4 us
    ppermute x4, waiting for transfers between devices: 12.7 us -> 17.1 us  [swap(): lax.ppermute(array, 'ctx', [(i, i ^ slot) for i in range(2 * half_blocks)])]
    unnamed x36 -> x30, local copies, waits for them, and re-layouts: 3.64 us -> 0.58 us
    pallas_call x5, Pallas kernels: 21.4 us -> 18.8 us  [call(): pl.pallas_call(kernel, in_specs=[pl.BlockSpec(memory_space=space)] * len(...]
    ppermute x3, waiting for transfers between devices: 1.63 us -> 0.9 us  [other_group(): return lax.ppermute(array, 'dp', [(0, 1), (1, 0)])]
  transfers between devices with their start and end apart: 12 -> 12, of which waited for: 7 -> 8; matrix products, arithmetic and copies ran while one was open for 0% -> 0% of each run, Pallas kernels for 18% -> 16%
where the time goes in v2:
time: 69.1 us; the launch traced here: 68.7 us
  starting transfers between devices  24.2 us (35%)
  waiting for transfers between devices  21.9 us (32%)
  Pallas kernels  20.4 us (30%)
  between operations  0.88 us (1%)
  other arithmetic  0.74 us (1%)
    pallas_call x5, Pallas kernels, call(): pl.pallas_call(kernel, in_specs=[pl.BlockSpec(memory_space=space)] * len(...  18.8 us
    ppermute x4, waiting for transfers between devices, swap(): lax.ppermute(array, 'ctx', [(i, i ^ slot) for i in range(2 * half_blocks)])  17.1 us
    ppermute x1, starting transfers between devices, body(): halves = (swap(give), lax.ppermute(give, ('dp', 'ctx'), to_first))  5.56 us
    all_to_all x1, starting transfers between devices, body(): lax.all_to_all(result, 'ctx', split_axis=0, concat_axis=0, tiled=True, ax...  4.97 us
    all_to_all x1, starting transfers between devices, body(): lax.all_to_all(near.reshape(blocks, rows, tokens), 'ctx', split_axis=0, c...  4.46 us
    ppermute x4, starting transfers between devices, swap(): lax.ppermute(array, 'ctx', [(i, i ^ slot) for i in range(2 * half_blocks)])  3.83 us
    ppermute x2, waiting for transfers between devices, swap(): lax.ppermute(array, 'ctx', [(i, i ^ half_blocks) for i in range(blocks)])  3.26 us
    ppermute x2, starting transfers between devices, swap(): lax.ppermute(array, 'ctx', [(i, i ^ half_blocks) for i in range(blocks)])  2.72 us
  transfers between devices with their start and end apart: 12, of which 8 were waited for; matrix products, arithmetic and copies ran while one was open for 0% of the time, Pallas kernels for 16%

profile of v2, /device:TPU:6, one launch (start us, length us, event | category | flops | bytes accessed | tf_op | source)
XLA Modules:
  0.0 68.7 jit_solution(1519368682075354696)
XLA Ops:
  0.6 2.8 %gate.1 = (bf16[2,8,4,2,16,256]{5,4,3,2,1,0:T(8,128)(2,1)}, bf16[4,4,2,16,256]{4,3,2,1,0:T(8,128)(2,1)}, bf16[4,4,2,16,256]{4,3,2,1,0:T(8,128)(2,1)}, bf16[16,2048]{1,0:T(8,128)(2,1)}) custom-call(bf16[1024,256]{1,0:T(8,128)(2,1)} %pre_ref.3, bf16[1024,256]{1,0:T(8,128)(2,1)} %value_ref.3, bf16[1024,256]{1,0:T(8,128)(2,1)} %post_ref.3, ...), custom_call_target="tpu_custom_call" | custom-call | flops 1 | bytes 1 | tf_op jit(solution)/shard_map/gate/pallas_call | solution.py:65
  3.5 2.7 %collective-permute-start = (bf16[16,2048]{1,0:T(8,128)(2,1)}, bf16[16,2048]{1,0:T(8,128)(2,1)S(1)}, u32[]{:S(2)}, u32[]{:S(2)}) collective-permute-start(bf16[16,2048]{1,0:T(8,128)(2,1)} %get-tuple-element.29.taps_ref), channel_id=1, source_target_pairs={{0,8},{1,9},{2,10},{3,11},{4,12},{5,13},{6,14},{7,15},{8,0},{9,1},... | collective-permute-start | bytes 196616 | tf_op jit(solution)/shard_map/ppermute | solution.py:569
  6.1 4.5 %all-to-all-start = ((bf16[16,128,256]{2,1,0:T(8,128)(2,1)}), bf16[16,128,256]{2,1,0:T(8,128)(2,1)S(1)}, u32[]{:S(2)}, u32[]{:S(2)}) async-start(bf16[16,128,256]{2,1,0:T(8,128)(2,1)} %bitcast.10), calls=%async_computation | async-start | bytes 2097152 | tf_op jit(solution)/shard_map/all_to_all | solution.py:577
  10.6 0.4 pack_taps.1.here_ref
  11.0 0.5 copy-done.14
  11.7 0.6 collective-permute-start.5
  12.4 0.7 %collective-permute-done.1 = bf16[4,128,256]{2,1,0:T(8,128)(2,1)S(1)} collective-permute-done((bf16[4,128,256]{2,1,0:T(8,128)(2,1)S(1)}, bf16[4,128,256]{2,1,0:T(8,128)(2,1)S(1)}, u32[]{:S(2)}, u32[]{:S(2)}) %collective-permute-start.1) | collective-permute-done | bytes 262176 | tf_op jit(solution)/shard_map/ppermute | solution.py:144
  13.1 0.2 collective-permute-start.2
  13.4 1.9 %collective-permute-start.3 = (bf16[2,128,256]{2,1,0:T(8,128)(2,1)S(1)}, bf16[2,128,256]{2,1,0:T(8,128)(2,1)S(1)}, u32[]{:S(2)}, u32[]{:S(2)}) collective-permute-start(bf16[2,128,256]{2,1,0:T(8,128)(2,1)S(1)} %pad_maximum_fusion.1), channel_id=1, source_target_pairs={{0,4},{1,5},{2,6},{3,7},{4,0},{5,1},{6,2},{7,3},{8,12},{9,13},{10,... | collective-permute-start | bytes 393224 | tf_op jit(solution)/shard_map/ppermute | solution.py:144
  15.3 1.5 %collective-permute-start.4 = (bf16[2,128,256]{2,1,0:T(8,128)(2,1)S(1)}, bf16[2,128,256]{2,1,0:T(8,128)(2,1)S(1)}, u32[]{:S(2)}, u32[]{:S(2)}) collective-permute-start(bf16[2,128,256]{2,1,0:T(8,128)(2,1)S(1)} %pad_maximum_fusion.2), channel_id=1, source_target_pairs={{0,6},{1,7},{2,4},{3,5},{4,2},{5,3},{6,0},{7,1},{8,14},{9,15},{10,... | collective-permute-start | bytes 393224 | tf_op jit(solution)/shard_map/ppermute | solution.py:144
  16.9 0.7 %collective-permute-done.5.there_ref = bf16[2,16,2048]{2,1,0:T(8,128)(2,1)S(1)} collective-permute-done((bf16[2,16,2048]{2,1,0:T(8,128)(2,1)S(1)}, bf16[2,16,2048]{2,1,0:T(8,128)(2,1)S(1)}, u32[]{:S(2)}, u32[]{:S(2)}) %collective-permute-start.5) | collective-permute-done | bytes 131104 | tf_op jit(solution)/shard_map/ppermute | solution.py:572
  17.6 1.8 %taps.1.refs_5_ = bf16[8,32,1024]{2,1,0:T(8,128)(2,1)S(1)} custom-call(bf16[2,16,2048]{2,1,0:T(8,128)(2,1)S(1)} %pack_taps.1.here_ref, bf16[2,16,2048]{2,1,0:T(8,128)(2,1)S(1)} %collective-permute-done.5.there_ref, bf16[512,1024]{1,0:T(8,128)(2,1)S(1)} %copy-done), custom_call_target="tpu_custom_call" | custom-call | flops 1 | bytes 1 | tf_op jit(solution)/shard_map/taps/pallas_call | solution.py:65
  19.3 3.8 %collective-permute-done.2.refs_2_ = bf16[2,128,256]{2,1,0:T(8,128)(2,1)S(1)} collective-permute-done((bf16[2,128,256]{2,1,0:T(8,128)(2,1)S(1)}, bf16[2,128,256]{2,1,0:T(8,128)(2,1)S(1)}, u32[]{:S(2)}, u32[]{:S(2)}) %collective-permute-start.2) | collective-permute-done | bytes 131104 | tf_op jit(solution)/shard_map/ppermute | solution.py:144
  23.2 8.4 %collective-permute-done.3.refs_3_ = bf16[2,128,256]{2,1,0:T(8,128)(2,1)S(1)} collective-permute-done((bf16[2,128,256]{2,1,0:T(8,128)(2,1)S(1)}, bf16[2,128,256]{2,1,0:T(8,128)(2,1)S(1)}, u32[]{:S(2)}, u32[]{:S(2)}) %collective-permute-start.3) | collective-permute-done | bytes 131104 | tf_op jit(solution)/shard_map/ppermute | solution.py:144
  31.6 4.2 %collective-permute-done.4.refs_4_ = bf16[2,128,256]{2,1,0:T(8,128)(2,1)S(1)} collective-permute-done((bf16[2,128,256]{2,1,0:T(8,128)(2,1)S(1)}, bf16[2,128,256]{2,1,0:T(8,128)(2,1)S(1)}, u32[]{:S(2)}, u32[]{:S(2)}) %collective-permute-start.4) | collective-permute-done | bytes 131104 | tf_op jit(solution)/shard_map/ppermute | solution.py:144
  35.8 6.8 %results.1 = bf16[8,2,128,256]{3,2,1,0:T(8,128)(2,1)} custom-call(bf16[16,128,256]{2,1,0:T(8,128)(2,1)S(1)} %all-to-all-done.near_ref.near_hbm, bf16[1,128,256]{2,1,0:T(8,128)(2,1)S(1)} %bitcast.8, bf16[1,128,256]{2,1,0:T(8,128)(2,1)S(1)} %get-tuple-element.54.refs_1_, bf16[2,128,256]{2,1,0:T(8,128)(2,1)S(1)} %collective-permute-done.2.refs_2_, ...), custom_call_target="tpu_custom_call" | custom-call | flops 137438953472 | bytes 137438953472 | tf_op jit(solution)/shard_map/results/pallas_call | solution.py:65
  42.6 5.0 %all-to-all-start.1 = ((bf16[8,2,128,256]{3,2,1,0:T(8,128)(2,1)}), bf16[8,2,128,256]{3,2,1,0:T(8,128)(2,1)S(1)}, u32[]{:S(2)}, u32[]{:S(2)}) async-start(bf16[8,2,128,256]{3,2,1,0:T(8,128)(2,1)} %results.1), calls=%async_computation.1 | async-start | bytes 2097152 | tf_op jit(solution)/shard_map/all_to_all | solution.py:584
  47.6 7.0 %filter_terms.1 = (bf16[16,2048]{1,0:T(8,128)(2,1)}, f32[16,2048]{1,0:T(8,128)}, bf16[8,2048]{1,0:T(8,128)(2,1)}, bf16[8,2048]{1,0:T(8,128)(2,1)}) custom-call(bf16[16,128,256]{2,1,0:T(8,128)(2,1)} %copy-done.1, bf16[1,128,256]{2,1,0:T(8,128)(2,1)} %bitcast.9, bf16[1,128,256]{2,1,0:T(8,128)(2,1)} %copy-done.7, bf16[2,128,256]{2,1,0:T(8,128)(2,1)} %copy-done.8, ...), custom_call_target="tpu_custom_call" | custom-call | flops 1 | bytes 1 | tf_op jit(solution)/shard_map/filter_terms/pallas_call | solution.py:65
  54.6 5.6 %collective-permute-start.9 = (bf16[16,2048]{1,0:T(8,128)(2,1)}, bf16[16,2048]{1,0:T(8,128)(2,1)S(1)}, u32[]{:S(2)}, u32[]{:S(2)}) collective-permute-start(bf16[16,2048]{1,0:T(8,128)(2,1)} %get-tuple-element.46), channel_id=1, source_target_pairs={{16,8},{17,9},{18,10},{19,11},{20,12},{21,13},{22,14},{23,15},{24,... | collective-permute-start | bytes 196616 | tf_op jit(solution)/shard_map/ppermute | solution.py:589
  60.3 2.0 %collective-permute-start.6 = (bf16[8,2048]{1,0:T(8,128)(2,1)}, bf16[8,2048]{1,0:T(8,128)(2,1)S(1)}, u32[]{:S(2)}, u32[]{:S(2)}) collective-permute-start(bf16[8,2048]{1,0:T(8,128)(2,1)} %get-tuple-element.44), channel_id=1, source_target_pairs={{0,16},{16,0},{1,17},{17,1},{2,18},{18,2},{3,19},{19,3},{4,20},{20... | collective-permute-start | bytes 98312 | tf_op jit(solution)/shard_map/ppermute | solution.py:572
  62.3 0.6 all-to-all-done.1
  62.9 1.6 %finish.1 = (bf16[1024,256]{1,0:T(8,128)(2,1)}, bf16[1024,256]{1,0:T(8,128)(2,1)}, bf16[1024,256]{1,0:T(8,128)(2,1)}, bf16[1024,256]{1,0:T(8,128)(2,1)}) custom-call(bf16[8,2,4,2,16,256]{5,4,3,2,1,0:T(8,128)(2,1)S(1)} %bitcast.7, bf16[1024,256]{1,0:T(8,128)(2,1)S(1)} %copy-done.2, bf16[1024,256]{1,0:T(8,128)(2,1)S(1)} %copy-done.3, ...), custom_call_target="tpu_custom_call" | custom-call | tf_op jit(solution)/shard_map/finish/pallas_call | solution.py:177
  64.8 3.3 %collective-permute-done.8 = bf16[16,2048]{1,0:T(8,128)(2,1)S(1)} collective-permute-done((bf16[16,2048]{1,0:T(8,128)(2,1)}, bf16[16,2048]{1,0:T(8,128)(2,1)S(1)}, u32[]{:S(2)}, u32[]{:S(2)}) %collective-permute-start.8) | collective-permute-done | bytes 65568 | tf_op jit(solution)/shard_map/ppermute | solution.py:569
  68.0 0.7 %multiply_add_fusion = f32[16,2048]{1,0:T(8,128)} fusion(bf16[16,2048]{1,0:T(8,128)(2,1)S(1)} %collective-permute-done.9, bf16[16,2048]{1,0:T(8,128)(2,1)S(1)} %collective-permute-done.8, f32[16,2048]{1,0:T(8,128)S(1)} %copy-done.13, bf16[8,2048]{1,0:T(8,128)(2,1)S(1)} %collective-permute-done.7, bf16[8,2048]{1,0:T(8,128)(2,1)S(1)} %collective-permute-done.6, ...), kind=kLoop, calls=%fused_computation.3 | loop fusion | flops 327680 | bytes 458756 | tf_op jit(solution)/shard_map/add | solution.py:594
  (42 shorter events, 0.6 us)
Async XLA Ops:
  3.5 7.1 %collective-permute-start = (bf16[16,2048]{1,0:T(8,128)(2,1)}, bf16[16,2048]{1,0:T(8,128)(2,1)S(1)}, u32[]{:S(2)}, u32[]{:S(2)}) collective-permute-start(bf16[16,2048]{1,0:T(8,128)(2,1)} %get-tuple-element.29.taps_ref), channel_id=1, source_target_pairs={{0,8},{1,9},{2,10},{3,11},{4,12},{5,13},{6,14},{7,15},{8,0},{9,1},... | collective-permute-start | bytes 196616 | tf_op jit(solution)/shard_map/ppermute | solution.py:569
  6.1 29.6 %all-to-all-start = ((bf16[16,128,256]{2,1,0:T(8,128)(2,1)}), bf16[16,128,256]{2,1,0:T(8,128)(2,1)S(1)}, u32[]{:S(2)}, u32[]{:S(2)}) async-start(bf16[16,128,256]{2,1,0:T(8,128)(2,1)} %bitcast.10), calls=%async_computation | async-start | bytes 2097152 | tf_op jit(solution)/shard_map/all_to_all | solution.py:577
  11.0 6.5 %copy-start = (bf16[512,1024]{1,0:T(8,128)(2,1)S(1)}, bf16[512,1024]{1,0:T(8,128)(2,1)}, u32[]{:S(2)}) copy-start(bf16[512,1024]{1,0:T(8,128)(2,1)} %constant.14.clone.table_hbm.refs_6_.refs_5_) | copy-start | bytes 3145732
  11.6 1.5 %collective-permute-start.1 = (bf16[4,128,256]{2,1,0:T(8,128)(2,1)S(1)}, bf16[4,128,256]{2,1,0:T(8,128)(2,1)S(1)}, u32[]{:S(2)}, u32[]{:S(2)}) collective-permute-start(bf16[4,128,256]{2,1,0:T(8,128)(2,1)S(1)} %bitcast.14), channel_id=1, source_target_pairs={{0,1},{1,0},{2,3},{3,2},{4,5},{5,4},{6,7},{7,6},{8,9},{9,8},{10,11... | collective-permute-start | bytes 786440 | tf_op jit(solution)/shard_map/ppermute | solution.py:144
  11.7 24.0 %copy-start.6 = (bf16[1,4,2,16,256]{4,3,2,1,0:T(8,128)(2,1)}, bf16[1,4,2,16,256]{4,3,2,1,0:T(8,128)(2,1)S(1)}, u32[]{:S(2)}) copy-start(bf16[1,4,2,16,256]{4,3,2,1,0:T(8,128)(2,1)S(1)} %get-tuple-element.50) | copy-start | bytes 196612
  11.7 5.8 %collective-permute-start.5 = (bf16[2,16,2048]{2,1,0:T(8,128)(2,1)S(1)}, bf16[2,16,2048]{2,1,0:T(8,128)(2,1)S(1)}, u32[]{:S(2)}, u32[]{:S(2)}) collective-permute-start(bf16[2,16,2048]{2,1,0:T(8,128)(2,1)S(1)} %pack_taps.1.here_ref), channel_id=1, source_target_pairs={{0,16},{16,0},{1,17},{17,1},{2,18},{18,2},{3,19},{19,3},{4,20},{20... | collective-permute-start | bytes 393224 | tf_op jit(solution)/shard_map/ppermute | solution.py:572
  13.1 22.6 %copy-start.7 = (bf16[1,128,256]{2,1,0:T(8,128)(2,1)}, bf16[1,128,256]{2,1,0:T(8,128)(2,1)S(1)}, u32[]{:S(2)}) copy-start(bf16[1,128,256]{2,1,0:T(8,128)(2,1)S(1)} %get-tuple-element.54.refs_1_) | copy-start | bytes 196612
  13.1 10.0 %collective-permute-start.2 = (bf16[2,128,256]{2,1,0:T(8,128)(2,1)S(1)}, bf16[2,128,256]{2,1,0:T(8,128)(2,1)S(1)}, u32[]{:S(2)}, u32[]{:S(2)}) collective-permute-start(bf16[2,128,256]{2,1,0:T(8,128)(2,1)S(1)} %pad_maximum_fusion), channel_id=1, source_target_pairs={{0,2},{1,3},{2,0},{3,1},{4,6},{5,7},{6,4},{7,5},{8,10},{9,11},{10,... | collective-permute-start | bytes 393224 | tf_op jit(solution)/shard_map/ppermute | solution.py:144
  13.4 18.2 %collective-permute-start.3 = (bf16[2,128,256]{2,1,0:T(8,128)(2,1)S(1)}, bf16[2,128,256]{2,1,0:T(8,128)(2,1)S(1)}, u32[]{:S(2)}, u32[]{:S(2)}) collective-permute-start(bf16[2,128,256]{2,1,0:T(8,128)(2,1)S(1)} %pad_maximum_fusion.1), channel_id=1, source_target_pairs={{0,4},{1,5},{2,6},{3,7},{4,0},{5,1},{6,2},{7,3},{8,12},{9,13},{10,... | collective-permute-start | bytes 393224 | tf_op jit(solution)/shard_map/ppermute | solution.py:144
  15.3 20.4 %collective-permute-start.4 = (bf16[2,128,256]{2,1,0:T(8,128)(2,1)S(1)}, bf16[2,128,256]{2,1,0:T(8,128)(2,1)S(1)}, u32[]{:S(2)}, u32[]{:S(2)}) collective-permute-start(bf16[2,128,256]{2,1,0:T(8,128)(2,1)S(1)} %pad_maximum_fusion.2), channel_id=1, source_target_pairs={{0,6},{1,7},{2,4},{3,5},{4,2},{5,3},{6,0},{7,1},{8,14},{9,15},{10,... | collective-permute-start | bytes 393224 | tf_op jit(solution)/shard_map/ppermute | solution.py:144
  23.1 19.4 %copy-start.8 = (bf16[2,128,256]{2,1,0:T(8,128)(2,1)}, bf16[2,128,256]{2,1,0:T(8,128)(2,1)S(1)}, u32[]{:S(2)}) copy-start(bf16[2,128,256]{2,1,0:T(8,128)(2,1)S(1)} %collective-permute-done.2.refs_2_) | copy-start | bytes 393220
  31.6 11.0 %copy-start.9 = (bf16[2,128,256]{2,1,0:T(8,128)(2,1)}, bf16[2,128,256]{2,1,0:T(8,128)(2,1)S(1)}, u32[]{:S(2)}) copy-start(bf16[2,128,256]{2,1,0:T(8,128)(2,1)S(1)} %collective-permute-done.3.refs_3_) | copy-start | bytes 393220
  35.7 6.9 %copy-start.10 = (bf16[2,128,256]{2,1,0:T(8,128)(2,1)}, bf16[2,128,256]{2,1,0:T(8,128)(2,1)S(1)}, u32[]{:S(2)}) copy-start(bf16[2,128,256]{2,1,0:T(8,128)(2,1)S(1)} %collective-permute-done.4.refs_4_) | copy-start | bytes 393220
  35.7 6.9 %copy-start.1 = (bf16[16,128,256]{2,1,0:T(8,128)(2,1)}, bf16[16,128,256]{2,1,0:T(8,128)(2,1)S(1)}, u32[]{:S(2)}) copy-start(bf16[16,128,256]{2,1,0:T(8,128)(2,1)S(1)} %all-to-all-done.near_ref.near_hbm) | copy-start | bytes 3145732
  42.6 20.3 %all-to-all-start.1 = ((bf16[8,2,128,256]{3,2,1,0:T(8,128)(2,1)}), bf16[8,2,128,256]{3,2,1,0:T(8,128)(2,1)S(1)}, u32[]{:S(2)}, u32[]{:S(2)}) async-start(bf16[8,2,128,256]{3,2,1,0:T(8,128)(2,1)} %results.1), calls=%async_computation.1 | async-start | bytes 2097152 | tf_op jit(solution)/shard_map/all_to_all | solution.py:584
  47.6 15.3 %copy-start.2 = (bf16[1024,256]{1,0:T(8,128)(2,1)S(1)}, bf16[1024,256]{1,0:T(8,128)(2,1)}, u32[]{:S(2)}) copy-start(bf16[1024,256]{1,0:T(8,128)(2,1)} %pre_ref.3) | copy-start | bytes 1572868
  47.6 15.3 %copy-start.3 = (bf16[1024,256]{1,0:T(8,128)(2,1)S(1)}, bf16[1024,256]{1,0:T(8,128)(2,1)}, u32[]{:S(2)}) copy-start(bf16[1024,256]{1,0:T(8,128)(2,1)} %value_ref.3) | copy-start | bytes 1572868
  47.6 15.3 %copy-start.4 = (bf16[1024,256]{1,0:T(8,128)(2,1)S(1)}, bf16[1024,256]{1,0:T(8,128)(2,1)}, u32[]{:S(2)}) copy-start(bf16[1024,256]{1,0:T(8,128)(2,1)} %post_ref.3) | copy-start | bytes 1572868
  47.6 15.3 %copy-start.5 = (bf16[1024,256]{1,0:T(8,128)(2,1)S(1)}, bf16[1024,256]{1,0:T(8,128)(2,1)}, u32[]{:S(2)}) copy-start(bf16[1024,256]{1,0:T(8,128)(2,1)} %cot_ref.3) | copy-start | bytes 1572868
  54.6 10.2 %collective-permute-start.9 = (bf16[16,2048]{1,0:T(8,128)(2,1)}, bf16[16,2048]{1,0:T(8,128)(2,1)S(1)}, u32[]{:S(2)}, u32[]{:S(2)}) collective-permute-start(bf16[16,2048]{1,0:T(8,128)(2,1)} %get-tuple-element.46), channel_id=1, source_target_pairs={{16,8},{17,9},{18,10},{19,11},{20,12},{21,13},{22,14},{23,15},{24,... | collective-permute-start | bytes 196616 | tf_op jit(solution)/shard_map/ppermute | solution.py:589
  60.1 7.9 %collective-permute-start.8 = (bf16[16,2048]{1,0:T(8,128)(2,1)}, bf16[16,2048]{1,0:T(8,128)(2,1)S(1)}, u32[]{:S(2)}, u32[]{:S(2)}) collective-permute-start(bf16[16,2048]{1,0:T(8,128)(2,1)} %get-tuple-element.46), channel_id=1, source_target_pairs={{0,8},{1,9},{2,10},{3,11},{4,12},{5,13},{6,14},{7,15},{8,0},{9,1},... | collective-permute-start | bytes 196616 | tf_op jit(solution)/shard_map/ppermute | solution.py:569
  60.2 4.3 %collective-permute-start.7 = (bf16[8,2048]{1,0:T(8,128)(2,1)}, bf16[8,2048]{1,0:T(8,128)(2,1)S(1)}, u32[]{:S(2)}, u32[]{:S(2)}) collective-permute-start(bf16[8,2048]{1,0:T(8,128)(2,1)} %get-tuple-element.45), channel_id=1, source_target_pairs={{0,16},{16,0},{1,17},{17,1},{2,18},{18,2},{3,19},{19,3},{4,20},{20... | collective-permute-start | bytes 98312 | tf_op jit(solution)/shard_map/ppermute | solution.py:572
  60.3 4.5 %collective-permute-start.6 = (bf16[8,2048]{1,0:T(8,128)(2,1)}, bf16[8,2048]{1,0:T(8,128)(2,1)S(1)}, u32[]{:S(2)}, u32[]{:S(2)}) collective-permute-start(bf16[8,2048]{1,0:T(8,128)(2,1)} %get-tuple-element.44), channel_id=1, source_target_pairs={{0,16},{16,0},{1,17},{17,1},{2,18},{18,2},{3,19},{19,3},{4,20},{20... | collective-permute-start | bytes 98312 | tf_op jit(solution)/shard_map/ppermute | solution.py:572
  62.9 5.1 %copy-start.13 = (f32[16,2048]{1,0:T(8,128)S(1)}, f32[16,2048]{1,0:T(8,128)}, u32[]{:S(2)}) copy-start(f32[16,2048]{1,0:T(8,128)} %get-tuple-element.43) | copy-start | bytes 393220
  (3 other events, 6.5 us)

commit v3 on v2

--- a/solution.py
+++ b/solution.py
@@ -470,8 +470,8 @@
 
     def kernel(near_hbm, *refs):
         own_hbm, refs = refs[: len(own)], refs[len(own) :]
-        table_hbm, give_hbm, mine_hbm, upper_hbm, lower_hbm, stage_ref, table_ref, spec_ref, local_ref, cross_ref, joint_ref = refs[:11]
-        held_ref, give_ref, mine_ref, theirs_ref, sems, stage_sems = refs[11:]
+        table_hbm, give_hbm, mine_hbm, theirs_hbm, stage_ref, table_ref, spec_ref, local_ref, cross_ref, joint_ref = refs[:10]
+        held_ref, give_ref, mine_ref, theirs_ref, sems, stage_sems = refs[10:]
         tabled = begin([pltpu.make_async_copy(table_hbm, table_ref, sems.at[0])])
         staged, later = stage_all(near_hbm, own_hbm, slots, stage_ref, stage_sems, half_blocks)
         half, _ = place(half_blocks)
@@ -519,9 +519,8 @@
             theirs_ref[:, columns] = held_ref[1 - group, k].astype(jnp.bfloat16)
         sent += begin(
             [
-                pltpu.make_async_copy(theirs_ref.at[pl.ds(0, kept // 2)], upper_hbm, sems.at[2]),
-                pltpu.make_async_copy(theirs_ref.at[pl.ds(kept // 2, kept // 2)], lower_hbm, sems.at[3]),
-                pltpu.make_async_copy(mine_ref, mine_hbm, sems.at[4]),
+                pltpu.make_async_copy(theirs_ref, theirs_hbm, sems.at[2]),
+                pltpu.make_async_copy(mine_ref, mine_hbm, sems.at[3]),
             ]
         )
         end(sent)
@@ -533,8 +532,7 @@
         [
             jax.ShapeDtypeStruct((kept, lags), jnp.bfloat16),
             jax.ShapeDtypeStruct((kept, lags), jnp.float32),
-            jax.ShapeDtypeStruct((kept // 2, lags), jnp.bfloat16),
-            jax.ShapeDtypeStruct((kept // 2, lags), jnp.bfloat16),
+            jax.ShapeDtypeStruct((kept, lags), jnp.bfloat16),
         ],
         [
             pltpu.VMEM((3, count, rows, size), jnp.bfloat16),
@@ -547,7 +545,7 @@
             pltpu.VMEM((kept, lags), jnp.bfloat16),
             pltpu.VMEM((kept, lags), jnp.float32),
             pltpu.VMEM((kept, lags), jnp.bfloat16),
-            pltpu.SemaphoreType.DMA((5,)),
+            pltpu.SemaphoreType.DMA((4,)),
             pltpu.SemaphoreType.DMA((3, count, merge)),
         ],
     )
@@ -584,14 +582,14 @@
     returned = lax.all_to_all(
         result, "ctx", split_axis=0, concat_axis=0, tiled=True, axis_index_groups=sides
     )
-    give, mine, upper, lower = filter_terms(near, own, 2 * local_filters, half_blocks, table)
-    to_first = [(blocks + i, i ^ half_blocks) for i in range(blocks)]
-    halves = (swap(give), lax.ppermute(give, ("dp", "ctx"), to_first))
-    theirs = jnp.concatenate([other_group(upper), other_group(lower)])
+    give, mine, theirs = filter_terms(near, own, 2 * local_filters, half_blocks, table)
+    halves = tuple(
+        lax.ppermute(give, ("dp", "ctx"), [(g * blocks + i, i ^ half_blocks) for i in range(blocks)]) for g in range(groups)
+    )
+    theirs = other_group(theirs)
     outputs = finish(returned.reshape(half_blocks, 2, repeats, 2, local_filters, tokens), arrays)
     mine, mixed, pre_grad, value_grad, post_grad = lax.optimization_barrier((mine, *outputs))
-    first = jnp.where(lax.axis_index("dp") == 0, 1.0, 0.0)
-    filter_grad = mine + theirs.astype(jnp.float32) + first * (halves[0].astype(jnp.float32) + halves[1].astype(jnp.float32))
+    filter_grad = mine + theirs.astype(jnp.float32) + (halves[0].astype(jnp.float32) + halves[1].astype(jnp.float32))
     return (mixed, pre_grad, value_grad, post_grad, filter_grad)
 
 

time: 69.1 us -> 68.2 us (0.987)
  the two profiles are of different devices: /device:TPU:6 before, /device:TPU:0 now
where the time goes in v3:
time: 68.2 us; the launch traced here: 67.8 us
  starting transfers between devices  25.1 us (37%)
  Pallas kernels  20.4 us (30%)
  waiting for transfers between devices  20 us (29%)
  between operations  0.91 us (1%)
  other arithmetic  0.74 us (1%)
    pallas_call x5, Pallas kernels, call(): pl.pallas_call(kernel, in_specs=[pl.BlockSpec(memory_space=space)] * len(...  18.8 us
    ppermute x4, waiting for transfers between devices, swap(): lax.ppermute(array, 'ctx', [(i, i ^ slot) for i in range(2 * half_blocks)])  17.8 us
    ppermute x2, starting transfers between devices, body(): lax.ppermute(give, ('dp', 'ctx'), [(g * blocks + i, i ^ half_blocks) for...  6.85 us
    ppermute x1, starting transfers between devices, swap(): lax.ppermute(array, 'ctx', [(i, i ^ half_blocks) for i in range(blocks)])  4.1 us
    ppermute x4, starting transfers between devices, swap(): lax.ppermute(array, 'ctx', [(i, i ^ slot) for i in range(2 * half_blocks)])  4.09 us
    all_to_all x1, starting transfers between devices, body(): lax.all_to_all(near.reshape(blocks, rows, tokens), 'ctx', split_axis=0, c...  4.04 us
    all_to_all x1, starting transfers between devices, body(): lax.all_to_all(result, 'ctx', split_axis=0, concat_axis=0, tiled=True, ax...  3.57 us
    ppermute x2, starting transfers between devices, other_group(): return lax.ppermute(array, 'dp', [(0, 1), (1, 0)])  2.46 us
  transfers between devices with their start and end apart: 11, of which 6 were waited for; matrix products, arithmetic and copies ran while one was open for 0% of the time, Pallas kernels for 16%

profile of v3, /device:TPU:0, one launch (start us, length us, event | category | flops | bytes accessed | tf_op | source)
XLA Modules:
  0.0 67.8 jit_solution(11771494128393593212)
XLA Ops:
  0.6 2.8 %gate.1 = (bf16[2,8,4,2,16,256]{5,4,3,2,1,0:T(8,128)(2,1)}, bf16[4,4,2,16,256]{4,3,2,1,0:T(8,128)(2,1)}, bf16[4,4,2,16,256]{4,3,2,1,0:T(8,128)(2,1)}, bf16[16,2048]{1,0:T(8,128)(2,1)}) custom-call(bf16[1024,256]{1,0:T(8,128)(2,1)} %pre_ref.3, bf16[1024,256]{1,0:T(8,128)(2,1)} %value_ref.3, bf16[1024,256]{1,0:T(8,128)(2,1)} %post_ref.3, ...), custom_call_target="tpu_custom_call" | custom-call | flops 1 | bytes 1 | tf_op jit(solution)/shard_map/gate/pallas_call | solution.py:65
  3.5 4.1 %collective-permute-start = (bf16[16,2048]{1,0:T(8,128)(2,1)}, bf16[16,2048]{1,0:T(8,128)(2,1)S(1)}, u32[]{:S(2)}, u32[]{:S(2)}) collective-permute-start(bf16[16,2048]{1,0:T(8,128)(2,1)} %get-tuple-element.28.taps_ref), channel_id=1, source_target_pairs={{0,8},{1,9},{2,10},{3,11},{4,12},{5,13},{6,14},{7,15},{8,0},{9,1},... | collective-permute-start | bytes 196616 | tf_op jit(solution)/shard_map/ppermute | solution.py:567
  7.6 4.0 %all-to-all-start = ((bf16[16,128,256]{2,1,0:T(8,128)(2,1)}), bf16[16,128,256]{2,1,0:T(8,128)(2,1)S(1)}, u32[]{:S(2)}, u32[]{:S(2)}) async-start(bf16[16,128,256]{2,1,0:T(8,128)(2,1)} %bitcast.10), calls=%async_computation | async-start | bytes 2097152 | tf_op jit(solution)/shard_map/all_to_all | solution.py:575
  11.7 0.4 pack_taps.1.here_ref
  12.1 0.5 copy-done.14
  12.6 0.4 collective-permute-start.1
  13.0 1.6 %collective-permute-start.5 = (bf16[2,16,2048]{2,1,0:T(8,128)(2,1)S(1)}, bf16[2,16,2048]{2,1,0:T(8,128)(2,1)S(1)}, u32[]{:S(2)}, u32[]{:S(2)}) collective-permute-start(bf16[2,16,2048]{2,1,0:T(8,128)(2,1)S(1)} %pack_taps.1.here_ref), channel_id=1, source_target_pairs={{0,16},{16,0},{1,17},{17,1},{2,18},{18,2},{3,19},{19,3},{4,20},{20... | collective-permute-start | bytes 393224 | tf_op jit(solution)/shard_map/ppermute | solution.py:570
  14.7 1.7 %collective-permute-start.2 = (bf16[2,128,256]{2,1,0:T(8,128)(2,1)S(1)}, bf16[2,128,256]{2,1,0:T(8,128)(2,1)S(1)}, u32[]{:S(2)}, u32[]{:S(2)}) collective-permute-start(bf16[2,128,256]{2,1,0:T(8,128)(2,1)S(1)} %pad_maximum_fusion), channel_id=1, source_target_pairs={{0,2},{1,3},{2,0},{3,1},{4,6},{5,7},{6,4},{7,5},{8,10},{9,11},{10,... | collective-permute-start | bytes 393224 | tf_op jit(solution)/shard_map/ppermute | solution.py:144
  16.4 1.5 %collective-permute-start.3 = (bf16[2,128,256]{2,1,0:T(8,128)(2,1)S(1)}, bf16[2,128,256]{2,1,0:T(8,128)(2,1)S(1)}, u32[]{:S(2)}, u32[]{:S(2)}) collective-permute-start(bf16[2,128,256]{2,1,0:T(8,128)(2,1)S(1)} %pad_maximum_fusion.1), channel_id=1, source_target_pairs={{0,4},{1,5},{2,6},{3,7},{4,0},{5,1},{6,2},{7,3},{8,12},{9,13},{10,... | collective-permute-start | bytes 393224 | tf_op jit(solution)/shard_map/ppermute | solution.py:144
  18.0 0.4 collective-permute-start.4
  18.6 1.8 %taps.1.refs_5_ = bf16[8,32,1024]{2,1,0:T(8,128)(2,1)S(1)} custom-call(bf16[2,16,2048]{2,1,0:T(8,128)(2,1)S(1)} %pack_taps.1.here_ref, bf16[2,16,2048]{2,1,0:T(8,128)(2,1)S(1)} %collective-permute-done.5.there_ref, bf16[512,1024]{1,0:T(8,128)(2,1)S(1)} %copy-done), custom_call_target="tpu_custom_call" | custom-call | flops 1 | bytes 1 | tf_op jit(solution)/shard_map/taps/pallas_call | solution.py:65
  20.4 4.7 %collective-permute-done.2.refs_2_ = bf16[2,128,256]{2,1,0:T(8,128)(2,1)S(1)} collective-permute-done((bf16[2,128,256]{2,1,0:T(8,128)(2,1)S(1)}, bf16[2,128,256]{2,1,0:T(8,128)(2,1)S(1)}, u32[]{:S(2)}, u32[]{:S(2)}) %collective-permute-start.2) | collective-permute-done | bytes 131104 | tf_op jit(solution)/shard_map/ppermute | solution.py:144
  25.1 7.7 %collective-permute-done.3.refs_3_ = bf16[2,128,256]{2,1,0:T(8,128)(2,1)S(1)} collective-permute-done((bf16[2,128,256]{2,1,0:T(8,128)(2,1)S(1)}, bf16[2,128,256]{2,1,0:T(8,128)(2,1)S(1)}, u32[]{:S(2)}, u32[]{:S(2)}) %collective-permute-start.3) | collective-permute-done | bytes 131104 | tf_op jit(solution)/shard_map/ppermute | solution.py:144
  32.8 5.4 %collective-permute-done.4.refs_4_ = bf16[2,128,256]{2,1,0:T(8,128)(2,1)S(1)} collective-permute-done((bf16[2,128,256]{2,1,0:T(8,128)(2,1)S(1)}, bf16[2,128,256]{2,1,0:T(8,128)(2,1)S(1)}, u32[]{:S(2)}, u32[]{:S(2)}) %collective-permute-start.4) | collective-permute-done | bytes 131104 | tf_op jit(solution)/shard_map/ppermute | solution.py:144
  38.2 6.8 %results.1 = bf16[8,2,128,256]{3,2,1,0:T(8,128)(2,1)} custom-call(bf16[16,128,256]{2,1,0:T(8,128)(2,1)S(1)} %all-to-all-done.near_ref.near_hbm, bf16[1,128,256]{2,1,0:T(8,128)(2,1)S(1)} %bitcast.8, bf16[1,128,256]{2,1,0:T(8,128)(2,1)S(1)} %get-tuple-element.52.refs_1_, bf16[2,128,256]{2,1,0:T(8,128)(2,1)S(1)} %collective-permute-done.2.refs_2_, ...), custom_call_target="tpu_custom_call" | custom-call | flops 137438953472 | bytes 137438953472 | tf_op jit(solution)/shard_map/results/pallas_call | solution.py:65
  45.1 3.6 %all-to-all-start.1 = ((bf16[8,2,128,256]{3,2,1,0:T(8,128)(2,1)}), bf16[8,2,128,256]{3,2,1,0:T(8,128)(2,1)S(1)}, u32[]{:S(2)}, u32[]{:S(2)}) async-start(bf16[8,2,128,256]{3,2,1,0:T(8,128)(2,1)} %results.1), calls=%async_computation.1 | async-start | bytes 2097152 | tf_op jit(solution)/shard_map/all_to_all | solution.py:582
  48.7 7.0 %filter_terms.1 = (bf16[16,2048]{1,0:T(8,128)(2,1)}, f32[16,2048]{1,0:T(8,128)}, bf16[16,2048]{1,0:T(8,128)(2,1)}) custom-call(bf16[16,128,256]{2,1,0:T(8,128)(2,1)} %copy-done.1, bf16[1,128,256]{2,1,0:T(8,128)(2,1)} %bitcast.9, bf16[1,128,256]{2,1,0:T(8,128)(2,1)} %copy-done.7, bf16[2,128,256]{2,1,0:T(8,128)(2,1)} %copy-done.8, ...), custom_call_target="tpu_custom_call" | custom-call | flops 1 | bytes 1 | tf_op jit(solution)/shard_map/filter_terms/pallas_call | solution.py:65
  55.7 1.3 %collective-permute-start.8 = (bf16[16,2048]{1,0:T(8,128)(2,1)}, bf16[16,2048]{1,0:T(8,128)(2,1)S(1)}, u32[]{:S(2)}, u32[]{:S(2)}) collective-permute-start(bf16[16,2048]{1,0:T(8,128)(2,1)} %get-tuple-element.44), channel_id=1, source_target_pairs={{16,8},{17,9},{18,10},{19,11},{20,12},{21,13},{22,14},{23,15},{24,... | collective-permute-start | bytes 196616 | tf_op jit(solution)/shard_map/ppermute | solution.py:587
  57.0 5.6 %collective-permute-start.7 = (bf16[16,2048]{1,0:T(8,128)(2,1)}, bf16[16,2048]{1,0:T(8,128)(2,1)S(1)}, u32[]{:S(2)}, u32[]{:S(2)}) collective-permute-start(bf16[16,2048]{1,0:T(8,128)(2,1)} %get-tuple-element.44), channel_id=1, source_target_pairs={{0,8},{1,9},{2,10},{3,11},{4,12},{5,13},{6,14},{7,15},{8,0},{9,1},... | collective-permute-start | bytes 196616 | tf_op jit(solution)/shard_map/ppermute | solution.py:587
  62.6 0.9 %collective-permute-start.6 = (bf16[16,2048]{1,0:T(8,128)(2,1)}, bf16[16,2048]{1,0:T(8,128)(2,1)S(1)}, u32[]{:S(2)}, u32[]{:S(2)}) collective-permute-start(bf16[16,2048]{1,0:T(8,128)(2,1)} %get-tuple-element.43), channel_id=1, source_target_pairs={{0,16},{16,0},{1,17},{17,1},{2,18},{18,2},{3,19},{19,3},{4,20},{20... | collective-permute-start | bytes 196616 | tf_op jit(solution)/shard_map/ppermute | solution.py:570
  63.5 1.6 %finish.1 = (bf16[1024,256]{1,0:T(8,128)(2,1)}, bf16[1024,256]{1,0:T(8,128)(2,1)}, bf16[1024,256]{1,0:T(8,128)(2,1)}, bf16[1024,256]{1,0:T(8,128)(2,1)}) custom-call(bf16[8,2,4,2,16,256]{5,4,3,2,1,0:T(8,128)(2,1)S(1)} %bitcast.7, bf16[1024,256]{1,0:T(8,128)(2,1)S(1)} %copy-done.2, bf16[1024,256]{1,0:T(8,128)(2,1)S(1)} %copy-done.3, ...), custom_call_target="tpu_custom_call" | custom-call | tf_op jit(solution)/shard_map/finish/pallas_call | solution.py:177
  65.1 0.2 collective-permute-done.7
  65.4 1.7 %collective-permute-done.6 = bf16[16,2048]{1,0:T(8,128)(2,1)S(1)} collective-permute-done((bf16[16,2048]{1,0:T(8,128)(2,1)}, bf16[16,2048]{1,0:T(8,128)(2,1)S(1)}, u32[]{:S(2)}, u32[]{:S(2)}) %collective-permute-start.6) | collective-permute-done | bytes 65568 | tf_op jit(solution)/shard_map/ppermute | solution.py:570
  67.1 0.7 %add_add_fusion = f32[16,2048]{1,0:T(8,128)} fusion(bf16[16,2048]{1,0:T(8,128)(2,1)S(1)} %collective-permute-done.8, bf16[16,2048]{1,0:T(8,128)(2,1)S(1)} %collective-permute-done.7, f32[16,2048]{1,0:T(8,128)S(1)} %copy-done.13, bf16[16,2048]{1,0:T(8,128)(2,1)S(1)} %collective-permute-done.6), kind=kLoop, calls=%fused_computation.3 | loop fusion | flops 196608 | bytes 458752 | tf_op jit(solution)/shard_map/add | solution.py:592
  (40 shorter events, 0.4 us)
Async XLA Ops:
  3.5 8.2 %collective-permute-start = (bf16[16,2048]{1,0:T(8,128)(2,1)}, bf16[16,2048]{1,0:T(8,128)(2,1)S(1)}, u32[]{:S(2)}, u32[]{:S(2)}) collective-permute-start(bf16[16,2048]{1,0:T(8,128)(2,1)} %get-tuple-element.28.taps_ref), channel_id=1, source_target_pairs={{0,8},{1,9},{2,10},{3,11},{4,12},{5,13},{6,14},{7,15},{8,0},{9,1},... | collective-permute-start | bytes 196616 | tf_op jit(solution)/shard_map/ppermute | solution.py:567
  7.6 4.1 %copy-start.11 = (bf16[16,2048]{1,0:T(8,128)(2,1)S(1)}, bf16[16,2048]{1,0:T(8,128)(2,1)}, u32[]{:S(2)}) copy-start(bf16[16,2048]{1,0:T(8,128)(2,1)} %get-tuple-element.28.taps_ref) | copy-start | bytes 196612
  7.6 30.6 %all-to-all-start = ((bf16[16,128,256]{2,1,0:T(8,128)(2,1)}), bf16[16,128,256]{2,1,0:T(8,128)(2,1)S(1)}, u32[]{:S(2)}, u32[]{:S(2)}) async-start(bf16[16,128,256]{2,1,0:T(8,128)(2,1)} %bitcast.10), calls=%async_computation | async-start | bytes 2097152 | tf_op jit(solution)/shard_map/all_to_all | solution.py:575
  12.1 6.5 %copy-start = (bf16[512,1024]{1,0:T(8,128)(2,1)S(1)}, bf16[512,1024]{1,0:T(8,128)(2,1)}, u32[]{:S(2)}) copy-start(bf16[512,1024]{1,0:T(8,128)(2,1)} %constant.2.clone.table_hbm.refs_6_.refs_5_) | copy-start | bytes 3145732
  12.6 2.0 %collective-permute-start.1 = (bf16[4,128,256]{2,1,0:T(8,128)(2,1)S(1)}, bf16[4,128,256]{2,1,0:T(8,128)(2,1)S(1)}, u32[]{:S(2)}, u32[]{:S(2)}) collective-permute-start(bf16[4,128,256]{2,1,0:T(8,128)(2,1)S(1)} %bitcast.14), channel_id=1, source_target_pairs={{0,1},{1,0},{2,3},{3,2},{4,5},{5,4},{6,7},{7,6},{8,9},{9,8},{10,11... | collective-permute-start | bytes 786440 | tf_op jit(solution)/shard_map/ppermute | solution.py:144
  13.0 25.1 %copy-start.6 = (bf16[1,4,2,16,256]{4,3,2,1,0:T(8,128)(2,1)}, bf16[1,4,2,16,256]{4,3,2,1,0:T(8,128)(2,1)S(1)}, u32[]{:S(2)}) copy-start(bf16[1,4,2,16,256]{4,3,2,1,0:T(8,128)(2,1)S(1)} %get-tuple-element.48) | copy-start | bytes 196612
  13.0 5.6 %collective-permute-start.5 = (bf16[2,16,2048]{2,1,0:T(8,128)(2,1)S(1)}, bf16[2,16,2048]{2,1,0:T(8,128)(2,1)S(1)}, u32[]{:S(2)}, u32[]{:S(2)}) collective-permute-start(bf16[2,16,2048]{2,1,0:T(8,128)(2,1)S(1)} %pack_taps.1.here_ref), channel_id=1, source_target_pairs={{0,16},{16,0},{1,17},{17,1},{2,18},{18,2},{3,19},{19,3},{4,20},{20... | collective-permute-start | bytes 393224 | tf_op jit(solution)/shard_map/ppermute | solution.py:570
  14.6 23.6 %copy-start.7 = (bf16[1,128,256]{2,1,0:T(8,128)(2,1)}, bf16[1,128,256]{2,1,0:T(8,128)(2,1)S(1)}, u32[]{:S(2)}) copy-start(bf16[1,128,256]{2,1,0:T(8,128)(2,1)S(1)} %get-tuple-element.52.refs_1_) | copy-start | bytes 196612
  14.7 10.4 %collective-permute-start.2 = (bf16[2,128,256]{2,1,0:T(8,128)(2,1)S(1)}, bf16[2,128,256]{2,1,0:T(8,128)(2,1)S(1)}, u32[]{:S(2)}, u32[]{:S(2)}) collective-permute-start(bf16[2,128,256]{2,1,0:T(8,128)(2,1)S(1)} %pad_maximum_fusion), channel_id=1, source_target_pairs={{0,2},{1,3},{2,0},{3,1},{4,6},{5,7},{6,4},{7,5},{8,10},{9,11},{10,... | collective-permute-start | bytes 393224 | tf_op jit(solution)/shard_map/ppermute | solution.py:144
  16.4 16.4 %collective-permute-start.3 = (bf16[2,128,256]{2,1,0:T(8,128)(2,1)S(1)}, bf16[2,128,256]{2,1,0:T(8,128)(2,1)S(1)}, u32[]{:S(2)}, u32[]{:S(2)}) collective-permute-start(bf16[2,128,256]{2,1,0:T(8,128)(2,1)S(1)} %pad_maximum_fusion.1), channel_id=1, source_target_pairs={{0,4},{1,5},{2,6},{3,7},{4,0},{5,1},{6,2},{7,3},{8,12},{9,13},{10,... | collective-permute-start | bytes 393224 | tf_op jit(solution)/shard_map/ppermute | solution.py:144
  18.0 20.2 %collective-permute-start.4 = (bf16[2,128,256]{2,1,0:T(8,128)(2,1)S(1)}, bf16[2,128,256]{2,1,0:T(8,128)(2,1)S(1)}, u32[]{:S(2)}, u32[]{:S(2)}) collective-permute-start(bf16[2,128,256]{2,1,0:T(8,128)(2,1)S(1)} %pad_maximum_fusion.2), channel_id=1, source_target_pairs={{0,6},{1,7},{2,4},{3,5},{4,2},{5,3},{6,0},{7,1},{8,14},{9,15},{10,... | collective-permute-start | bytes 393224 | tf_op jit(solution)/shard_map/ppermute | solution.py:144
  25.1 20.0 %copy-start.8 = (bf16[2,128,256]{2,1,0:T(8,128)(2,1)}, bf16[2,128,256]{2,1,0:T(8,128)(2,1)S(1)}, u32[]{:S(2)}) copy-start(bf16[2,128,256]{2,1,0:T(8,128)(2,1)S(1)} %collective-permute-done.2.refs_2_) | copy-start | bytes 393220
  32.8 12.3 %copy-start.9 = (bf16[2,128,256]{2,1,0:T(8,128)(2,1)}, bf16[2,128,256]{2,1,0:T(8,128)(2,1)S(1)}, u32[]{:S(2)}) copy-start(bf16[2,128,256]{2,1,0:T(8,128)(2,1)S(1)} %collective-permute-done.3.refs_3_) | copy-start | bytes 393220
  38.2 6.9 %copy-start.10 = (bf16[2,128,256]{2,1,0:T(8,128)(2,1)}, bf16[2,128,256]{2,1,0:T(8,128)(2,1)S(1)}, u32[]{:S(2)}) copy-start(bf16[2,128,256]{2,1,0:T(8,128)(2,1)S(1)} %collective-permute-done.4.refs_4_) | copy-start | bytes 393220
  38.2 6.9 %copy-start.1 = (bf16[16,128,256]{2,1,0:T(8,128)(2,1)}, bf16[16,128,256]{2,1,0:T(8,128)(2,1)S(1)}, u32[]{:S(2)}) copy-start(bf16[16,128,256]{2,1,0:T(8,128)(2,1)S(1)} %all-to-all-done.near_ref.near_hbm) | copy-start | bytes 3145732
  45.1 18.4 %all-to-all-start.1 = ((bf16[8,2,128,256]{3,2,1,0:T(8,128)(2,1)}), bf16[8,2,128,256]{3,2,1,0:T(8,128)(2,1)S(1)}, u32[]{:S(2)}, u32[]{:S(2)}) async-start(bf16[8,2,128,256]{3,2,1,0:T(8,128)(2,1)} %results.1), calls=%async_computation.1 | async-start | bytes 2097152 | tf_op jit(solution)/shard_map/all_to_all | solution.py:582
  48.6 14.8 %copy-start.2 = (bf16[1024,256]{1,0:T(8,128)(2,1)S(1)}, bf16[1024,256]{1,0:T(8,128)(2,1)}, u32[]{:S(2)}) copy-start(bf16[1024,256]{1,0:T(8,128)(2,1)} %pre_ref.3) | copy-start | bytes 1572868
  48.7 14.8 %copy-start.3 = (bf16[1024,256]{1,0:T(8,128)(2,1)S(1)}, bf16[1024,256]{1,0:T(8,128)(2,1)}, u32[]{:S(2)}) copy-start(bf16[1024,256]{1,0:T(8,128)(2,1)} %value_ref.3) | copy-start | bytes 1572868
  48.7 14.8 %copy-start.4 = (bf16[1024,256]{1,0:T(8,128)(2,1)S(1)}, bf16[1024,256]{1,0:T(8,128)(2,1)}, u32[]{:S(2)}) copy-start(bf16[1024,256]{1,0:T(8,128)(2,1)} %post_ref.3) | copy-start | bytes 1572868
  48.7 14.8 %copy-start.5 = (bf16[1024,256]{1,0:T(8,128)(2,1)S(1)}, bf16[1024,256]{1,0:T(8,128)(2,1)}, u32[]{:S(2)}) copy-start(bf16[1024,256]{1,0:T(8,128)(2,1)} %cot_ref.3) | copy-start | bytes 1572868
  55.7 9.4 %collective-permute-start.8 = (bf16[16,2048]{1,0:T(8,128)(2,1)}, bf16[16,2048]{1,0:T(8,128)(2,1)S(1)}, u32[]{:S(2)}, u32[]{:S(2)}) collective-permute-start(bf16[16,2048]{1,0:T(8,128)(2,1)} %get-tuple-element.44), channel_id=1, source_target_pairs={{16,8},{17,9},{18,10},{19,11},{20,12},{21,13},{22,14},{23,15},{24,... | collective-permute-start | bytes 196616 | tf_op jit(solution)/shard_map/ppermute | solution.py:587
  57.0 8.4 %collective-permute-start.7 = (bf16[16,2048]{1,0:T(8,128)(2,1)}, bf16[16,2048]{1,0:T(8,128)(2,1)S(1)}, u32[]{:S(2)}, u32[]{:S(2)}) collective-permute-start(bf16[16,2048]{1,0:T(8,128)(2,1)} %get-tuple-element.44), channel_id=1, source_target_pairs={{0,8},{1,9},{2,10},{3,11},{4,12},{5,13},{6,14},{7,15},{8,0},{9,1},... | collective-permute-start | bytes 196616 | tf_op jit(solution)/shard_map/ppermute | solution.py:587
  62.6 4.5 %collective-permute-start.6 = (bf16[16,2048]{1,0:T(8,128)(2,1)}, bf16[16,2048]{1,0:T(8,128)(2,1)S(1)}, u32[]{:S(2)}, u32[]{:S(2)}) collective-permute-start(bf16[16,2048]{1,0:T(8,128)(2,1)} %get-tuple-element.43), channel_id=1, source_target_pairs={{0,16},{16,0},{1,17},{17,1},{2,18},{18,2},{3,19},{19,3},{4,20},{20... | collective-permute-start | bytes 196616 | tf_op jit(solution)/shard_map/ppermute | solution.py:570
  63.5 3.6 %copy-start.13 = (f32[16,2048]{1,0:T(8,128)S(1)}, f32[16,2048]{1,0:T(8,128)}, u32[]{:S(2)}) copy-start(f32[16,2048]{1,0:T(8,128)} %get-tuple-element.42) | copy-start | bytes 393220
  (2 other events, 2.3 us)

commit v4 on v3

--- a/solution.py
+++ b/solution.py
@@ -74,68 +74,79 @@
     )(*operands)
 
 
-def gate(arrays, filters, repeats, half_blocks):
+def gate(near, arrays, filters, repeats, half_blocks):
     rows_all, tokens = arrays[0].shape
     rows = rows_all // repeats
     share = rows // (2 * half_blocks)
     piece = (repeats, 2, share, tokens)
 
-    def kernel(pre_ref, value_ref, post_ref, cot_ref, filt_ref, out_ref, even_ref, odd_ref, taps_ref, in_ref, result_ref, filt_in, taps_out, in_sems, out_sems, own_sems, taps_sems):
+    def kernel(pre_ref, value_ref, post_ref, cot_ref, *refs):
+        if near:
+            filt_ref, out_ref, taps_ref, left_ref, right_ref, result_ref, in_sems, out_sems, filt_in, taps_out, taps_sems = refs
+            loaded = begin([pltpu.make_async_copy(filt_ref, filt_in, taps_sems.at[0])])
+        else:
+            even_ref, odd_ref, left_ref, right_ref, result_ref, in_sems, out_sems = refs
         half, me = place(half_blocks)
-        sources = (pre_ref, value_ref, cot_ref, post_ref)
-
-        def fetch(r):
+        use_gated = half == 0 if near else half != 0
+
+        def fetch(r, left, right):
             at = pl.ds(r * rows, rows)
-            return [
-                pltpu.make_async_copy(ref.at[at], in_ref.at[which, r], in_sems.at[which, r])
-                for which, ref in enumerate(sources)
-            ]
-
-        for r in range(repeats):
-            begin(fetch(r))
-        loaded = begin([pltpu.make_async_copy(filt_ref, filt_in, taps_sems.at[0])])
+            return (
+                pltpu.make_async_copy(left.at[at], left_ref.at[r], in_sems.at[0, r]),
+                pltpu.make_async_copy(right.at[at], right_ref.at[r], in_sems.at[1, r]),
+            )
+
+        @pl.when(use_gated)
+        def _():
+            for r in range(repeats):
+                begin(fetch(r, pre_ref, value_ref))
+
+        @pl.when(jnp.logical_not(use_gated))
+        def _():
+            for r in range(repeats):
+                begin(fetch(r, cot_ref, post_ref))
+
         sent = []
         for r in range(repeats):
-            end(fetch(r))
-            for which in range(2):
-                product = in_ref[2 * which, r].astype(jnp.float32) * in_ref[2 * which + 1, r].astype(jnp.float32)
-                product = product.astype(jnp.bfloat16).reshape(2, half_blocks, share, tokens)
-                at = half if which == 0 else 1 - half
-                for side in range(2):
-                    result_ref[at, :, r, side] = product[side]
-            for to in range(2):
-                copy = pltpu.make_async_copy(result_ref.at[0, :, r], out_ref.at[to, :, r], out_sems.at[to, r])
-                sent += begin([copy])
-        for at in range(half_blocks // 2):
-            for odd, target in enumerate((even_ref, odd_ref)):
-                source = result_ref.at[1, jnp.bitwise_xor(me, 2 * at + odd)]
-                sent += begin([pltpu.make_async_copy(source, target.at[at], own_sems.at[odd, at])])
-        end(loaded)
-        taps_out[...] = filt_in[...].astype(jnp.bfloat16)
-        sent += begin([pltpu.make_async_copy(taps_out, taps_ref, taps_sems.at[1])])
+            end(fetch(r, pre_ref, value_ref))
+            product = left_ref[r].astype(jnp.float32) * right_ref[r].astype(jnp.float32)
+            product = product.astype(jnp.bfloat16).reshape(2, half_blocks, share, tokens)
+            for side in range(2):
+                result_ref[:, r, side] = product[side]
+            for to in range(2 if near else 0):
+                sent += begin([pltpu.make_async_copy(result_ref.at[:, r], out_ref.at[to, :, r], out_sems.at[to, r])])
+        if near:
+            end(loaded)
+            taps_out[...] = filt_in[...].astype(jnp.bfloat16)
+            sent += begin([pltpu.make_async_copy(taps_out, taps_ref, taps_sems.at[1])])
+        else:
+            for at in range(half_blocks // 2):
+                for odd, target in enumerate((even_ref, odd_ref)):
+                    source = result_ref.at[jnp.bitwise_xor(me, 2 * at + odd)]
+                    sent += begin([pltpu.make_async_copy(source, target.at[at], out_sems.at[odd, at])])
         end(sent)
 
     own_shape = jax.ShapeDtypeStruct((half_blocks // 2, *piece), jnp.bfloat16)
+    near_shape = jax.ShapeDtypeStruct((2, half_blocks, *piece), jnp.bfloat16)
+    scratch = [
+        pltpu.VMEM((repeats, rows, tokens), jnp.bfloat16),
+        pltpu.VMEM((repeats, rows, tokens), jnp.bfloat16),
+        pltpu.VMEM((half_blocks, *piece), jnp.bfloat16),
+        pltpu.SemaphoreType.DMA((2, repeats)),
+        pltpu.SemaphoreType.DMA((2, repeats if near else half_blocks // 2)),
+    ]
+    if near:
+        scratch += [
+            pltpu.VMEM(filters.shape, filters.dtype),
+            pltpu.VMEM(filters.shape, jnp.bfloat16),
+            pltpu.SemaphoreType.DMA((2,)),
+        ]
     return call(
         kernel,
-        "gate",
-        (*arrays, filters),
-        [
-            jax.ShapeDtypeStruct((2, half_blocks, *piece), jnp.bfloat16),
-            own_shape,
-            own_shape,
-            jax.ShapeDtypeStruct(filters.shape, jnp.bfloat16),
-        ],
-        [
-            pltpu.VMEM((4, repeats, rows, tokens), jnp.bfloat16),
-            pltpu.VMEM((2, half_blocks, *piece), jnp.bfloat16),
-            pltpu.VMEM(filters.shape, filters.dtype),
-            pltpu.VMEM(filters.shape, jnp.bfloat16),
-            pltpu.SemaphoreType.DMA((4, repeats)),
-            pltpu.SemaphoreType.DMA((2, repeats)),
-            pltpu.SemaphoreType.DMA((2, half_blocks // 2)),
-            pltpu.SemaphoreType.DMA((2,)),
-        ],
+        "gate_near" if near else "gate_own",
+        (*arrays, filters) if near else arrays,
+        [near_shape, jax.ShapeDtypeStruct(filters.shape, jnp.bfloat16)] if near else [own_shape, own_shape],
+        scratch,
     )
 
 
@@ -286,36 +297,23 @@
         spec_ref[..., columns] = dot(staged, table_ref[:, columns]).reshape(spec_ref.shape[:-1] + (2 * LANES,))
 
 
-def stage_copies(source, base, stage_ref, sems, outer, half_blocks):
-    count, _, size = stage_ref.shape
-    tokens = source.shape[2]
-    merge = size // tokens
-    half, _ = place(half_blocks)
-    copies = []
-    for k in range(count):
-        block = order(k, count, half, outer)
-        for q in range(merge):
-            target = stage_ref.at[k, :, pl.ds(q * tokens, tokens)]
-            copies.append(pltpu.make_async_copy(source.at[base + block * merge + q], target, sems.at[k, q]))
-    return copies
-
-
-def stage_all(near_hbm, own_refs, slots, stage_ref, sems, half_blocks):
+def stage_all(near_ref, own_refs, slots, stage_ref, half_blocks):
     _, count, _, size = stage_ref.shape
-    tokens = near_hbm.shape[2]
+    tokens = near_ref.shape[2]
     merge = size // tokens
     half, me = place(half_blocks)
-    near = stage_copies(near_hbm, half * half_blocks, stage_ref.at[0], sems.at[0], True, half_blocks)
-    far = stage_copies(near_hbm, (1 - half) * half_blocks, stage_ref.at[1], sems.at[1], False, half_blocks)
-    own = []
+    for k in range(count):
+        outer, inner = order(k, count, half, True), order(k, count, half, False)
+        for q in range(merge):
+            lanes = pl.ds(q * tokens, tokens)
+            stage_ref[0, k, :, lanes] = near_ref[half * half_blocks + outer * merge + q]
+            stage_ref[1, k, :, lanes] = near_ref[(1 - half) * half_blocks + inner * merge + q]
     for group, ref in zip(slots, own_refs):
         for at, slot in enumerate(group):
             position = jnp.bitwise_xor(me, slot)
             k = order(position // merge, count, half, False)
             start = pl.multiple_of(lax.rem(position, merge) * tokens, tokens)
-            target = stage_ref.at[2, k, :, pl.ds(start, tokens)]
-            own.append(pltpu.make_async_copy(ref.at[at], target, sems.at[2, slot // merge, slot % merge]))
-    return begin(near) + begin(far), begin(own)
+            stage_ref[2, k, :, pl.ds(start, tokens)] = ref[at]
 
 
 def order(k, count, half, outer):
@@ -364,21 +362,10 @@
     def kernel(near_ref, *refs):
         own_refs, (filt_in, table_ref, out_hbm) = refs[: len(own)], refs[len(own) : len(own) + 3]
         stage_ref, filt_ref, spec_ref, prod_ref, held_ref, out_sems = refs[len(own) + 3 :]
-        half, me = place(half_blocks)
-        for k in range(count):
-            for q in range(merge):
-                lanes = pl.ds(q * tokens, tokens)
-                outer, inner = order(k, count, half, True), order(k, count, half, False)
-                stage_ref[0, k, :, lanes] = near_ref[half * half_blocks + outer * merge + q]
-                stage_ref[1, k, :, lanes] = near_ref[(1 - half) * half_blocks + inner * merge + q]
-        for group, ref in zip(slots, own_refs):
-            for at, slot in enumerate(group):
-                position = jnp.bitwise_xor(me, slot)
-                k = order(position // merge, count, half, False)
-                start = pl.multiple_of(lax.rem(position, merge) * tokens, tokens)
-                stage_ref[2, k, :, pl.ds(start, tokens)] = ref[at]
+        stage_all(near_ref, own_refs, slots, stage_ref, half_blocks)
         filt_ref[...] = filt_in[...].astype(jnp.float32)
         transform(stage_ref, table_ref, spec_ref)
+        half, _ = place(half_blocks)
 
         def tile(first):
             row = pl.ds(first, SUBLANES)
@@ -468,24 +455,20 @@
     kept, lags = filters // 2, count * size
     repeats = rows // filters
 
-    def kernel(near_hbm, *refs):
-        own_hbm, refs = refs[: len(own)], refs[len(own) :]
-        table_hbm, give_hbm, mine_hbm, theirs_hbm, stage_ref, table_ref, spec_ref, local_ref, cross_ref, joint_ref = refs[:10]
-        held_ref, give_ref, mine_ref, theirs_ref, sems, stage_sems = refs[10:]
-        tabled = begin([pltpu.make_async_copy(table_hbm, table_ref, sems.at[0])])
-        staged, later = stage_all(near_hbm, own_hbm, slots, stage_ref, stage_sems, half_blocks)
+    def kernel(near_ref, *refs):
+        own_refs, refs = refs[: len(own)], refs[len(own) :]
+        table_ref, give_hbm, mine_hbm, theirs_hbm, stage_ref, spec_ref, local_ref, cross_ref, joint_ref = refs[:9]
+        held_ref, give_ref, mine_ref, theirs_ref, sems = refs[9:]
         half, _ = place(half_blocks)
         group = lax.axis_index("dp")
         turn = jnp.where(half == 0, 1.0, -1.0).astype(jnp.float32)
-        end(tabled)
-        end(staged)
-        end(later)
+        stage_all(near_ref, own_refs, slots, stage_ref, half_blocks)
         transform(stage_ref, table_ref, spec_ref)
-        near_ref, far_ref, own_ref = (spec_ref.at[which] for which in range(3))
+        near_spec, far_spec, own_spec = (spec_ref.at[which] for which in range(3))
 
         def local_tile(first):
             for strip in range(size // LANES):
-                sums = lag_products(near_ref, own_ref, first, strip, repeats, filters, [count - 1 - k for k in range(count)])
+                sums = lag_products(near_spec, own_spec, first, strip, repeats, filters, [count - 1 - k for k in range(count)])
                 for k, (real, imag) in enumerate(sums):
                     keep(local_ref, k, pl.ds(first, SUBLANES), strip, (real, turn * imag))
 
@@ -503,7 +486,7 @@
             at = pl.ds(pl.multiple_of(mine + first, SUBLANES), SUBLANES)
             for strip in range(size // LANES):
                 totals = [2 * count - 1 - k for k in range(1, 2 * count)]
-                sums = lag_products(near_ref, far_ref, mine + first, strip, repeats, filters, totals)
+                sums = lag_products(near_spec, far_spec, mine + first, strip, repeats, filters, totals)
                 keep(cross_ref, 0, row, strip, parts(local_ref, 0, at, strip))
                 for k, (real, imag) in enumerate(sums, 1):
                     value = (real, turn * imag)
@@ -536,7 +519,6 @@
         ],
         [
             pltpu.VMEM((3, count, rows, size), jnp.bfloat16),
-            pltpu.VMEM(table.shape, jnp.bfloat16),
             pltpu.VMEM((3, count, rows, width), jnp.float32),
             pltpu.VMEM((count, filters, width), jnp.float32),
             pltpu.VMEM((2 * count, kept, width), jnp.float32),
@@ -546,8 +528,9 @@
             pltpu.VMEM((kept, lags), jnp.float32),
             pltpu.VMEM((kept, lags), jnp.bfloat16),
             pltpu.SemaphoreType.DMA((4,)),
-            pltpu.SemaphoreType.DMA((3, count, merge)),
         ],
+        vmem=VMEM_BYTES - (5 << 20),
+        space=pltpu.VMEM,
     )
 
 
@@ -569,7 +552,8 @@
     def other_group(array):
         return lax.ppermute(array, "dp", [(0, 1), (1, 0)])
 
-    near, even, odd, taps = gate(arrays, filters, repeats, half_blocks)
+    near, taps = gate(True, arrays, filters, repeats, half_blocks)
+    even, odd = gate(False, arrays, filters, repeats, half_blocks)
     here = pack_taps(taps, swap(taps), half_blocks)
     odd, here = lax.optimization_barrier((odd, here))
     near = lax.all_to_all(near.reshape(blocks, rows, tokens), "ctx", split_axis=0, concat_axis=0, tiled=True)
@@ -589,7 +573,7 @@
     theirs = other_group(theirs)
     outputs = finish(returned.reshape(half_blocks, 2, repeats, 2, local_filters, tokens), arrays)
     mine, mixed, pre_grad, value_grad, post_grad = lax.optimization_barrier((mine, *outputs))
-    filter_grad = mine + theirs.astype(jnp.float32) + (halves[0].astype(jnp.float32) + halves[1].astype(jnp.float32))
+    filter_grad = mine + (halves[1].astype(jnp.float32) + halves[0].astype(jnp.float32)) + theirs.astype(jnp.float32)
     return (mixed, pre_grad, value_grad, post_grad, filter_grad)
 
 

time: 68.2 us -> 66.1 us (0.969)
  waiting for transfers between devices: 20 us -> 16.8 us
  Pallas kernels: 20.4 us -> 21.8 us
    ppermute x4, waiting for transfers between devices: 17.8 us -> 14.6 us  [swap(): lax.ppermute(array, 'ctx', [(i, i ^ slot) for i in range(2 * half_blocks)])]
    pallas_call x5 -> x6, Pallas kernels: 18.8 us -> 20.2 us  [call(): pl.pallas_call(kernel, in_specs=[pl.BlockSpec(memory_space=space)] * len(...]
  transfers between devices with their start and end apart: 11 -> 11, of which waited for: 6 -> 5; matrix products, arithmetic and copies ran while one was open for 0% -> 0% of each run, Pallas kernels for 16% -> 19%
where the time goes in v4:
time: 66.1 us; the launch traced here: 65.8 us
  starting transfers between devices  24.9 us (38%)
  Pallas kernels  21.8 us (33%)
  waiting for transfers between devices  16.8 us (25%)
  between operations  0.94 us (1%)
  other arithmetic  0.73 us (1%)
    pallas_call x6, Pallas kernels, call(): pl.pallas_call(kernel, in_specs=[pl.BlockSpec(memory_space=space)] * len(...  20.2 us
    ppermute x4, waiting for transfers between devices, swap(): lax.ppermute(array, 'ctx', [(i, i ^ slot) for i in range(2 * half_blocks)])  14.6 us
    ppermute x2, starting transfers between devices, body(): lax.ppermute(give, ('dp', 'ctx'), [(g * blocks + i, i ^ half_blocks) for...  6.69 us
    ppermute x1, starting transfers between devices, swap(): lax.ppermute(array, 'ctx', [(i, i ^ half_blocks) for i in range(blocks)])  4.12 us
    ppermute x4, starting transfers between devices, swap(): lax.ppermute(array, 'ctx', [(i, i ^ slot) for i in range(2 * half_blocks)])  4.11 us
    all_to_all x1, starting transfers between devices, body(): lax.all_to_all(near.reshape(blocks, rows, tokens), 'ctx', split_axis=0, c...  3.91 us
    all_to_all x1, starting transfers between devices, body(): lax.all_to_all(result, 'ctx', split_axis=0, concat_axis=0, tiled=True, ax...  3.57 us
    ppermute x2, starting transfers between devices, other_group(): return lax.ppermute(array, 'dp', [(0, 1), (1, 0)])  2.46 us
  transfers between devices with their start and end apart: 11, of which 5 were waited for; matrix products, arithmetic and copies ran while one was open for 0% of the time, Pallas kernels for 19%

profile of v4, /device:TPU:0, one launch (start us, length us, event | category | flops | bytes accessed | tf_op | source)
XLA Modules:
  0.0 65.8 jit_solution(12494648815480532487)
XLA Ops:
  0.6 2.2 %gate_near.1 = (bf16[2,8,4,2,16,256]{5,4,3,2,1,0:T(8,128)(2,1)}, bf16[16,2048]{1,0:T(8,128)(2,1)}) custom-call(bf16[1024,256]{1,0:T(8,128)(2,1)} %pre_ref.5, bf16[1024,256]{1,0:T(8,128)(2,1)} %value_ref.5, bf16[1024,256]{1,0:T(8,128)(2,1)} %post_ref.5, bf16[1024,256]{1,0:T(8,128)(2,1)} %cot_ref.5, f32[16,2048]{1,0:T(8,128)} %refs_0_.1), custom_call_target="tpu_custom_call" | custom-call | flops 1 | bytes 1 | tf_op jit(solution)/shard_map/gate_near/pallas_call | solution.py:65
  2.9 4.1 %collective-permute-start = (bf16[16,2048]{1,0:T(8,128)(2,1)}, bf16[16,2048]{1,0:T(8,128)(2,1)S(1)}, u32[]{:S(2)}, u32[]{:S(2)}) collective-permute-start(bf16[16,2048]{1,0:T(8,128)(2,1)} %get-tuple-element.28.taps_ref), channel_id=1, source_target_pairs={{0,8},{1,9},{2,10},{3,11},{4,12},{5,13},{6,14},{7,15},{8,0},{9,1},... | collective-permute-start | bytes 196616 | tf_op jit(solution)/shard_map/ppermute | solution.py:550
  7.0 3.9 %all-to-all-start = ((bf16[16,128,256]{2,1,0:T(8,128)(2,1)}), bf16[16,128,256]{2,1,0:T(8,128)(2,1)S(1)}, u32[]{:S(2)}, u32[]{:S(2)}) async-start(bf16[16,128,256]{2,1,0:T(8,128)(2,1)} %bitcast.10), calls=%async_computation | async-start | bytes 2097152 | tf_op jit(solution)/shard_map/all_to_all | solution.py:559
  10.9 2.3 %gate_own.1 = (bf16[4,4,2,16,256]{4,3,2,1,0:T(8,128)(2,1)}, bf16[4,4,2,16,256]{4,3,2,1,0:T(8,128)(2,1)}) custom-call(bf16[1024,256]{1,0:T(8,128)(2,1)} %pre_ref.5, bf16[1024,256]{1,0:T(8,128)(2,1)} %value_ref.5, bf16[1024,256]{1,0:T(8,128)(2,1)} %post_ref.5, bf16[1024,256]{1,0:T(8,128)(2,1)} %cot_ref.5), custom_call_target="tpu_custom_call" | custom-call | flops 1 | bytes 1 | tf_op jit(solution)/shard_map/gate_own/pallas_call | solution.py:65
  13.2 0.4 pack_taps.1.here_ref
  13.6 0.5 copy-done.14
  14.1 0.4 collective-permute-start.1
  14.6 1.6 %collective-permute-start.5 = (bf16[2,16,2048]{2,1,0:T(8,128)(2,1)S(1)}, bf16[2,16,2048]{2,1,0:T(8,128)(2,1)S(1)}, u32[]{:S(2)}, u32[]{:S(2)}) collective-permute-start(bf16[2,16,2048]{2,1,0:T(8,128)(2,1)S(1)} %pack_taps.1.here_ref), channel_id=1, source_target_pairs={{0,16},{16,0},{1,17},{17,1},{2,18},{18,2},{3,19},{19,3},{4,20},{20... | collective-permute-start | bytes 393224 | tf_op jit(solution)/shard_map/ppermute | solution.py:553
  16.2 2.6 %collective-permute-start.4 = (bf16[2,128,256]{2,1,0:T(8,128)(2,1)S(1)}, bf16[2,128,256]{2,1,0:T(8,128)(2,1)S(1)}, u32[]{:S(2)}, u32[]{:S(2)}) collective-permute-start(bf16[2,128,256]{2,1,0:T(8,128)(2,1)S(1)} %pad_maximum_fusion.2), channel_id=1, source_target_pairs={{0,6},{1,7},{2,4},{3,5},{4,2},{5,3},{6,0},{7,1},{8,14},{9,15},{10,... | collective-permute-start | bytes 393224 | tf_op jit(solution)/shard_map/ppermute | solution.py:155
  18.9 0.6 collective-permute-start.3
  19.5 0.4 collective-permute-start.2
  20.1 1.8 %taps.1.refs_5_ = bf16[8,32,1024]{2,1,0:T(8,128)(2,1)S(1)} custom-call(bf16[2,16,2048]{2,1,0:T(8,128)(2,1)S(1)} %pack_taps.1.here_ref, bf16[2,16,2048]{2,1,0:T(8,128)(2,1)S(1)} %collective-permute-done.5.there_ref, bf16[512,1024]{1,0:T(8,128)(2,1)S(1)} %copy-done.4), custom_call_target="tpu_custom_call" | custom-call | flops 1 | bytes 1 | tf_op jit(solution)/shard_map/taps/pallas_call | solution.py:65
  21.9 10.9 %collective-permute-done.4.refs_4_ = bf16[2,128,256]{2,1,0:T(8,128)(2,1)S(1)} collective-permute-done((bf16[2,128,256]{2,1,0:T(8,128)(2,1)S(1)}, bf16[2,128,256]{2,1,0:T(8,128)(2,1)S(1)}, u32[]{:S(2)}, u32[]{:S(2)}) %collective-permute-start.4) | collective-permute-done | bytes 131104 | tf_op jit(solution)/shard_map/ppermute | solution.py:155
  32.8 3.7 %collective-permute-done.3.refs_3_ = bf16[2,128,256]{2,1,0:T(8,128)(2,1)S(1)} collective-permute-done((bf16[2,128,256]{2,1,0:T(8,128)(2,1)S(1)}, bf16[2,128,256]{2,1,0:T(8,128)(2,1)S(1)}, u32[]{:S(2)}, u32[]{:S(2)}) %collective-permute-start.3) | collective-permute-done | bytes 131104 | tf_op jit(solution)/shard_map/ppermute | solution.py:155
  36.5 6.8 %results.1 = bf16[8,2,128,256]{3,2,1,0:T(8,128)(2,1)} custom-call(bf16[16,128,256]{2,1,0:T(8,128)(2,1)S(1)} %all-to-all-done.near_ref, bf16[1,128,256]{2,1,0:T(8,128)(2,1)S(1)} %bitcast.8, bf16[1,128,256]{2,1,0:T(8,128)(2,1)S(1)} %get-tuple-element.52.refs_1_, bf16[2,128,256]{2,1,0:T(8,128)(2,1)S(1)} %collective-permute-done.2.refs_2_, ...), custom_call_target="tpu_custom_call" | custom-call | flops 137438953472 | bytes 137438953472 | tf_op jit(solution)/shard_map/results/pallas_call | solution.py:65
  43.4 3.6 %all-to-all-start.1 = ((bf16[8,2,128,256]{3,2,1,0:T(8,128)(2,1)}), bf16[8,2,128,256]{3,2,1,0:T(8,128)(2,1)S(1)}, u32[]{:S(2)}, u32[]{:S(2)}) async-start(bf16[8,2,128,256]{3,2,1,0:T(8,128)(2,1)} %results.1), calls=%async_computation.1 | async-start | bytes 2097152 | tf_op jit(solution)/shard_map/all_to_all | solution.py:566
  47.0 6.8 %filter_terms.1 = (bf16[16,2048]{1,0:T(8,128)(2,1)}, f32[16,2048]{1,0:T(8,128)}, bf16[16,2048]{1,0:T(8,128)(2,1)}) custom-call(bf16[16,128,256]{2,1,0:T(8,128)(2,1)} %copy-done.5, bf16[1,128,256]{2,1,0:T(8,128)(2,1)} %bitcast.9, bf16[1,128,256]{2,1,0:T(8,128)(2,1)} %copy-done.7, bf16[2,128,256]{2,1,0:T(8,128)(2,1)} %copy-done.10, ...), custom_call_target="tpu_custom_call" | custom-call | flops 1 | bytes 1 | tf_op jit(solution)/shard_map/filter_terms/pallas_call | solution.py:65
  53.8 1.3 %collective-permute-start.6 = (bf16[16,2048]{1,0:T(8,128)(2,1)}, bf16[16,2048]{1,0:T(8,128)(2,1)S(1)}, u32[]{:S(2)}, u32[]{:S(2)}) collective-permute-start(bf16[16,2048]{1,0:T(8,128)(2,1)} %get-tuple-element.43), channel_id=1, source_target_pairs={{16,8},{17,9},{18,10},{19,11},{20,12},{21,13},{22,14},{23,15},{24,... | collective-permute-start | bytes 196616 | tf_op jit(solution)/shard_map/ppermute | solution.py:571
  55.1 5.4 %collective-permute-start.7 = (bf16[16,2048]{1,0:T(8,128)(2,1)}, bf16[16,2048]{1,0:T(8,128)(2,1)S(1)}, u32[]{:S(2)}, u32[]{:S(2)}) collective-permute-start(bf16[16,2048]{1,0:T(8,128)(2,1)} %get-tuple-element.43), channel_id=1, source_target_pairs={{0,8},{1,9},{2,10},{3,11},{4,12},{5,13},{6,14},{7,15},{8,0},{9,1},... | collective-permute-start | bytes 196616 | tf_op jit(solution)/shard_map/ppermute | solution.py:571
  60.5 0.9 %collective-permute-start.8 = (bf16[16,2048]{1,0:T(8,128)(2,1)}, bf16[16,2048]{1,0:T(8,128)(2,1)S(1)}, u32[]{:S(2)}, u32[]{:S(2)}) collective-permute-start(bf16[16,2048]{1,0:T(8,128)(2,1)} %get-tuple-element.44), channel_id=1, source_target_pairs={{0,16},{16,0},{1,17},{17,1},{2,18},{18,2},{3,19},{19,3},{4,20},{20... | collective-permute-start | bytes 196616 | tf_op jit(solution)/shard_map/ppermute | solution.py:553
  61.5 1.6 %finish.1 = (bf16[1024,256]{1,0:T(8,128)(2,1)}, bf16[1024,256]{1,0:T(8,128)(2,1)}, bf16[1024,256]{1,0:T(8,128)(2,1)}, bf16[1024,256]{1,0:T(8,128)(2,1)}) custom-call(bf16[8,2,4,2,16,256]{5,4,3,2,1,0:T(8,128)(2,1)S(1)} %bitcast.7, bf16[1024,256]{1,0:T(8,128)(2,1)S(1)} %copy-done, bf16[1024,256]{1,0:T(8,128)(2,1)S(1)} %copy-done.1, ...), custom_call_target="tpu_custom_call" | custom-call | tf_op jit(solution)/shard_map/finish/pallas_call | solution.py:188
  63.1 0.2 collective-permute-done.7
  63.3 1.7 %collective-permute-done.8 = bf16[16,2048]{1,0:T(8,128)(2,1)S(1)} collective-permute-done((bf16[16,2048]{1,0:T(8,128)(2,1)}, bf16[16,2048]{1,0:T(8,128)(2,1)S(1)}, u32[]{:S(2)}, u32[]{:S(2)}) %collective-permute-start.8) | collective-permute-done | bytes 65568 | tf_op jit(solution)/shard_map/ppermute | solution.py:553
  65.1 0.7 %convert_add_fusion = f32[16,2048]{1,0:T(8,128)} fusion(bf16[16,2048]{1,0:T(8,128)(2,1)S(1)} %collective-permute-done.8, f32[16,2048]{1,0:T(8,128)S(1)} %copy-done.13, bf16[16,2048]{1,0:T(8,128)(2,1)S(1)} %collective-permute-done.7, bf16[16,2048]{1,0:T(8,128)(2,1)S(1)} %collective-permute-done.6), kind=kLoop, calls=%fused_computation.3 | loop fusion | flops 196608 | bytes 458752 | tf_op jit(solution)/shard_map/add | solution.py:576
  (41 shorter events, 0.4 us)
Async XLA Ops:
  2.9 10.3 %collective-permute-start = (bf16[16,2048]{1,0:T(8,128)(2,1)}, bf16[16,2048]{1,0:T(8,128)(2,1)S(1)}, u32[]{:S(2)}, u32[]{:S(2)}) collective-permute-start(bf16[16,2048]{1,0:T(8,128)(2,1)} %get-tuple-element.28.taps_ref), channel_id=1, source_target_pairs={{0,8},{1,9},{2,10},{3,11},{4,12},{5,13},{6,14},{7,15},{8,0},{9,1},... | collective-permute-start | bytes 196616 | tf_op jit(solution)/shard_map/ppermute | solution.py:550
  7.0 29.5 %all-to-all-start = ((bf16[16,128,256]{2,1,0:T(8,128)(2,1)}), bf16[16,128,256]{2,1,0:T(8,128)(2,1)S(1)}, u32[]{:S(2)}, u32[]{:S(2)}) async-start(bf16[16,128,256]{2,1,0:T(8,128)(2,1)} %bitcast.10), calls=%async_computation | async-start | bytes 2097152 | tf_op jit(solution)/shard_map/all_to_all | solution.py:559
  10.9 2.3 %copy-start.11 = (bf16[16,2048]{1,0:T(8,128)(2,1)S(1)}, bf16[16,2048]{1,0:T(8,128)(2,1)}, u32[]{:S(2)}) copy-start(bf16[16,2048]{1,0:T(8,128)(2,1)} %get-tuple-element.28.taps_ref) | copy-start | bytes 196612
  13.6 6.5 %copy-start.4 = (bf16[512,1024]{1,0:T(8,128)(2,1)S(1)}, bf16[512,1024]{1,0:T(8,128)(2,1)}, u32[]{:S(2)}) copy-start(bf16[512,1024]{1,0:T(8,128)(2,1)} %constant.2.clone.table_hbm.refs_6_.refs_5_) | copy-start | bytes 3145732
  14.1 2.0 %collective-permute-start.1 = (bf16[4,128,256]{2,1,0:T(8,128)(2,1)S(1)}, bf16[4,128,256]{2,1,0:T(8,128)(2,1)S(1)}, u32[]{:S(2)}, u32[]{:S(2)}) collective-permute-start(bf16[4,128,256]{2,1,0:T(8,128)(2,1)S(1)} %bitcast.14), channel_id=1, source_target_pairs={{0,1},{1,0},{2,3},{3,2},{4,5},{5,4},{6,7},{7,6},{8,9},{9,8},{10,11... | collective-permute-start | bytes 786440 | tf_op jit(solution)/shard_map/ppermute | solution.py:155
  14.6 21.9 %copy-start.6 = (bf16[1,4,2,16,256]{4,3,2,1,0:T(8,128)(2,1)}, bf16[1,4,2,16,256]{4,3,2,1,0:T(8,128)(2,1)S(1)}, u32[]{:S(2)}) copy-start(bf16[1,4,2,16,256]{4,3,2,1,0:T(8,128)(2,1)S(1)} %get-tuple-element.48) | copy-start | bytes 196612
  14.6 5.5 %collective-permute-start.5 = (bf16[2,16,2048]{2,1,0:T(8,128)(2,1)S(1)}, bf16[2,16,2048]{2,1,0:T(8,128)(2,1)S(1)}, u32[]{:S(2)}, u32[]{:S(2)}) collective-permute-start(bf16[2,16,2048]{2,1,0:T(8,128)(2,1)S(1)} %pack_taps.1.here_ref), channel_id=1, source_target_pairs={{0,16},{16,0},{1,17},{17,1},{2,18},{18,2},{3,19},{19,3},{4,20},{20... | collective-permute-start | bytes 393224 | tf_op jit(solution)/shard_map/ppermute | solution.py:553
  16.2 20.4 %copy-start.7 = (bf16[1,128,256]{2,1,0:T(8,128)(2,1)}, bf16[1,128,256]{2,1,0:T(8,128)(2,1)S(1)}, u32[]{:S(2)}) copy-start(bf16[1,128,256]{2,1,0:T(8,128)(2,1)S(1)} %get-tuple-element.52.refs_1_) | copy-start | bytes 196612
  16.2 16.6 %collective-permute-start.4 = (bf16[2,128,256]{2,1,0:T(8,128)(2,1)S(1)}, bf16[2,128,256]{2,1,0:T(8,128)(2,1)S(1)}, u32[]{:S(2)}, u32[]{:S(2)}) collective-permute-start(bf16[2,128,256]{2,1,0:T(8,128)(2,1)S(1)} %pad_maximum_fusion.2), channel_id=1, source_target_pairs={{0,6},{1,7},{2,4},{3,5},{4,2},{5,3},{6,0},{7,1},{8,14},{9,15},{10,... | collective-permute-start | bytes 393224 | tf_op jit(solution)/shard_map/ppermute | solution.py:155
  18.9 17.6 %collective-permute-start.3 = (bf16[2,128,256]{2,1,0:T(8,128)(2,1)S(1)}, bf16[2,128,256]{2,1,0:T(8,128)(2,1)S(1)}, u32[]{:S(2)}, u32[]{:S(2)}) collective-permute-start(bf16[2,128,256]{2,1,0:T(8,128)(2,1)S(1)} %pad_maximum_fusion.1), channel_id=1, source_target_pairs={{0,4},{1,5},{2,6},{3,7},{4,0},{5,1},{6,2},{7,3},{8,12},{9,13},{10,... | collective-permute-start | bytes 393224 | tf_op jit(solution)/shard_map/ppermute | solution.py:155
  19.5 17.0 %collective-permute-start.2 = (bf16[2,128,256]{2,1,0:T(8,128)(2,1)S(1)}, bf16[2,128,256]{2,1,0:T(8,128)(2,1)S(1)}, u32[]{:S(2)}, u32[]{:S(2)}) collective-permute-start(bf16[2,128,256]{2,1,0:T(8,128)(2,1)S(1)} %pad_maximum_fusion), channel_id=1, source_target_pairs={{0,2},{1,3},{2,0},{3,1},{4,6},{5,7},{6,4},{7,5},{8,10},{9,11},{10,... | collective-permute-start | bytes 393224 | tf_op jit(solution)/shard_map/ppermute | solution.py:155
  32.8 10.6 %copy-start.8 = (bf16[2,128,256]{2,1,0:T(8,128)(2,1)}, bf16[2,128,256]{2,1,0:T(8,128)(2,1)S(1)}, u32[]{:S(2)}) copy-start(bf16[2,128,256]{2,1,0:T(8,128)(2,1)S(1)} %collective-permute-done.4.refs_4_) | copy-start | bytes 393220
  36.5 6.9 %copy-start.9 = (bf16[2,128,256]{2,1,0:T(8,128)(2,1)}, bf16[2,128,256]{2,1,0:T(8,128)(2,1)S(1)}, u32[]{:S(2)}) copy-start(bf16[2,128,256]{2,1,0:T(8,128)(2,1)S(1)} %collective-permute-done.3.refs_3_) | copy-start | bytes 393220
  36.5 6.9 %copy-start.10 = (bf16[2,128,256]{2,1,0:T(8,128)(2,1)}, bf16[2,128,256]{2,1,0:T(8,128)(2,1)S(1)}, u32[]{:S(2)}) copy-start(bf16[2,128,256]{2,1,0:T(8,128)(2,1)S(1)} %collective-permute-done.2.refs_2_) | copy-start | bytes 393220
  36.5 6.9 %copy-start.5 = (bf16[16,128,256]{2,1,0:T(8,128)(2,1)}, bf16[16,128,256]{2,1,0:T(8,128)(2,1)S(1)}, u32[]{:S(2)}) copy-start(bf16[16,128,256]{2,1,0:T(8,128)(2,1)S(1)} %all-to-all-done.near_ref) | copy-start | bytes 3145732
  43.4 18.0 %all-to-all-start.1 = ((bf16[8,2,128,256]{3,2,1,0:T(8,128)(2,1)}), bf16[8,2,128,256]{3,2,1,0:T(8,128)(2,1)S(1)}, u32[]{:S(2)}, u32[]{:S(2)}) async-start(bf16[8,2,128,256]{3,2,1,0:T(8,128)(2,1)} %results.1), calls=%async_computation.1 | async-start | bytes 2097152 | tf_op jit(solution)/shard_map/all_to_all | solution.py:566
  47.0 14.4 %copy-start = (bf16[1024,256]{1,0:T(8,128)(2,1)S(1)}, bf16[1024,256]{1,0:T(8,128)(2,1)}, u32[]{:S(2)}) copy-start(bf16[1024,256]{1,0:T(8,128)(2,1)} %pre_ref.5) | copy-start | bytes 1572868
  47.0 14.4 %copy-start.1 = (bf16[1024,256]{1,0:T(8,128)(2,1)S(1)}, bf16[1024,256]{1,0:T(8,128)(2,1)}, u32[]{:S(2)}) copy-start(bf16[1024,256]{1,0:T(8,128)(2,1)} %value_ref.5) | copy-start | bytes 1572868
  47.0 14.4 %copy-start.2 = (bf16[1024,256]{1,0:T(8,128)(2,1)S(1)}, bf16[1024,256]{1,0:T(8,128)(2,1)}, u32[]{:S(2)}) copy-start(bf16[1024,256]{1,0:T(8,128)(2,1)} %post_ref.5) | copy-start | bytes 1572868
  47.0 14.4 %copy-start.3 = (bf16[1024,256]{1,0:T(8,128)(2,1)S(1)}, bf16[1024,256]{1,0:T(8,128)(2,1)}, u32[]{:S(2)}) copy-start(bf16[1024,256]{1,0:T(8,128)(2,1)} %cot_ref.5) | copy-start | bytes 1572868
  53.8 9.3 %collective-permute-start.6 = (bf16[16,2048]{1,0:T(8,128)(2,1)}, bf16[16,2048]{1,0:T(8,128)(2,1)S(1)}, u32[]{:S(2)}, u32[]{:S(2)}) collective-permute-start(bf16[16,2048]{1,0:T(8,128)(2,1)} %get-tuple-element.43), channel_id=1, source_target_pairs={{16,8},{17,9},{18,10},{19,11},{20,12},{21,13},{22,14},{23,15},{24,... | collective-permute-start | bytes 196616 | tf_op jit(solution)/shard_map/ppermute | solution.py:571
  55.1 8.2 %collective-permute-start.7 = (bf16[16,2048]{1,0:T(8,128)(2,1)}, bf16[16,2048]{1,0:T(8,128)(2,1)S(1)}, u32[]{:S(2)}, u32[]{:S(2)}) collective-permute-start(bf16[16,2048]{1,0:T(8,128)(2,1)} %get-tuple-element.43), channel_id=1, source_target_pairs={{0,8},{1,9},{2,10},{3,11},{4,12},{5,13},{6,14},{7,15},{8,0},{9,1},... | collective-permute-start | bytes 196616 | tf_op jit(solution)/shard_map/ppermute | solution.py:571
  60.5 4.5 %collective-permute-start.8 = (bf16[16,2048]{1,0:T(8,128)(2,1)}, bf16[16,2048]{1,0:T(8,128)(2,1)S(1)}, u32[]{:S(2)}, u32[]{:S(2)}) collective-permute-start(bf16[16,2048]{1,0:T(8,128)(2,1)} %get-tuple-element.44), channel_id=1, source_target_pairs={{0,16},{16,0},{1,17},{17,1},{2,18},{18,2},{3,19},{19,3},{4,20},{20... | collective-permute-start | bytes 196616 | tf_op jit(solution)/shard_map/ppermute | solution.py:553
  61.4 3.6 %copy-start.13 = (f32[16,2048]{1,0:T(8,128)S(1)}, f32[16,2048]{1,0:T(8,128)}, u32[]{:S(2)}) copy-start(f32[16,2048]{1,0:T(8,128)} %get-tuple-element.42) | copy-start | bytes 393220
  (2 other events, 2.3 us)

commit v5 on v4

--- a/solution.py
+++ b/solution.py
@@ -297,8 +297,8 @@
         spec_ref[..., columns] = dot(staged, table_ref[:, columns]).reshape(spec_ref.shape[:-1] + (2 * LANES,))
 
 
-def stage_all(near_ref, own_refs, slots, stage_ref, half_blocks):
-    _, count, _, size = stage_ref.shape
+def stage_all(near_ref, own_refs, slots, near_stage, far_stage, own_stage, half_blocks, far_rows):
+    count, _, size = near_stage.shape
     tokens = near_ref.shape[2]
     merge = size // tokens
     half, me = place(half_blocks)
@@ -306,14 +306,18 @@
         outer, inner = order(k, count, half, True), order(k, count, half, False)
         for q in range(merge):
             lanes = pl.ds(q * tokens, tokens)
-            stage_ref[0, k, :, lanes] = near_ref[half * half_blocks + outer * merge + q]
-            stage_ref[1, k, :, lanes] = near_ref[(1 - half) * half_blocks + inner * merge + q]
+            near_stage[k, :, lanes] = near_ref[half * half_blocks + outer * merge + q]
+            at = 0
+            for first, rows in far_rows:
+                far = near_ref[(1 - half) * half_blocks + inner * merge + q, pl.ds(first, rows)]
+                far_stage[k, at : at + rows, lanes] = far
+                at += rows
     for group, ref in zip(slots, own_refs):
         for at, slot in enumerate(group):
             position = jnp.bitwise_xor(me, slot)
             k = order(position // merge, count, half, False)
             start = pl.multiple_of(lax.rem(position, merge) * tokens, tokens)
-            stage_ref[2, k, :, pl.ds(start, tokens)] = ref[at]
+            own_stage[k, :, pl.ds(start, tokens)] = ref[at]
 
 
 def order(k, count, half, outer):
@@ -362,7 +366,8 @@
     def kernel(near_ref, *refs):
         own_refs, (filt_in, table_ref, out_hbm) = refs[: len(own)], refs[len(own) : len(own) + 3]
         stage_ref, filt_ref, spec_ref, prod_ref, held_ref, out_sems = refs[len(own) + 3 :]
-        stage_all(near_ref, own_refs, slots, stage_ref, half_blocks)
+        near_stage, far_stage, own_stage = (stage_ref.at[which] for which in range(3))
+        stage_all(near_ref, own_refs, slots, near_stage, far_stage, own_stage, half_blocks, [(0, rows)])
         filt_ref[...] = filt_in[...].astype(jnp.float32)
         transform(stage_ref, table_ref, spec_ref)
         half, _ = place(half_blocks)
@@ -420,18 +425,21 @@
     )[0]
 
 
-def lag_products(near_ref, other_ref, row_at, strip, repeats, filters, totals):
+def lag_products(near_ref, near_rows, other_ref, other_rows, strip, totals):
     count = near_ref.shape[0]
     sums = [None] * len(totals)
-    for repeat in range(repeats):
-        row = pl.ds(pl.multiple_of(repeat * filters + row_at, SUBLANES), SUBLANES)
-        near = [parts(near_ref, k, row, strip) for k in range(count)]
-        other = [parts(other_ref, k, row, strip) for k in range(count)]
+    for near_row, other_row in zip(near_rows, other_rows):
+        near = [parts(near_ref, k, pl.ds(near_row, SUBLANES), strip) for k in range(count)]
+        other = [parts(other_ref, k, pl.ds(other_row, SUBLANES), strip) for k in range(count)]
         for at, total in enumerate(totals):
             for a in range(count):
                 if 0 <= total - a < count:
                     sums[at] = add(sums[at], conj_times(near[a], other[total - a]))
     return sums
+
+
+def repeat_rows(first, step, repeats):
+    return [pl.multiple_of(r * step + first, SUBLANES) for r in range(repeats)]
 
 
 def join_lags(ref, row, joint_ref, base):
@@ -457,36 +465,36 @@
 
     def kernel(near_ref, *refs):
         own_refs, refs = refs[: len(own)], refs[len(own) :]
-        table_ref, give_hbm, mine_hbm, theirs_hbm, stage_ref, spec_ref, local_ref, cross_ref, joint_ref = refs[:9]
-        held_ref, give_ref, mine_ref, theirs_ref, sems = refs[9:]
+        table_ref, give_hbm, mine_hbm, theirs_hbm, stage_ref, far_stage, spec_ref, far_ref, local_ref, cross_ref, joint_ref = refs[:11]
+        held_ref, give_ref, mine_ref, theirs_ref, sems = refs[11:]
         half, _ = place(half_blocks)
         group = lax.axis_index("dp")
         turn = jnp.where(half == 0, 1.0, -1.0).astype(jnp.float32)
-        stage_all(near_ref, own_refs, slots, stage_ref, half_blocks)
+        mine = pl.multiple_of(half * kept, SUBLANES)
+        other = pl.multiple_of((1 - half) * kept, SUBLANES)
+        far_rows = [(pl.multiple_of(r * filters + half * kept, kept), kept) for r in range(repeats)]
+        stage_all(near_ref, own_refs, slots, stage_ref.at[0], far_stage, stage_ref.at[1], half_blocks, far_rows)
         transform(stage_ref, table_ref, spec_ref)
-        near_spec, far_spec, own_spec = (spec_ref.at[which] for which in range(3))
+        transform(far_stage, table_ref, far_ref)
+        near_spec, own_spec = spec_ref.at[0], spec_ref.at[1]
 
         def local_tile(first):
+            rows_at = repeat_rows(first, filters, repeats)
             for strip in range(size // LANES):
-                sums = lag_products(near_spec, own_spec, first, strip, repeats, filters, [count - 1 - k for k in range(count)])
+                totals = [count - 1 - k for k in range(count)]
+                sums = lag_products(near_spec, rows_at, own_spec, rows_at, strip, totals)
                 for k, (real, imag) in enumerate(sums):
                     keep(local_ref, k, pl.ds(first, SUBLANES), strip, (real, turn * imag))
 
         tile_loop(filters, local_tile)
-        mine = pl.multiple_of(half * kept, SUBLANES)
-        other = pl.multiple_of((1 - half) * kept, SUBLANES)
-        join_lags(local_ref, pl.ds(other, kept), joint_ref, 0)
-        result = back(joint_ref[:count].reshape(count * kept, width), table_ref[...]).reshape(count, kept, size)
-        for k in range(count):
-            give_ref[:, k * size : (k + 1) * size] = result[k].astype(jnp.bfloat16)
-        sent = begin([pltpu.make_async_copy(give_ref, give_hbm, sems.at[1])])
 
         def cross_tile(first):
             row = pl.ds(first, SUBLANES)
             at = pl.ds(pl.multiple_of(mine + first, SUBLANES), SUBLANES)
+            near_at, far_at = repeat_rows(mine + first, filters, repeats), repeat_rows(first, kept, repeats)
             for strip in range(size // LANES):
                 totals = [2 * count - 1 - k for k in range(1, 2 * count)]
-                sums = lag_products(near_spec, far_spec, mine + first, strip, repeats, filters, totals)
+                sums = lag_products(near_spec, near_at, far_ref, far_at, strip, totals)
                 keep(cross_ref, 0, row, strip, parts(local_ref, 0, at, strip))
                 for k, (real, imag) in enumerate(sums, 1):
                     value = (real, turn * imag)
@@ -494,8 +502,12 @@
 
         tile_loop(kept, cross_tile)
         join_lags(cross_ref, slice(None), joint_ref, 0)
-        result = back(joint_ref[...].reshape(2 * count * kept, width), table_ref[...])
-        held_ref[...] = result.reshape(2, count, kept, size)
+        join_lags(local_ref, pl.ds(other, kept), joint_ref, 2 * count)
+        result = back(joint_ref[...].reshape(3 * count * kept, width), table_ref[...]).reshape(3, count, kept, size)
+        held_ref[...] = result[:2]
+        for k in range(count):
+            give_ref[:, k * size : (k + 1) * size] = result[2, k].astype(jnp.bfloat16)
+        sent = begin([pltpu.make_async_copy(give_ref, give_hbm, sems.at[1])])
         for k in range(count):
             columns = slice(k * size, (k + 1) * size)
             mine_ref[:, columns] = held_ref[group, k]
@@ -518,11 +530,13 @@
             jax.ShapeDtypeStruct((kept, lags), jnp.bfloat16),
         ],
         [
-            pltpu.VMEM((3, count, rows, size), jnp.bfloat16),
-            pltpu.VMEM((3, count, rows, width), jnp.float32),
+            pltpu.VMEM((2, count, rows, size), jnp.bfloat16),
+            pltpu.VMEM((count, rows // 2, size), jnp.bfloat16),
+            pltpu.VMEM((2, count, rows, width), jnp.float32),
+            pltpu.VMEM((count, rows // 2, width), jnp.float32),
             pltpu.VMEM((count, filters, width), jnp.float32),
             pltpu.VMEM((2 * count, kept, width), jnp.float32),
-            pltpu.VMEM((2 * count, kept, width), jnp.bfloat16),
+            pltpu.VMEM((3 * count, kept, width), jnp.bfloat16),
             pltpu.VMEM((2, count, kept, size), jnp.float32),
             pltpu.VMEM((kept, lags), jnp.bfloat16),
             pltpu.VMEM((kept, lags), jnp.float32),

time: 66.1 us -> 65.6 us (level)
  Pallas kernels: 21.8 us -> 21.1 us
    all_to_all x1, waiting for transfers between devices: 0.01 us -> 2.02 us  [body(): lax.all_to_all(result, 'ctx', split_axis=0, concat_axis=0, tiled=True, ax...]
    ppermute x2, waiting for transfers between devices: 1.94 us -> 0.22 us  [other_group(): return lax.ppermute(array, 'dp', [(0, 1), (1, 0)])]
    pallas_call x6, Pallas kernels: 20.2 us -> 19.5 us  [call(): pl.pallas_call(kernel, in_specs=[pl.BlockSpec(memory_space=space)] * len(...]
  transfers between devices with their start and end apart: 11 -> 11, of which waited for: 5 -> 4; matrix products, arithmetic and copies ran while one was open for 0% -> 0% of each run, Pallas kernels for 19% -> 19%
where the time goes in v5:
time: 65.6 us; the launch traced here: 65.1 us
  starting transfers between devices  24.9 us (38%)
  Pallas kernels  21.1 us (32%)
  waiting for transfers between devices  16.8 us (26%)
  between operations  0.95 us (1%)
  other arithmetic  0.73 us (1%)
    pallas_call x6, Pallas kernels, call(): pl.pallas_call(kernel, in_specs=[pl.BlockSpec(memory_space=space)] * len(...  19.5 us
    ppermute x4, waiting for transfers between devices, swap(): lax.ppermute(array, 'ctx', [(i, i ^ slot) for i in range(2 * half_blocks)])  14.6 us
    ppermute x2, starting transfers between devices, body(): lax.ppermute(give, ('dp', 'ctx'), [(g * blocks + i, i ^ half_blocks) for...  6.7 us
    ppermute x1, starting transfers between devices, swap(): lax.ppermute(array, 'ctx', [(i, i ^ half_blocks) for i in range(blocks)])  4.12 us
    ppermute x4, starting transfers between devices, swap(): lax.ppermute(array, 'ctx', [(i, i ^ slot) for i in range(2 * half_blocks)])  4.11 us
    all_to_all x1, starting transfers between devices, body(): lax.all_to_all(near.reshape(blocks, rows, tokens), 'ctx', split_axis=0, c...  3.91 us
    all_to_all x1, starting transfers between devices, body(): lax.all_to_all(result, 'ctx', split_axis=0, concat_axis=0, tiled=True, ax...  3.57 us
    ppermute x2, starting transfers between devices, other_group(): return lax.ppermute(array, 'dp', [(0, 1), (1, 0)])  2.46 us
  transfers between devices with their start and end apart: 11, of which 4 were waited for; matrix products, arithmetic and copies ran while one was open for 0% of the time, Pallas kernels for 19%

profile of v5, /device:TPU:0, one launch (start us, length us, event | category | flops | bytes accessed | tf_op | source)
XLA Modules:
  0.0 65.1 jit_solution(11749799851212473483)
XLA Ops:
  0.6 2.2 %gate_near.1 = (bf16[2,8,4,2,16,256]{5,4,3,2,1,0:T(8,128)(2,1)}, bf16[16,2048]{1,0:T(8,128)(2,1)}) custom-call(bf16[1024,256]{1,0:T(8,128)(2,1)} %pre_ref.5, bf16[1024,256]{1,0:T(8,128)(2,1)} %value_ref.5, bf16[1024,256]{1,0:T(8,128)(2,1)} %post_ref.5, bf16[1024,256]{1,0:T(8,128)(2,1)} %cot_ref.5, f32[16,2048]{1,0:T(8,128)} %refs_0_.1), custom_call_target="tpu_custom_call" | custom-call | flops 1 | bytes 1 | tf_op jit(solution)/shard_map/gate_near/pallas_call | solution.py:65
  2.9 4.1 %collective-permute-start = (bf16[16,2048]{1,0:T(8,128)(2,1)}, bf16[16,2048]{1,0:T(8,128)(2,1)S(1)}, u32[]{:S(2)}, u32[]{:S(2)}) collective-permute-start(bf16[16,2048]{1,0:T(8,128)(2,1)} %get-tuple-element.28.taps_ref), channel_id=1, source_target_pairs={{0,8},{1,9},{2,10},{3,11},{4,12},{5,13},{6,14},{7,15},{8,0},{9,1},... | collective-permute-start | bytes 196616 | tf_op jit(solution)/shard_map/ppermute | solution.py:564
  7.0 3.9 %all-to-all-start = ((bf16[16,128,256]{2,1,0:T(8,128)(2,1)}), bf16[16,128,256]{2,1,0:T(8,128)(2,1)S(1)}, u32[]{:S(2)}, u32[]{:S(2)}) async-start(bf16[16,128,256]{2,1,0:T(8,128)(2,1)} %bitcast.10), calls=%async_computation | async-start | bytes 2097152 | tf_op jit(solution)/shard_map/all_to_all | solution.py:573
  10.9 2.3 %gate_own.1 = (bf16[4,4,2,16,256]{4,3,2,1,0:T(8,128)(2,1)}, bf16[4,4,2,16,256]{4,3,2,1,0:T(8,128)(2,1)}) custom-call(bf16[1024,256]{1,0:T(8,128)(2,1)} %pre_ref.5, bf16[1024,256]{1,0:T(8,128)(2,1)} %value_ref.5, bf16[1024,256]{1,0:T(8,128)(2,1)} %post_ref.5, bf16[1024,256]{1,0:T(8,128)(2,1)} %cot_ref.5), custom_call_target="tpu_custom_call" | custom-call | flops 1 | bytes 1 | tf_op jit(solution)/shard_map/gate_own/pallas_call | solution.py:65
  13.2 0.4 pack_taps.1.here_ref
  13.6 0.5 copy-done.14
  14.1 0.4 collective-permute-start.1
  14.6 1.6 %collective-permute-start.5 = (bf16[2,16,2048]{2,1,0:T(8,128)(2,1)S(1)}, bf16[2,16,2048]{2,1,0:T(8,128)(2,1)S(1)}, u32[]{:S(2)}, u32[]{:S(2)}) collective-permute-start(bf16[2,16,2048]{2,1,0:T(8,128)(2,1)S(1)} %pack_taps.1.here_ref), channel_id=1, source_target_pairs={{0,16},{16,0},{1,17},{17,1},{2,18},{18,2},{3,19},{19,3},{4,20},{20... | collective-permute-start | bytes 393224 | tf_op jit(solution)/shard_map/ppermute | solution.py:567
  16.2 2.6 %collective-permute-start.4 = (bf16[2,128,256]{2,1,0:T(8,128)(2,1)S(1)}, bf16[2,128,256]{2,1,0:T(8,128)(2,1)S(1)}, u32[]{:S(2)}, u32[]{:S(2)}) collective-permute-start(bf16[2,128,256]{2,1,0:T(8,128)(2,1)S(1)} %pad_maximum_fusion.2), channel_id=1, source_target_pairs={{0,6},{1,7},{2,4},{3,5},{4,2},{5,3},{6,0},{7,1},{8,14},{9,15},{10,... | collective-permute-start | bytes 393224 | tf_op jit(solution)/shard_map/ppermute | solution.py:155
  18.9 0.6 collective-permute-start.3
  19.5 0.4 collective-permute-start.2
  19.9 0.2 collective-permute-done.5.there_ref
  20.1 1.8 %taps.1.refs_5_ = bf16[8,32,1024]{2,1,0:T(8,128)(2,1)S(1)} custom-call(bf16[2,16,2048]{2,1,0:T(8,128)(2,1)S(1)} %pack_taps.1.here_ref, bf16[2,16,2048]{2,1,0:T(8,128)(2,1)S(1)} %collective-permute-done.5.there_ref, bf16[512,1024]{1,0:T(8,128)(2,1)S(1)} %copy-done.4), custom_call_target="tpu_custom_call" | custom-call | flops 1 | bytes 1 | tf_op jit(solution)/shard_map/taps/pallas_call | solution.py:65
  21.9 10.9 %collective-permute-done.4.refs_4_ = bf16[2,128,256]{2,1,0:T(8,128)(2,1)S(1)} collective-permute-done((bf16[2,128,256]{2,1,0:T(8,128)(2,1)S(1)}, bf16[2,128,256]{2,1,0:T(8,128)(2,1)S(1)}, u32[]{:S(2)}, u32[]{:S(2)}) %collective-permute-start.4) | collective-permute-done | bytes 131104 | tf_op jit(solution)/shard_map/ppermute | solution.py:155
  32.8 3.7 %collective-permute-done.3.refs_3_ = bf16[2,128,256]{2,1,0:T(8,128)(2,1)S(1)} collective-permute-done((bf16[2,128,256]{2,1,0:T(8,128)(2,1)S(1)}, bf16[2,128,256]{2,1,0:T(8,128)(2,1)S(1)}, u32[]{:S(2)}, u32[]{:S(2)}) %collective-permute-start.3) | collective-permute-done | bytes 131104 | tf_op jit(solution)/shard_map/ppermute | solution.py:155
  36.5 6.8 %results.1 = bf16[8,2,128,256]{3,2,1,0:T(8,128)(2,1)} custom-call(bf16[16,128,256]{2,1,0:T(8,128)(2,1)S(1)} %all-to-all-done.near_ref, bf16[1,128,256]{2,1,0:T(8,128)(2,1)S(1)} %bitcast.8, bf16[1,128,256]{2,1,0:T(8,128)(2,1)S(1)} %get-tuple-element.52.refs_1_, bf16[2,128,256]{2,1,0:T(8,128)(2,1)S(1)} %collective-permute-done.2.refs_2_, ...), custom_call_target="tpu_custom_call" | custom-call | flops 137438953472 | bytes 137438953472 | tf_op jit(solution)/shard_map/results/pallas_call | solution.py:65
  43.4 3.6 %all-to-all-start.1 = ((bf16[8,2,128,256]{3,2,1,0:T(8,128)(2,1)}), bf16[8,2,128,256]{3,2,1,0:T(8,128)(2,1)S(1)}, u32[]{:S(2)}, u32[]{:S(2)}) async-start(bf16[8,2,128,256]{3,2,1,0:T(8,128)(2,1)} %results.1), calls=%async_computation.1 | async-start | bytes 2097152 | tf_op jit(solution)/shard_map/all_to_all | solution.py:580
  47.0 6.1 %filter_terms.1 = (bf16[16,2048]{1,0:T(8,128)(2,1)}, f32[16,2048]{1,0:T(8,128)}, bf16[16,2048]{1,0:T(8,128)(2,1)}) custom-call(bf16[16,128,256]{2,1,0:T(8,128)(2,1)} %copy-done.5, bf16[1,128,256]{2,1,0:T(8,128)(2,1)} %bitcast.9, bf16[1,128,256]{2,1,0:T(8,128)(2,1)} %copy-done.7, bf16[2,128,256]{2,1,0:T(8,128)(2,1)} %copy-done.10, ...), custom_call_target="tpu_custom_call" | custom-call | flops 1 | bytes 1 | tf_op jit(solution)/shard_map/filter_terms/pallas_call | solution.py:65
  53.1 1.3 %collective-permute-start.6 = (bf16[16,2048]{1,0:T(8,128)(2,1)}, bf16[16,2048]{1,0:T(8,128)(2,1)S(1)}, u32[]{:S(2)}, u32[]{:S(2)}) collective-permute-start(bf16[16,2048]{1,0:T(8,128)(2,1)} %get-tuple-element.43), channel_id=1, source_target_pairs={{16,8},{17,9},{18,10},{19,11},{20,12},{21,13},{22,14},{23,15},{24,... | collective-permute-start | bytes 196616 | tf_op jit(solution)/shard_map/ppermute | solution.py:585
  54.4 5.4 %collective-permute-start.7 = (bf16[16,2048]{1,0:T(8,128)(2,1)}, bf16[16,2048]{1,0:T(8,128)(2,1)S(1)}, u32[]{:S(2)}, u32[]{:S(2)}) collective-permute-start(bf16[16,2048]{1,0:T(8,128)(2,1)} %get-tuple-element.43), channel_id=1, source_target_pairs={{0,8},{1,9},{2,10},{3,11},{4,12},{5,13},{6,14},{7,15},{8,0},{9,1},... | collective-permute-start | bytes 196616 | tf_op jit(solution)/shard_map/ppermute | solution.py:585
  59.8 0.9 %collective-permute-start.8 = (bf16[16,2048]{1,0:T(8,128)(2,1)}, bf16[16,2048]{1,0:T(8,128)(2,1)S(1)}, u32[]{:S(2)}, u32[]{:S(2)}) collective-permute-start(bf16[16,2048]{1,0:T(8,128)(2,1)} %get-tuple-element.44), channel_id=1, source_target_pairs={{0,16},{16,0},{1,17},{17,1},{2,18},{18,2},{3,19},{19,3},{4,20},{20... | collective-permute-start | bytes 196616 | tf_op jit(solution)/shard_map/ppermute | solution.py:567
  60.7 2.0 %all-to-all-done.1 = bf16[8,2,128,256]{3,2,1,0:T(8,128)(2,1)S(1)} async-done(((bf16[8,2,128,256]{3,2,1,0:T(8,128)(2,1)}), bf16[8,2,128,256]{3,2,1,0:T(8,128)(2,1)S(1)}, u32[]{:S(2)}, u32[]{:S(2)}) %all-to-all-start.1) | async-done | bytes 1048608 | tf_op jit(solution)/shard_map/all_to_all | solution.py:580
  62.8 1.6 %finish.1 = (bf16[1024,256]{1,0:T(8,128)(2,1)}, bf16[1024,256]{1,0:T(8,128)(2,1)}, bf16[1024,256]{1,0:T(8,128)(2,1)}, bf16[1024,256]{1,0:T(8,128)(2,1)}) custom-call(bf16[8,2,4,2,16,256]{5,4,3,2,1,0:T(8,128)(2,1)S(1)} %bitcast.7, bf16[1024,256]{1,0:T(8,128)(2,1)S(1)} %copy-done, bf16[1024,256]{1,0:T(8,128)(2,1)S(1)} %copy-done.1, ...), custom_call_target="tpu_custom_call" | custom-call | tf_op jit(solution)/shard_map/finish/pallas_call | solution.py:188
  64.5 0.7 %convert_add_fusion = f32[16,2048]{1,0:T(8,128)} fusion(bf16[16,2048]{1,0:T(8,128)(2,1)S(1)} %collective-permute-done.8, f32[16,2048]{1,0:T(8,128)S(1)} %copy-done.13, bf16[16,2048]{1,0:T(8,128)(2,1)S(1)} %collective-permute-done.7, bf16[16,2048]{1,0:T(8,128)(2,1)S(1)} %collective-permute-done.6), kind=kLoop, calls=%fused_computation.3 | loop fusion | flops 196608 | bytes 458752 | tf_op jit(solution)/shard_map/add | solution.py:590
  (41 shorter events, 0.2 us)
Async XLA Ops:
  2.9 10.3 %collective-permute-start = (bf16[16,2048]{1,0:T(8,128)(2,1)}, bf16[16,2048]{1,0:T(8,128)(2,1)S(1)}, u32[]{:S(2)}, u32[]{:S(2)}) collective-permute-start(bf16[16,2048]{1,0:T(8,128)(2,1)} %get-tuple-element.28.taps_ref), channel_id=1, source_target_pairs={{0,8},{1,9},{2,10},{3,11},{4,12},{5,13},{6,14},{7,15},{8,0},{9,1},... | collective-permute-start | bytes 196616 | tf_op jit(solution)/shard_map/ppermute | solution.py:564
  7.0 29.5 %all-to-all-start = ((bf16[16,128,256]{2,1,0:T(8,128)(2,1)}), bf16[16,128,256]{2,1,0:T(8,128)(2,1)S(1)}, u32[]{:S(2)}, u32[]{:S(2)}) async-start(bf16[16,128,256]{2,1,0:T(8,128)(2,1)} %bitcast.10), calls=%async_computation | async-start | bytes 2097152 | tf_op jit(solution)/shard_map/all_to_all | solution.py:573
  10.9 2.3 %copy-start.11 = (bf16[16,2048]{1,0:T(8,128)(2,1)S(1)}, bf16[16,2048]{1,0:T(8,128)(2,1)}, u32[]{:S(2)}) copy-start(bf16[16,2048]{1,0:T(8,128)(2,1)} %get-tuple-element.28.taps_ref) | copy-start | bytes 196612
  13.6 6.5 %copy-start.4 = (bf16[512,1024]{1,0:T(8,128)(2,1)S(1)}, bf16[512,1024]{1,0:T(8,128)(2,1)}, u32[]{:S(2)}) copy-start(bf16[512,1024]{1,0:T(8,128)(2,1)} %constant.2.clone.table_hbm.refs_6_.refs_5_) | copy-start | bytes 3145732
  14.1 2.0 %collective-permute-start.1 = (bf16[4,128,256]{2,1,0:T(8,128)(2,1)S(1)}, bf16[4,128,256]{2,1,0:T(8,128)(2,1)S(1)}, u32[]{:S(2)}, u32[]{:S(2)}) collective-permute-start(bf16[4,128,256]{2,1,0:T(8,128)(2,1)S(1)} %bitcast.14), channel_id=1, source_target_pairs={{0,1},{1,0},{2,3},{3,2},{4,5},{5,4},{6,7},{7,6},{8,9},{9,8},{10,11... | collective-permute-start | bytes 786440 | tf_op jit(solution)/shard_map/ppermute | solution.py:155
  14.6 21.9 %copy-start.6 = (bf16[1,4,2,16,256]{4,3,2,1,0:T(8,128)(2,1)}, bf16[1,4,2,16,256]{4,3,2,1,0:T(8,128)(2,1)S(1)}, u32[]{:S(2)}) copy-start(bf16[1,4,2,16,256]{4,3,2,1,0:T(8,128)(2,1)S(1)} %get-tuple-element.48) | copy-start | bytes 196612
  14.6 5.5 %collective-permute-start.5 = (bf16[2,16,2048]{2,1,0:T(8,128)(2,1)S(1)}, bf16[2,16,2048]{2,1,0:T(8,128)(2,1)S(1)}, u32[]{:S(2)}, u32[]{:S(2)}) collective-permute-start(bf16[2,16,2048]{2,1,0:T(8,128)(2,1)S(1)} %pack_taps.1.here_ref), channel_id=1, source_target_pairs={{0,16},{16,0},{1,17},{17,1},{2,18},{18,2},{3,19},{19,3},{4,20},{20... | collective-permute-start | bytes 393224 | tf_op jit(solution)/shard_map/ppermute | solution.py:567
  16.2 20.4 %copy-start.7 = (bf16[1,128,256]{2,1,0:T(8,128)(2,1)}, bf16[1,128,256]{2,1,0:T(8,128)(2,1)S(1)}, u32[]{:S(2)}) copy-start(bf16[1,128,256]{2,1,0:T(8,128)(2,1)S(1)} %get-tuple-element.52.refs_1_) | copy-start | bytes 196612
  16.2 16.6 %collective-permute-start.4 = (bf16[2,128,256]{2,1,0:T(8,128)(2,1)S(1)}, bf16[2,128,256]{2,1,0:T(8,128)(2,1)S(1)}, u32[]{:S(2)}, u32[]{:S(2)}) collective-permute-start(bf16[2,128,256]{2,1,0:T(8,128)(2,1)S(1)} %pad_maximum_fusion.2), channel_id=1, source_target_pairs={{0,6},{1,7},{2,4},{3,5},{4,2},{5,3},{6,0},{7,1},{8,14},{9,15},{10,... | collective-permute-start | bytes 393224 | tf_op jit(solution)/shard_map/ppermute | solution.py:155
  18.9 17.6 %collective-permute-start.3 = (bf16[2,128,256]{2,1,0:T(8,128)(2,1)S(1)}, bf16[2,128,256]{2,1,0:T(8,128)(2,1)S(1)}, u32[]{:S(2)}, u32[]{:S(2)}) collective-permute-start(bf16[2,128,256]{2,1,0:T(8,128)(2,1)S(1)} %pad_maximum_fusion.1), channel_id=1, source_target_pairs={{0,4},{1,5},{2,6},{3,7},{4,0},{5,1},{6,2},{7,3},{8,12},{9,13},{10,... | collective-permute-start | bytes 393224 | tf_op jit(solution)/shard_map/ppermute | solution.py:155
  19.5 17.0 %collective-permute-start.2 = (bf16[2,128,256]{2,1,0:T(8,128)(2,1)S(1)}, bf16[2,128,256]{2,1,0:T(8,128)(2,1)S(1)}, u32[]{:S(2)}, u32[]{:S(2)}) collective-permute-start(bf16[2,128,256]{2,1,0:T(8,128)(2,1)S(1)} %pad_maximum_fusion), channel_id=1, source_target_pairs={{0,2},{1,3},{2,0},{3,1},{4,6},{5,7},{6,4},{7,5},{8,10},{9,11},{10,... | collective-permute-start | bytes 393224 | tf_op jit(solution)/shard_map/ppermute | solution.py:155
  32.8 10.6 %copy-start.8 = (bf16[2,128,256]{2,1,0:T(8,128)(2,1)}, bf16[2,128,256]{2,1,0:T(8,128)(2,1)S(1)}, u32[]{:S(2)}) copy-start(bf16[2,128,256]{2,1,0:T(8,128)(2,1)S(1)} %collective-permute-done.4.refs_4_) | copy-start | bytes 393220
  36.5 6.9 %copy-start.9 = (bf16[2,128,256]{2,1,0:T(8,128)(2,1)}, bf16[2,128,256]{2,1,0:T(8,128)(2,1)S(1)}, u32[]{:S(2)}) copy-start(bf16[2,128,256]{2,1,0:T(8,128)(2,1)S(1)} %collective-permute-done.3.refs_3_) | copy-start | bytes 393220
  36.5 6.9 %copy-start.10 = (bf16[2,128,256]{2,1,0:T(8,128)(2,1)}, bf16[2,128,256]{2,1,0:T(8,128)(2,1)S(1)}, u32[]{:S(2)}) copy-start(bf16[2,128,256]{2,1,0:T(8,128)(2,1)S(1)} %collective-permute-done.2.refs_2_) | copy-start | bytes 393220
  36.5 6.9 %copy-start.5 = (bf16[16,128,256]{2,1,0:T(8,128)(2,1)}, bf16[16,128,256]{2,1,0:T(8,128)(2,1)S(1)}, u32[]{:S(2)}) copy-start(bf16[16,128,256]{2,1,0:T(8,128)(2,1)S(1)} %all-to-all-done.near_ref) | copy-start | bytes 3145732
  43.4 19.4 %all-to-all-start.1 = ((bf16[8,2,128,256]{3,2,1,0:T(8,128)(2,1)}), bf16[8,2,128,256]{3,2,1,0:T(8,128)(2,1)S(1)}, u32[]{:S(2)}, u32[]{:S(2)}) async-start(bf16[8,2,128,256]{3,2,1,0:T(8,128)(2,1)} %results.1), calls=%async_computation.1 | async-start | bytes 2097152 | tf_op jit(solution)/shard_map/all_to_all | solution.py:580
  47.0 15.8 %copy-start = (bf16[1024,256]{1,0:T(8,128)(2,1)S(1)}, bf16[1024,256]{1,0:T(8,128)(2,1)}, u32[]{:S(2)}) copy-start(bf16[1024,256]{1,0:T(8,128)(2,1)} %pre_ref.5) | copy-start | bytes 1572868
  47.0 15.8 %copy-start.1 = (bf16[1024,256]{1,0:T(8,128)(2,1)S(1)}, bf16[1024,256]{1,0:T(8,128)(2,1)}, u32[]{:S(2)}) copy-start(bf16[1024,256]{1,0:T(8,128)(2,1)} %value_ref.5) | copy-start | bytes 1572868
  47.0 15.8 %copy-start.2 = (bf16[1024,256]{1,0:T(8,128)(2,1)S(1)}, bf16[1024,256]{1,0:T(8,128)(2,1)}, u32[]{:S(2)}) copy-start(bf16[1024,256]{1,0:T(8,128)(2,1)} %post_ref.5) | copy-start | bytes 1572868
  47.0 15.8 %copy-start.3 = (bf16[1024,256]{1,0:T(8,128)(2,1)S(1)}, bf16[1024,256]{1,0:T(8,128)(2,1)}, u32[]{:S(2)}) copy-start(bf16[1024,256]{1,0:T(8,128)(2,1)} %cot_ref.5) | copy-start | bytes 1572868
  53.1 11.3 %collective-permute-start.6 = (bf16[16,2048]{1,0:T(8,128)(2,1)}, bf16[16,2048]{1,0:T(8,128)(2,1)S(1)}, u32[]{:S(2)}, u32[]{:S(2)}) collective-permute-start(bf16[16,2048]{1,0:T(8,128)(2,1)} %get-tuple-element.43), channel_id=1, source_target_pairs={{16,8},{17,9},{18,10},{19,11},{20,12},{21,13},{22,14},{23,15},{24,... | collective-permute-start | bytes 196616 | tf_op jit(solution)/shard_map/ppermute | solution.py:585
  54.4 10.0 %collective-permute-start.7 = (bf16[16,2048]{1,0:T(8,128)(2,1)}, bf16[16,2048]{1,0:T(8,128)(2,1)S(1)}, u32[]{:S(2)}, u32[]{:S(2)}) collective-permute-start(bf16[16,2048]{1,0:T(8,128)(2,1)} %get-tuple-element.43), channel_id=1, source_target_pairs={{0,8},{1,9},{2,10},{3,11},{4,12},{5,13},{6,14},{7,15},{8,0},{9,1},... | collective-permute-start | bytes 196616 | tf_op jit(solution)/shard_map/ppermute | solution.py:585
  59.8 4.6 %collective-permute-start.8 = (bf16[16,2048]{1,0:T(8,128)(2,1)}, bf16[16,2048]{1,0:T(8,128)(2,1)S(1)}, u32[]{:S(2)}, u32[]{:S(2)}) collective-permute-start(bf16[16,2048]{1,0:T(8,128)(2,1)} %get-tuple-element.44), channel_id=1, source_target_pairs={{0,16},{16,0},{1,17},{17,1},{2,18},{18,2},{3,19},{19,3},{4,20},{20... | collective-permute-start | bytes 196616 | tf_op jit(solution)/shard_map/ppermute | solution.py:567
  62.8 1.7 %copy-start.13 = (f32[16,2048]{1,0:T(8,128)S(1)}, f32[16,2048]{1,0:T(8,128)}, u32[]{:S(2)}) copy-start(f32[16,2048]{1,0:T(8,128)} %get-tuple-element.42) | copy-start | bytes 393220
  (2 other events, 2.3 us)

commit v6 on v5

--- a/solution.py
+++ b/solution.py
@@ -154,11 +154,14 @@
     def swap(array, slot):
         return lax.ppermute(array, "ctx", [(i, i ^ slot) for i in range(2 * half_blocks)])
 
+    far = half_blocks // 4
+    groups = [([2 * at], swap(even[at : at + 1], 2 * at)) for at in reversed(range(far, half_blocks // 2))]
     odd = swap(odd, 1)
-    groups = [([0], even[:1]), ([1], odd[:1])]
-    for at in range(1, half_blocks // 2):
+    groups += [([2 * at + 1], swap(odd[at : at + 1], 2 * at)) for at in reversed(range(far, half_blocks // 2))]
+    for at in reversed(range(1, far)):
         pair = jnp.concatenate([even[at : at + 1], odd[at : at + 1]])
         groups.append(([2 * at, 2 * at + 1], swap(pair, 2 * at)))
+    groups += [([0], even[:1]), ([1], odd[:1])]
     return groups
 
 
@@ -363,9 +366,9 @@
     count = half_blocks // merge
     filters = filt.shape[1]
 
-    def kernel(near_ref, *refs):
-        own_refs, (filt_in, table_ref, out_hbm) = refs[: len(own)], refs[len(own) : len(own) + 3]
-        stage_ref, filt_ref, spec_ref, prod_ref, held_ref, out_sems = refs[len(own) + 3 :]
+    def kernel(near_ref, filt_in, table_ref, *refs):
+        own_refs, out_hbm = refs[: len(own)], refs[len(own)]
+        stage_ref, filt_ref, spec_ref, prod_ref, held_ref, out_sems = refs[len(own) + 1 :]
         near_stage, far_stage, own_stage = (stage_ref.at[which] for which in range(3))
         stage_all(near_ref, own_refs, slots, near_stage, far_stage, own_stage, half_blocks, [(0, rows)])
         filt_ref[...] = filt_in[...].astype(jnp.float32)
@@ -409,7 +412,7 @@
     return call(
         kernel,
         "results",
-        (near, *[array for _, array in own], filt, table),
+        (near, filt, table, *[array for _, array in own]),
         [jax.ShapeDtypeStruct((half_blocks, 2, rows, tokens), jnp.bfloat16)],
         [
             pltpu.VMEM((3, count, rows, size), jnp.bfloat16),

time: 65.6 us -> 64.9 us (0.989)
  waiting for transfers between devices: 16.8 us -> 12.8 us
  starting transfers between devices: 24.9 us -> 28.2 us
    ppermute x4 -> x6, starting transfers between devices: 4.11 us -> 7.12 us  [swap(): lax.ppermute(array, 'ctx', [(i, i ^ slot) for i in range(2 * half_blocks)])]
    ppermute x4 -> x6, waiting for transfers between devices: 14.6 us -> 11.8 us  [swap(): lax.ppermute(array, 'ctx', [(i, i ^ slot) for i in range(2 * half_blocks)])]
    all_to_all x1, waiting for transfers between devices: 2.02 us -> 0.29 us  [body(): lax.all_to_all(result, 'ctx', split_axis=0, concat_axis=0, tiled=True, ax...]
    ppermute x2, waiting for transfers between devices: 0.01 us -> 0.7 us  [body(): lax.ppermute(give, ('dp', 'ctx'), [(g * blocks + i, i ^ half_blocks) for...]
    ppermute x2, starting transfers between devices: 2.46 us -> 3.13 us  [other_group(): return lax.ppermute(array, 'dp', [(0, 1), (1, 0)])]
  transfers between devices with their start and end apart: 11 -> 13, of which waited for: 4 -> 5; matrix products, arithmetic and copies ran while one was open for 0% -> 0% of each run, Pallas kernels for 19% -> 19%
where the time goes in v6:
time: 64.9 us; the launch traced here: 64.5 us
  starting transfers between devices  28.2 us (43%)
  Pallas kernels  21.1 us (33%)
  waiting for transfers between devices  12.8 us (20%)
  between operations  0.96 us (1%)
  other arithmetic  0.7 us (1%)
    pallas_call x6, Pallas kernels, call(): pl.pallas_call(kernel, in_specs=[pl.BlockSpec(memory_space=space)] * len(...  19.5 us
    ppermute x6, waiting for transfers between devices, swap(): lax.ppermute(array, 'ctx', [(i, i ^ slot) for i in range(2 * half_blocks)])  11.8 us
    ppermute x6, starting transfers between devices, swap(): lax.ppermute(array, 'ctx', [(i, i ^ slot) for i in range(2 * half_blocks)])  7.12 us
    ppermute x2, starting transfers between devices, body(): lax.ppermute(give, ('dp', 'ctx'), [(g * blocks + i, i ^ half_blocks) for...  6.35 us
    ppermute x1, starting transfers between devices, swap(): lax.ppermute(array, 'ctx', [(i, i ^ half_blocks) for i in range(blocks)])  4.14 us
    all_to_all x1, starting transfers between devices, body(): lax.all_to_all(near.reshape(blocks, rows, tokens), 'ctx', split_axis=0, c...  3.91 us
    all_to_all x1, starting transfers between devices, body(): lax.all_to_all(result, 'ctx', split_axis=0, concat_axis=0, tiled=True, ax...  3.57 us
    ppermute x2, starting transfers between devices, other_group(): return lax.ppermute(array, 'dp', [(0, 1), (1, 0)])  3.13 us
  transfers between devices with their start and end apart: 13, of which 5 were waited for; matrix products, arithmetic and copies ran while one was open for 0% of the time, Pallas kernels for 19%

profile of v6, /device:TPU:0, one launch (start us, length us, event | category | flops | bytes accessed | tf_op | source)
XLA Modules:
  0.0 64.5 jit_solution(5815738525592662105)
XLA Ops:
  0.6 2.2 %gate_near.1 = (bf16[2,8,4,2,16,256]{5,4,3,2,1,0:T(8,128)(2,1)}, bf16[16,2048]{1,0:T(8,128)(2,1)}) custom-call(bf16[1024,256]{1,0:T(8,128)(2,1)} %pre_ref.5, bf16[1024,256]{1,0:T(8,128)(2,1)} %value_ref.5, bf16[1024,256]{1,0:T(8,128)(2,1)} %post_ref.5, bf16[1024,256]{1,0:T(8,128)(2,1)} %cot_ref.5, f32[16,2048]{1,0:T(8,128)} %refs_0_.1), custom_call_target="tpu_custom_call" | custom-call | flops 1 | bytes 1 | tf_op jit(solution)/shard_map/gate_near/pallas_call | solution.py:65
  2.8 4.1 %collective-permute-start = (bf16[16,2048]{1,0:T(8,128)(2,1)}, bf16[16,2048]{1,0:T(8,128)(2,1)S(1)}, u32[]{:S(2)}, u32[]{:S(2)}) collective-permute-start(bf16[16,2048]{1,0:T(8,128)(2,1)} %get-tuple-element.27.taps_ref), channel_id=1, source_target_pairs={{0,8},{1,9},{2,10},{3,11},{4,12},{5,13},{6,14},{7,15},{8,0},{9,1},... | collective-permute-start | bytes 196616 | tf_op jit(solution)/shard_map/ppermute | solution.py:567
  7.0 3.9 %all-to-all-start = ((bf16[16,128,256]{2,1,0:T(8,128)(2,1)}), bf16[16,128,256]{2,1,0:T(8,128)(2,1)S(1)}, u32[]{:S(2)}, u32[]{:S(2)}) async-start(bf16[16,128,256]{2,1,0:T(8,128)(2,1)} %bitcast.10), calls=%async_computation | async-start | bytes 2097152 | tf_op jit(solution)/shard_map/all_to_all | solution.py:576
  10.9 2.3 %gate_own.1 = (bf16[4,4,2,16,256]{4,3,2,1,0:T(8,128)(2,1)}, bf16[4,4,2,16,256]{4,3,2,1,0:T(8,128)(2,1)}) custom-call(bf16[1024,256]{1,0:T(8,128)(2,1)} %pre_ref.5, bf16[1024,256]{1,0:T(8,128)(2,1)} %value_ref.5, bf16[1024,256]{1,0:T(8,128)(2,1)} %post_ref.5, bf16[1024,256]{1,0:T(8,128)(2,1)} %cot_ref.5), custom_call_target="tpu_custom_call" | custom-call | flops 1 | bytes 1 | tf_op jit(solution)/shard_map/gate_own/pallas_call | solution.py:65
  13.6 0.5 copy-done.16
  14.1 0.4 collective-permute-start.4
  14.6 1.6 %collective-permute-start.1 = (bf16[2,16,2048]{2,1,0:T(8,128)(2,1)S(1)}, bf16[2,16,2048]{2,1,0:T(8,128)(2,1)S(1)}, u32[]{:S(2)}, u32[]{:S(2)}) collective-permute-start(bf16[2,16,2048]{2,1,0:T(8,128)(2,1)S(1)} %pack_taps.1.here_ref), channel_id=1, source_target_pairs={{0,16},{16,0},{1,17},{17,1},{2,18},{18,2},{3,19},{19,3},{4,20},{20... | collective-permute-start | bytes 393224 | tf_op jit(solution)/shard_map/ppermute | solution.py:570
  16.2 1.7 %collective-permute-start.7 = (bf16[2,128,256]{2,1,0:T(8,128)(2,1)S(1)}, bf16[2,128,256]{2,1,0:T(8,128)(2,1)S(1)}, u32[]{:S(2)}, u32[]{:S(2)}) collective-permute-start(bf16[2,128,256]{2,1,0:T(8,128)(2,1)S(1)} %pad_maximum_fusion), channel_id=1, source_target_pairs={{0,2},{1,3},{2,0},{3,1},{4,6},{5,7},{6,4},{7,5},{8,10},{9,11},{10,... | collective-permute-start | bytes 393224 | tf_op jit(solution)/shard_map/ppermute | solution.py:155
  18.0 1.5 %collective-permute-start.2 = (bf16[1,128,256]{2,1,0:T(8,128)(2,1)S(1)}, bf16[1,128,256]{2,1,0:T(8,128)(2,1)S(1)}, u32[]{:S(2)}, u32[]{:S(2)}) collective-permute-start(bf16[1,128,256]{2,1,0:T(8,128)(2,1)S(1)} %bitcast.13), channel_id=1, source_target_pairs={{0,6},{1,7},{2,4},{3,5},{4,2},{5,3},{6,0},{7,1},{8,14},{9,15},{10,... | collective-permute-start | bytes 196616 | tf_op jit(solution)/shard_map/ppermute | solution.py:155
  19.8 2.6 %collective-permute-start.5 = (bf16[1,128,256]{2,1,0:T(8,128)(2,1)S(1)}, bf16[1,128,256]{2,1,0:T(8,128)(2,1)S(1)}, u32[]{:S(2)}, u32[]{:S(2)}) collective-permute-start(bf16[1,128,256]{2,1,0:T(8,128)(2,1)S(1)} %get-tuple-element.48), channel_id=1, source_target_pairs={{0,6},{1,7},{2,4},{3,5},{4,2},{5,3},{6,0},{7,1},{8,14},{9,15},{10,... | collective-permute-start | bytes 196616 | tf_op jit(solution)/shard_map/ppermute | solution.py:155
  22.3 0.6 collective-permute-start.6
  22.9 1.8 %taps.1.filt_in = bf16[8,32,1024]{2,1,0:T(8,128)(2,1)S(1)} custom-call(bf16[2,16,2048]{2,1,0:T(8,128)(2,1)S(1)} %pack_taps.1.here_ref, bf16[2,16,2048]{2,1,0:T(8,128)(2,1)S(1)} %collective-permute-done.1.there_ref, bf16[512,1024]{1,0:T(8,128)(2,1)S(1)} %copy-done.4), custom_call_target="tpu_custom_call" | custom-call | flops 1 | bytes 1 | tf_op jit(solution)/shard_map/taps/pallas_call | solution.py:65
  24.7 6.1 %collective-permute-done.2.refs_0_ = bf16[1,128,256]{2,1,0:T(8,128)(2,1)S(1)} collective-permute-done((bf16[1,128,256]{2,1,0:T(8,128)(2,1)S(1)}, bf16[1,128,256]{2,1,0:T(8,128)(2,1)S(1)}, u32[]{:S(2)}, u32[]{:S(2)}) %collective-permute-start.2) | collective-permute-done | bytes 65568 | tf_op jit(solution)/shard_map/ppermute | solution.py:155
  30.8 1.4 %collective-permute-done.3.refs_1_ = bf16[1,128,256]{2,1,0:T(8,128)(2,1)S(1)} collective-permute-done((bf16[1,128,256]{2,1,0:T(8,128)(2,1)S(1)}, bf16[1,128,256]{2,1,0:T(8,128)(2,1)S(1)}, u32[]{:S(2)}, u32[]{:S(2)}) %collective-permute-start.3) | collective-permute-done | bytes 65568 | tf_op jit(solution)/shard_map/ppermute | solution.py:155
  32.2 4.3 %collective-permute-done.5.refs_2_ = bf16[1,128,256]{2,1,0:T(8,128)(2,1)S(1)} collective-permute-done((bf16[1,128,256]{2,1,0:T(8,128)(2,1)S(1)}, bf16[1,128,256]{2,1,0:T(8,128)(2,1)S(1)}, u32[]{:S(2)}, u32[]{:S(2)}) %collective-permute-start.5) | collective-permute-done | bytes 65568 | tf_op jit(solution)/shard_map/ppermute | solution.py:155
  36.6 6.8 %results.1 = bf16[8,2,128,256]{3,2,1,0:T(8,128)(2,1)} custom-call(bf16[16,128,256]{2,1,0:T(8,128)(2,1)S(1)} %all-to-all-done.near_ref, bf16[8,32,1024]{2,1,0:T(8,128)(2,1)S(1)} %taps.1.filt_in, bf16[512,1024]{1,0:T(8,128)(2,1)S(1)} %copy-done.4, bf16[1,128,256]{2,1,0:T(8,128)(2,1)S(1)} %collective-permute-done.2.refs_0_, ...), custom_call_target="tpu_custom_call" | custom-call | flops 137438953472 | bytes 137438953472 | tf_op jit(solution)/shard_map/results/pallas_call | solution.py:65
  43.4 3.6 %all-to-all-start.1 = ((bf16[8,2,128,256]{3,2,1,0:T(8,128)(2,1)}), bf16[8,2,128,256]{3,2,1,0:T(8,128)(2,1)S(1)}, u32[]{:S(2)}, u32[]{:S(2)}) async-start(bf16[8,2,128,256]{3,2,1,0:T(8,128)(2,1)} %results.1), calls=%async_computation.1 | async-start | bytes 2097152 | tf_op jit(solution)/shard_map/all_to_all | solution.py:583
  47.1 6.1 %filter_terms.1 = (bf16[16,2048]{1,0:T(8,128)(2,1)}, f32[16,2048]{1,0:T(8,128)}, bf16[16,2048]{1,0:T(8,128)(2,1)}) custom-call(bf16[16,128,256]{2,1,0:T(8,128)(2,1)} %copy-done.5, bf16[1,128,256]{2,1,0:T(8,128)(2,1)} %copy-done.9, bf16[1,128,256]{2,1,0:T(8,128)(2,1)} %copy-done.10, bf16[1,128,256]{2,1,0:T(8,128)(2,1)} %copy-done.11, ...), custom_call_target="tpu_custom_call" | custom-call | flops 1 | bytes 1 | tf_op jit(solution)/shard_map/filter_terms/pallas_call | solution.py:65
  53.2 1.6 %collective-permute-start.10 = (bf16[16,2048]{1,0:T(8,128)(2,1)}, bf16[16,2048]{1,0:T(8,128)(2,1)S(1)}, u32[]{:S(2)}, u32[]{:S(2)}) collective-permute-start(bf16[16,2048]{1,0:T(8,128)(2,1)} %get-tuple-element.44), channel_id=1, source_target_pairs={{0,16},{16,0},{1,17},{17,1},{2,18},{18,2},{3,19},{19,3},{4,20},{20... | collective-permute-start | bytes 196616 | tf_op jit(solution)/shard_map/ppermute | solution.py:570
  54.7 1.3 %collective-permute-start.8 = (bf16[16,2048]{1,0:T(8,128)(2,1)}, bf16[16,2048]{1,0:T(8,128)(2,1)S(1)}, u32[]{:S(2)}, u32[]{:S(2)}) collective-permute-start(bf16[16,2048]{1,0:T(8,128)(2,1)} %get-tuple-element.43), channel_id=1, source_target_pairs={{16,8},{17,9},{18,10},{19,11},{20,12},{21,13},{22,14},{23,15},{24,... | collective-permute-start | bytes 196616 | tf_op jit(solution)/shard_map/ppermute | solution.py:588
  56.0 5.1 %collective-permute-start.9 = (bf16[16,2048]{1,0:T(8,128)(2,1)}, bf16[16,2048]{1,0:T(8,128)(2,1)S(1)}, u32[]{:S(2)}, u32[]{:S(2)}) collective-permute-start(bf16[16,2048]{1,0:T(8,128)(2,1)} %get-tuple-element.43), channel_id=1, source_target_pairs={{0,8},{1,9},{2,10},{3,11},{4,12},{5,13},{6,14},{7,15},{8,0},{9,1},... | collective-permute-start | bytes 196616 | tf_op jit(solution)/shard_map/ppermute | solution.py:588
  61.4 1.6 %finish.1 = (bf16[1024,256]{1,0:T(8,128)(2,1)}, bf16[1024,256]{1,0:T(8,128)(2,1)}, bf16[1024,256]{1,0:T(8,128)(2,1)}, bf16[1024,256]{1,0:T(8,128)(2,1)}) custom-call(bf16[8,2,4,2,16,256]{5,4,3,2,1,0:T(8,128)(2,1)S(1)} %bitcast.7, bf16[1024,256]{1,0:T(8,128)(2,1)S(1)} %copy-done, bf16[1024,256]{1,0:T(8,128)(2,1)S(1)} %copy-done.1, ...), custom_call_target="tpu_custom_call" | custom-call | tf_op jit(solution)/shard_map/finish/pallas_call | solution.py:191
  63.1 0.7 %collective-permute-done.9 = bf16[16,2048]{1,0:T(8,128)(2,1)S(1)} collective-permute-done((bf16[16,2048]{1,0:T(8,128)(2,1)}, bf16[16,2048]{1,0:T(8,128)(2,1)S(1)}, u32[]{:S(2)}, u32[]{:S(2)}) %collective-permute-start.9) | collective-permute-done | bytes 65568 | tf_op jit(solution)/shard_map/ppermute | solution.py:588
  63.8 0.7 %convert_add_fusion = f32[16,2048]{1,0:T(8,128)} fusion(bf16[16,2048]{1,0:T(8,128)(2,1)S(1)} %collective-permute-done.10, f32[16,2048]{1,0:T(8,128)S(1)} %copy-done.15, bf16[16,2048]{1,0:T(8,128)(2,1)S(1)} %collective-permute-done.9, bf16[16,2048]{1,0:T(8,128)(2,1)S(1)} %collective-permute-done.8), kind=kLoop, calls=%fused_computation.1 | loop fusion | flops 196608 | bytes 458752 | tf_op jit(solution)/shard_map/add | solution.py:593
  (47 shorter events, 1.2 us)
Async XLA Ops:
  2.8 10.4 %collective-permute-start = (bf16[16,2048]{1,0:T(8,128)(2,1)}, bf16[16,2048]{1,0:T(8,128)(2,1)S(1)}, u32[]{:S(2)}, u32[]{:S(2)}) collective-permute-start(bf16[16,2048]{1,0:T(8,128)(2,1)} %get-tuple-element.27.taps_ref), channel_id=1, source_target_pairs={{0,8},{1,9},{2,10},{3,11},{4,12},{5,13},{6,14},{7,15},{8,0},{9,1},... | collective-permute-start | bytes 196616 | tf_op jit(solution)/shard_map/ppermute | solution.py:567
  7.0 29.5 %all-to-all-start = ((bf16[16,128,256]{2,1,0:T(8,128)(2,1)}), bf16[16,128,256]{2,1,0:T(8,128)(2,1)S(1)}, u32[]{:S(2)}, u32[]{:S(2)}) async-start(bf16[16,128,256]{2,1,0:T(8,128)(2,1)} %bitcast.10), calls=%async_computation | async-start | bytes 2097152 | tf_op jit(solution)/shard_map/all_to_all | solution.py:576
  13.6 9.3 %copy-start.4 = (bf16[512,1024]{1,0:T(8,128)(2,1)S(1)}, bf16[512,1024]{1,0:T(8,128)(2,1)}, u32[]{:S(2)}) copy-start(bf16[512,1024]{1,0:T(8,128)(2,1)} %constant.2.clone.table_hbm.table_ref.refs_7_) | copy-start | bytes 3145732
  14.1 2.0 %collective-permute-start.4 = (bf16[4,128,256]{2,1,0:T(8,128)(2,1)S(1)}, bf16[4,128,256]{2,1,0:T(8,128)(2,1)S(1)}, u32[]{:S(2)}, u32[]{:S(2)}) collective-permute-start(bf16[4,128,256]{2,1,0:T(8,128)(2,1)S(1)} %bitcast.14), channel_id=1, source_target_pairs={{0,1},{1,0},{2,3},{3,2},{4,5},{5,4},{6,7},{7,6},{8,9},{9,8},{10,11... | collective-permute-start | bytes 786440 | tf_op jit(solution)/shard_map/ppermute | solution.py:155
  14.6 22.0 %copy-start.6 = (bf16[1,4,2,16,256]{4,3,2,1,0:T(8,128)(2,1)}, bf16[1,4,2,16,256]{4,3,2,1,0:T(8,128)(2,1)S(1)}, u32[]{:S(2)}) copy-start(bf16[1,4,2,16,256]{4,3,2,1,0:T(8,128)(2,1)S(1)} %get-tuple-element.49) | copy-start | bytes 196612
  14.6 7.8 %collective-permute-start.1 = (bf16[2,16,2048]{2,1,0:T(8,128)(2,1)S(1)}, bf16[2,16,2048]{2,1,0:T(8,128)(2,1)S(1)}, u32[]{:S(2)}, u32[]{:S(2)}) collective-permute-start(bf16[2,16,2048]{2,1,0:T(8,128)(2,1)S(1)} %pack_taps.1.here_ref), channel_id=1, source_target_pairs={{0,16},{16,0},{1,17},{17,1},{2,18},{18,2},{3,19},{19,3},{4,20},{20... | collective-permute-start | bytes 393224 | tf_op jit(solution)/shard_map/ppermute | solution.py:570
  16.2 20.4 %copy-start.7 = (bf16[1,128,256]{2,1,0:T(8,128)(2,1)}, bf16[1,128,256]{2,1,0:T(8,128)(2,1)S(1)}, u32[]{:S(2)}) copy-start(bf16[1,128,256]{2,1,0:T(8,128)(2,1)S(1)} %get-tuple-element.45.refs_6_) | copy-start | bytes 196612
  16.2 20.3 %collective-permute-start.7 = (bf16[2,128,256]{2,1,0:T(8,128)(2,1)S(1)}, bf16[2,128,256]{2,1,0:T(8,128)(2,1)S(1)}, u32[]{:S(2)}, u32[]{:S(2)}) collective-permute-start(bf16[2,128,256]{2,1,0:T(8,128)(2,1)S(1)} %pad_maximum_fusion), channel_id=1, source_target_pairs={{0,2},{1,3},{2,0},{3,1},{4,6},{5,7},{6,4},{7,5},{8,10},{9,11},{10,... | collective-permute-start | bytes 393224 | tf_op jit(solution)/shard_map/ppermute | solution.py:155
  18.0 12.8 %collective-permute-start.2 = (bf16[1,128,256]{2,1,0:T(8,128)(2,1)S(1)}, bf16[1,128,256]{2,1,0:T(8,128)(2,1)S(1)}, u32[]{:S(2)}, u32[]{:S(2)}) collective-permute-start(bf16[1,128,256]{2,1,0:T(8,128)(2,1)S(1)} %bitcast.13), channel_id=1, source_target_pairs={{0,6},{1,7},{2,4},{3,5},{4,2},{5,3},{6,0},{7,1},{8,14},{9,15},{10,... | collective-permute-start | bytes 196616 | tf_op jit(solution)/shard_map/ppermute | solution.py:155
  19.4 12.8 %collective-permute-start.3 = (bf16[1,128,256]{2,1,0:T(8,128)(2,1)S(1)}, bf16[1,128,256]{2,1,0:T(8,128)(2,1)S(1)}, u32[]{:S(2)}, u32[]{:S(2)}) collective-permute-start(bf16[1,128,256]{2,1,0:T(8,128)(2,1)S(1)} %bitcast.12), channel_id=1, source_target_pairs={{0,4},{1,5},{2,6},{3,7},{4,0},{5,1},{6,2},{7,3},{8,12},{9,13},{10,... | collective-permute-start | bytes 196616 | tf_op jit(solution)/shard_map/ppermute | solution.py:155
  19.8 16.7 %collective-permute-start.5 = (bf16[1,128,256]{2,1,0:T(8,128)(2,1)S(1)}, bf16[1,128,256]{2,1,0:T(8,128)(2,1)S(1)}, u32[]{:S(2)}, u32[]{:S(2)}) collective-permute-start(bf16[1,128,256]{2,1,0:T(8,128)(2,1)S(1)} %get-tuple-element.48), channel_id=1, source_target_pairs={{0,6},{1,7},{2,4},{3,5},{4,2},{5,3},{6,0},{7,1},{8,14},{9,15},{10,... | collective-permute-start | bytes 196616 | tf_op jit(solution)/shard_map/ppermute | solution.py:155
  22.3 14.2 %collective-permute-start.6 = (bf16[1,128,256]{2,1,0:T(8,128)(2,1)S(1)}, bf16[1,128,256]{2,1,0:T(8,128)(2,1)S(1)}, u32[]{:S(2)}, u32[]{:S(2)}) collective-permute-start(bf16[1,128,256]{2,1,0:T(8,128)(2,1)S(1)} %get-tuple-element.47), channel_id=1, source_target_pairs={{0,4},{1,5},{2,6},{3,7},{4,0},{5,1},{6,2},{7,3},{8,12},{9,13},{10,... | collective-permute-start | bytes 196616 | tf_op jit(solution)/shard_map/ppermute | solution.py:155
  30.8 12.6 %copy-start.9 = (bf16[1,128,256]{2,1,0:T(8,128)(2,1)}, bf16[1,128,256]{2,1,0:T(8,128)(2,1)S(1)}, u32[]{:S(2)}) copy-start(bf16[1,128,256]{2,1,0:T(8,128)(2,1)S(1)} %collective-permute-done.2.refs_0_) | copy-start | bytes 196612
  32.2 11.2 %copy-start.10 = (bf16[1,128,256]{2,1,0:T(8,128)(2,1)}, bf16[1,128,256]{2,1,0:T(8,128)(2,1)S(1)}, u32[]{:S(2)}) copy-start(bf16[1,128,256]{2,1,0:T(8,128)(2,1)S(1)} %collective-permute-done.3.refs_1_) | copy-start | bytes 196612
  36.5 6.9 %copy-start.11 = (bf16[1,128,256]{2,1,0:T(8,128)(2,1)}, bf16[1,128,256]{2,1,0:T(8,128)(2,1)S(1)}, u32[]{:S(2)}) copy-start(bf16[1,128,256]{2,1,0:T(8,128)(2,1)S(1)} %collective-permute-done.5.refs_2_) | copy-start | bytes 196612
  36.5 6.9 %copy-start.8 = (bf16[2,128,256]{2,1,0:T(8,128)(2,1)}, bf16[2,128,256]{2,1,0:T(8,128)(2,1)S(1)}, u32[]{:S(2)}) copy-start(bf16[2,128,256]{2,1,0:T(8,128)(2,1)S(1)} %collective-permute-done.7.refs_4_) | copy-start | bytes 393220
  43.4 18.0 %all-to-all-start.1 = ((bf16[8,2,128,256]{3,2,1,0:T(8,128)(2,1)}), bf16[8,2,128,256]{3,2,1,0:T(8,128)(2,1)S(1)}, u32[]{:S(2)}, u32[]{:S(2)}) async-start(bf16[8,2,128,256]{3,2,1,0:T(8,128)(2,1)} %results.1), calls=%async_computation.1 | async-start | bytes 2097152 | tf_op jit(solution)/shard_map/all_to_all | solution.py:583
  47.0 14.4 %copy-start = (bf16[1024,256]{1,0:T(8,128)(2,1)S(1)}, bf16[1024,256]{1,0:T(8,128)(2,1)}, u32[]{:S(2)}) copy-start(bf16[1024,256]{1,0:T(8,128)(2,1)} %pre_ref.5) | copy-start | bytes 1572868
  47.0 14.4 %copy-start.1 = (bf16[1024,256]{1,0:T(8,128)(2,1)S(1)}, bf16[1024,256]{1,0:T(8,128)(2,1)}, u32[]{:S(2)}) copy-start(bf16[1024,256]{1,0:T(8,128)(2,1)} %value_ref.5) | copy-start | bytes 1572868
  47.0 14.4 %copy-start.2 = (bf16[1024,256]{1,0:T(8,128)(2,1)S(1)}, bf16[1024,256]{1,0:T(8,128)(2,1)}, u32[]{:S(2)}) copy-start(bf16[1024,256]{1,0:T(8,128)(2,1)} %post_ref.5) | copy-start | bytes 1572868
  47.1 14.4 %copy-start.3 = (bf16[1024,256]{1,0:T(8,128)(2,1)S(1)}, bf16[1024,256]{1,0:T(8,128)(2,1)}, u32[]{:S(2)}) copy-start(bf16[1024,256]{1,0:T(8,128)(2,1)} %cot_ref.5) | copy-start | bytes 1572868
  53.2 9.9 %collective-permute-start.10 = (bf16[16,2048]{1,0:T(8,128)(2,1)}, bf16[16,2048]{1,0:T(8,128)(2,1)S(1)}, u32[]{:S(2)}, u32[]{:S(2)}) collective-permute-start(bf16[16,2048]{1,0:T(8,128)(2,1)} %get-tuple-element.44), channel_id=1, source_target_pairs={{0,16},{16,0},{1,17},{17,1},{2,18},{18,2},{3,19},{19,3},{4,20},{20... | collective-permute-start | bytes 196616 | tf_op jit(solution)/shard_map/ppermute | solution.py:570
  54.7 8.3 %collective-permute-start.8 = (bf16[16,2048]{1,0:T(8,128)(2,1)}, bf16[16,2048]{1,0:T(8,128)(2,1)S(1)}, u32[]{:S(2)}, u32[]{:S(2)}) collective-permute-start(bf16[16,2048]{1,0:T(8,128)(2,1)} %get-tuple-element.43), channel_id=1, source_target_pairs={{16,8},{17,9},{18,10},{19,11},{20,12},{21,13},{22,14},{23,15},{24,... | collective-permute-start | bytes 196616 | tf_op jit(solution)/shard_map/ppermute | solution.py:588
  56.0 7.7 %collective-permute-start.9 = (bf16[16,2048]{1,0:T(8,128)(2,1)}, bf16[16,2048]{1,0:T(8,128)(2,1)S(1)}, u32[]{:S(2)}, u32[]{:S(2)}) collective-permute-start(bf16[16,2048]{1,0:T(8,128)(2,1)} %get-tuple-element.43), channel_id=1, source_target_pairs={{0,8},{1,9},{2,10},{3,11},{4,12},{5,13},{6,14},{7,15},{8,0},{9,1},... | collective-permute-start | bytes 196616 | tf_op jit(solution)/shard_map/ppermute | solution.py:588
  (6 other events, 20.8 us)
